TPU v7x, 32 devices: a whole 2x2x4 slice. The times are simulated.
32 devices in a mesh: attn: 4 (over x, core), ffn: 8 (over z, y).
Axes of the slice: x: 2, y: 2, z: 4, core: 2. Of those that a mesh axis runs over, the one named last changes fastest.
Arguments:
- queries: bfloat16 [256, 2, 64, 576], P(('attn', 'ffn')), may hold values from -9 to 9
- latent_cache: bfloat16 [256, 512, 576], P(('attn', 'ffn')), may hold values from -4 to 4
- fresh_latent: bfloat16 [256, 2, 576], P(('attn', 'ffn')), may hold values from -4 to 4
- lengths: int32 [256], P(('attn', 'ffn')), may hold values from 1 to 512, 65536 in all
- handoff: int32 [8, 8], P('ffn'), may hold values 0 or 1
- residual: bfloat16 [256, 2, 7168], P(('attn', 'ffn')), may hold values from -30 to 30
- value_up_matrix: bfloat16 [64, 512, 128], P('ffn'), may hold values from -0.5 to 0.5
- output_weight: bfloat16 [8192, 7168], P('ffn'), may hold values from -0.1875 to 0.1875
- norm_gain: float32 [7168], replicated, may hold values from 0.3 to 3
- router: bfloat16 [7168, 8], replicated, may hold values from -0.0625 to 0.0625
- expert_ids: int32 [256, 2, 2], P('attn'), may hold values from 0 to 7, all different within a row; in each aligned block of 128 rows (0 to 127, 128 to 255, ..., all dimensions but the last counted through in order) at most 64 rows name the same one
- gate_weight: bfloat16 [8, 7168, 2048], P('ffn', None, 'attn'), may hold values from -0.0625 to 0.0625
- up_weight: bfloat16 [8, 7168, 2048], P('ffn', None, 'attn'), may hold values from -0.0625 to 0.0625
- down_weight: bfloat16 [8, 2048, 7168], P('ffn', 'attn'), may hold values from -0.125 to 0.125
Outputs:
- attended: bfloat16 [256, 2, 7168], P(('attn', 'ffn'))
- expert_out: bfloat16 [256, 2, 7168], P(('attn', 'ffn'))
Inputs may be any that keep to these rules, and one draw needn't show every extreme that they name: `expert_ids`: the 2 ids of a token differ. In each aligned block of 128 tokens (the requests of one index of attn, all new tokens of each, in order) no expert is chosen by more than 64 tokens, and some expert is chosen by exactly 64 in some block.
All inputs are finite; a program needn't handle non-finite values. No bound on the sum of `lengths` or of `handoff` on one device may be relied on, other than what follows from the above.
Results may differ from a plain program's by a relative error of at most 0.014.
Values may be sent and summed in bfloat16 or wider, within the bound.
No kernel may reach another device: no remote copies, remote signals or barrier semaphores. Data moves between devices by JAX's collectives and lax.ppermute only.
A program may use at most 128 MiB of HBM per device.

v0:
```python
import jax
import jax.numpy as jnp
from jax import lax
from jax.sharding import PartitionSpec as P

KV_RANK = 512


score_scale = 192.0 ** (-0.5)
norm_epsilon = 1e-06


def shifted(value, axis, by):
    count = lax.axis_size(axis)
    return lax.ppermute(value, axis, [(i, (i + by) % count) for i in range(count)])


def attend_block(queries, latent_cache, fresh_latent, lengths):
    req_count, steps_here, heads_here, latent_width = queries.shape
    cache_span = latent_cache.shape[1]
    row_count = steps_here * heads_here
    rows_flat = queries.reshape(req_count, row_count, latent_width)
    old_scores = (
        jnp.einsum("rqc,rnc->rqn", rows_flat, latent_cache, preferred_element_type=jnp.float32)
        * score_scale
    )
    position = lax.broadcasted_iota(jnp.int32, (1, 1, cache_span), 2)
    old_scores = jnp.where(position < lengths[:, None, None], old_scores, -jnp.inf)
    new_scores = (
        jnp.einsum("rqc,rjc->rqj", rows_flat, fresh_latent, preferred_element_type=jnp.float32)
        * score_scale
    )
    row_step = lax.broadcasted_iota(jnp.int32, (1, row_count, steps_here), 1) // heads_here
    column_step = lax.broadcasted_iota(jnp.int32, (1, row_count, steps_here), 2)
    new_scores = jnp.where(column_step <= row_step, new_scores, -jnp.inf)
    row_peak = jnp.maximum(jnp.max(old_scores, axis=2), jnp.max(new_scores, axis=2))[:, :, None]
    old_exp = jnp.exp(old_scores - row_peak)
    new_exp = jnp.exp(new_scores - row_peak)
    denominator = jnp.sum(old_exp, axis=2, keepdims=True) + jnp.sum(new_exp, axis=2, keepdims=True)
    old_probs = (old_exp / denominator).astype(jnp.bfloat16)
    new_probs = (new_exp / denominator).astype(jnp.bfloat16)
    latent_mix = jnp.einsum(
        "rqn,rnc->rqc", old_probs, latent_cache[:, :, :KV_RANK], preferred_element_type=jnp.float32
    )
    latent_mix = latent_mix + jnp.einsum(
        "rqj,rjc->rqc", new_probs, fresh_latent[:, :, :KV_RANK], preferred_element_type=jnp.float32
    )
    return latent_mix.astype(jnp.bfloat16).reshape(req_count, steps_here, heads_here, KV_RANK)


def rms_normalize(state, norm_gain):
    scale_rows = lax.rsqrt(jnp.mean(state * state, axis=-1, keepdims=True) + norm_epsilon)
    return (state * scale_rows * norm_gain).astype(jnp.bfloat16)


def local(
    queries,
    latent_cache,
    fresh_latent,
    lengths,
    handoff,
    residual,
    value_up_matrix,
    output_weight,
    norm_gain,
    router,
    expert_ids,
    gate_weight,
    up_weight,
    down_weight,
):
    moved_flag = handoff[0] == 1
    moved_here = moved_flag[:, None, None, None]
    arrived = shifted((queries, latent_cache, fresh_latent, lengths), "attn", 1)
    queries_now = jnp.where(moved_here, arrived[0], queries)
    cache_now = jnp.where(moved_here[:, :, :, 0], arrived[1], latent_cache)
    fresh_now = jnp.where(moved_here[:, :, :, 0], arrived[2], fresh_latent)
    lengths_now = jnp.where(moved_flag, arrived[3], lengths)
    latent_out = attend_block(queries_now, cache_now, fresh_now, lengths_now)
    heads_local = value_up_matrix.shape[0]
    model_width = output_weight.shape[1]
    head_weight = output_weight.reshape(heads_local, value_up_matrix.shape[2], model_width)
    value_rows = jnp.einsum(
        "olfb,fbw->olfw",
        lax.all_to_all(latent_out, "ffn", split_axis=2, concat_axis=0, tiled=True),
        value_up_matrix,
        preferred_element_type=jnp.float32,
    ).astype(jnp.bfloat16)
    partial_out = jnp.einsum(
        "rshv,hvd->rsd", value_rows, head_weight, preferred_element_type=jnp.float32
    )
    req_dev = residual.shape[0]
    steps_here = residual.shape[1]
    ffn_index = lax.axis_index("ffn")
    local_token_rows = residual.astype(jnp.float32)
    placed_rows = lax.dynamic_update_slice(
        jnp.zeros_like(partial_out), local_token_rows, (ffn_index * req_dev, 0, 0)
    )
    state_rows = lax.psum(partial_out + placed_rows, "ffn")
    own_state = lax.dynamic_slice_in_dim(state_rows, ffn_index * req_dev, req_dev, 0)
    normed_rows = rms_normalize(state_rows, norm_gain)
    attended = own_state.astype(jnp.bfloat16)
    row_req = normed_rows.shape[0]
    row_tokens = row_req * steps_here
    normed_flat = normed_rows.reshape(row_tokens, model_width)
    expert_count = router.shape[1]
    logits = jnp.dot(normed_flat, router, preferred_element_type=jnp.float32)
    affinity = jax.nn.sigmoid(logits)
    ids_flat = expert_ids.reshape(row_tokens, expert_ids.shape[2])
    onehot = ids_flat[:, :, None] == lax.broadcasted_iota(jnp.int32, (1, 1, expert_count), 2)
    chosen = jnp.sum(jnp.where(onehot, affinity[:, None, :], 0.0), axis=2)
    gate_fraction_value = 2.5 * chosen / jnp.sum(chosen, axis=1, keepdims=True)
    routed_here = ids_flat == ffn_index
    token_weight = jnp.sum(jnp.where(routed_here, gate_fraction_value, 0.0), axis=1)
    token_hit = jnp.sum(routed_here.astype(jnp.int32), axis=1)
    slot_rank = jnp.cumsum(token_hit) - 1
    capacity = 4 * steps_here * req_dev
    slot_ids = lax.broadcasted_iota(jnp.int32, (capacity, row_tokens), 0)
    selector = ((token_hit[None, :] == 1) & (slot_rank[None, :] == slot_ids)).astype(jnp.bfloat16)
    expert_input = jnp.dot(selector, normed_flat, preferred_element_type=jnp.float32).astype(
        jnp.bfloat16
    )
    gate_local = gate_weight[0]
    up_local = up_weight[0]
    down_local = down_weight[0]
    rows_in = lax.all_gather(expert_input, "attn", axis=0, tiled=True)
    gate_part = jnp.dot(rows_in, gate_local, preferred_element_type=jnp.float32)
    up_part = jnp.dot(rows_in, up_local, preferred_element_type=jnp.float32)
    hidden_all = (jax.nn.silu(gate_part) * up_part).astype(jnp.bfloat16)
    rows_in = hidden_all
    expert_rows = lax.psum_scatter(
        jnp.dot(rows_in, down_local, preferred_element_type=jnp.float32),
        "attn",
        scatter_dimension=0,
        tiled=True,
    ).astype(jnp.bfloat16)
    returned = (
        jnp.einsum("ct,cd->td", selector, expert_rows, preferred_element_type=jnp.float32)
        * token_weight[:, None]
    )
    summed = lax.psum_scatter(
        returned.reshape(row_req, steps_here, model_width), "ffn", scatter_dimension=0, tiled=True
    )
    return (attended, summed.astype(jnp.bfloat16))


def solution(mesh):
    return jax.shard_map(
        local,
        mesh=mesh,
        in_specs=(
            P(("attn", "ffn"), None, None, None),
            P(("attn", "ffn"), None, None),
            P(("attn", "ffn"), None, None),
            P(("attn", "ffn")),
            P("ffn", None),
            P(("attn", "ffn"), None, None),
            P("ffn", None, None),
            P("ffn", None),
            P(),
            P(),
            P("attn", None, None),
            P("ffn", None, "attn"),
            P("ffn", None, "attn"),
            P("ffn", "attn", None),
        ),
        out_specs=(P(("attn", "ffn"), None, None), P(("attn", "ffn"), None, None)),
        check_vma=False,
    )
```

profile of v0, /device:TPU:0, one launch (start us, length us, event | category | flops | bytes accessed | tf_op | source)
XLA Modules:
  0.0 574.5 jit_solution(13283807279791806019)
XLA Ops:
  7.7 2.6 collective-permute-start.3
  10.4 7.7 %copy.113 = bf16[8,512,576]{2,1,0:T(8,128)(2,1)} copy(bf16[8,512,576]{1,2,0:T(8,128)(2,1)} %param.15) | data formatting | bytes 9437184 | tf_op args[1]
  18.2 57.8 %collective-permute-done = s32[8]{0:T(128)S(1)} collective-permute-done((s32[8]{0:T(128)}, s32[8]{0:T(128)S(1)}, u32[]{:S(2)}, u32[]{:S(2)}) %collective-permute-start) | collective-permute-done | bytes 64 | tf_op jit(solution)/shard_map/ppermute | solution.py:15
  76.2 1.9 broadcast_select_fusion.1
  78.7 7.7 %copy.112 = bf16[8,512,576]{2,1,0:T(8,128)(2,1)} copy(bf16[8,512,576]{1,2,0:T(8,128)(2,1)} %collective-permute-done.2) | data formatting | bytes 9437184 | tf_op jit(solution)/shard_map/ppermute | solution.py:15
  86.4 4.7 broadcast_select_fusion
  91.1 1.9 fusion.8
  93.0 0.6 fusion.11
  94.2 1.3 add_convert_fusion
  95.5 2.1 copy.117
  97.5 6.6 %all-to-all-start = ((bf16[8,2,64,512]{3,1,0,2:T(2,128)(2,1)}), bf16[8,2,64,512]{3,1,0,2:T(2,128)(2,1)S(1)}, u32[]{:S(2)}, u32[]{:S(2)}) async-start(bf16[8,2,64,512]{3,1,0,2:T(2,128)(2,1)} %copy.117), calls=%async_computation | async-start | bytes 2097152 | tf_op jit(solution)/shard_map/all_to_all | solution.py:85
  104.2 25.2 %all-to-all-done = bf16[8,2,64,512]{3,1,0,2:T(2,128)(2,1)S(1)} async-done(((bf16[8,2,64,512]{3,1,0,2:T(2,128)(2,1)}), bf16[8,2,64,512]{3,1,0,2:T(2,128)(2,1)S(1)}, u32[]{:S(2)}, u32[]{:S(2)}) %all-to-all-start) | async-done | bytes 1048608 | tf_op jit(solution)/shard_map/all_to_all | solution.py:85
  129.5 0.6 copy.140
  130.2 9.0 %convolution_bitcast_fusion = f32[64,2,7168]{2,0,1:T(8,128)} fusion(bf16[8,128,7168,1]{2,1,0,3:T(8,128)(2,1)} %bitcast.56, bf16[8,512,128]{2,1,0:T(8,128)(2,1)S(1)} %copy-done, bf16[64,2,8,512]{3,2,1,0:T(8,128)(2,1)S(1)} %bitcast.59), kind=kOutput, calls=%fused_computation.1 | convolution fusion | flops 2013396992 | bytes 20447232 | tf_op jit(solution)/shard_map/rshv,hvd->rsd/dot_general | solution.py:89
  139.2 1.9 add_dynamic-update-slice_fusion
  142.1 140.3 %all-reduce.4.cloned.1.call-done = f32[64,2,7168]{2,0,1:T(8,128)} async-done(((f32[64,2,7168]{2,0,1:T(8,128)}), f32[64,2,7168]{2,0,1:T(8,128)}) %all-reduce.4.cloned.1.call-update) | async-done | bytes 3670032 | tf_op jit(solution)/shard_map/psum | solution.py:99
  282.3 2.5 multiply_reduce_fusion
  284.9 0.6 copy-done.2
  285.9 3.1 copy.125
  289.0 4.1 reshape.169
  293.1 1.3 convolution_convert_fusion
  294.5 30.6 %all-gather.2.cloned.1.call-done = bf16[256,7168]{1,0:T(8,128)(2,1)} async-done(((bf16[64,7168]{1,0:T(8,128)(2,1)}), bf16[256,7168]{1,0:T(8,128)(2,1)}) %all-gather.2.cloned.1.call-update) | async-done | bytes 3670032 | tf_op jit(solution)/shard_map/all_gather | solution.py:126
  325.2 6.2 %fusion.4 = f32[256,512]{1,0:T(8,128)S(1)} fusion(bf16[256,7168]{1,0:T(8,128)(2,1)} %all-gather.2.cloned.1.call-done, bf16[1,7168,512]{2,1,0:T(8,128)(2,1)} %param.25), kind=kOutput, calls=%fused_computation.7 | convolution fusion | flops 1879048192 | bytes 11534336 | tf_op jit(solution)/shard_map/dot_general | solution.py:127
  331.4 13.3 %fusion = f32[256,7168]{1,0:T(8,128)} fusion(bf16[1,512,7168]{2,1,0:T(8,128)(2,1)} %param.27, bf16[256,7168]{1,0:T(8,128)(2,1)} %all-gather.2.cloned.1.call-done, bf16[1,7168,512]{2,1,0:T(8,128)(2,1)} %param.26, f32[256,512]{1,0:T(8,128)S(1)} %fusion.4), kind=kOutput, calls=%fused_computation.3 | convolution fusion | flops 3758882816 | bytes 26214400 | tf_op jit(solution)/shard_map/dot_general | solution.py:132
  345.4 0.6 dynamic-slice.1
  346.6 1.1 dynamic-slice_convert_fusion.1
  347.7 0.9 copy.130
  350.0 60.4 %reduce-scatter.2.cloned.1.call-done = f32[64,7168]{1,0:T(8,128)} async-done(((f32[256,7168]{1,0:T(8,128)}), f32[64,7168]{1,0:T(8,128)}) %reduce-scatter.2.cloned.1.call-update) | async-done | bytes 1835024 | tf_op jit(solution)/shard_map/reduce_scatter | solution.py:131
  410.4 4.0 convolution_multiply_fusion
  414.4 5.6 reshape.170
  420.0 147.1 %all-reduce.5 = bf16[64,2,7168]{2,1,0:T(2,128)(2,1)S(1)} all-reduce(f32[64,2,7168]{2,1,0:T(2,128)} %reshape.170), channel_id=3, replica_groups=mesh['attn'=4,'ffn'=8] {'ffn'}, use_global_device_ids=true, to_apply=%region_12.13.clone | all-reduce | flops 917504 | bytes 5505024
  567.1 0.9 dynamic-slice_convert_fusion
  (68 shorter events, 5.5 us)
Async XLA Ops:
  7.2 123.0 %copy-start = (bf16[8,512,128]{2,1,0:T(8,128)(2,1)S(1)}, bf16[8,512,128]{2,1,0:T(8,128)(2,1)}, u32[]{:S(2)}) copy-start(bf16[8,512,128]{2,1,0:T(8,128)(2,1)} %param.20) | copy-start | bytes 3145732
  7.2 68.9 %copy-start.6 = (bf16[8,2,576]{2,1,0:T(2,128)(2,1)S(1)}, bf16[8,2,576]{2,1,0:T(2,128)(2,1)}, u32[]{:S(2)}) copy-start(bf16[8,2,576]{2,1,0:T(2,128)(2,1)} %param.16) | copy-start | bytes 55300
  7.2 68.8 %copy-start.9 = (s32[8]{0:T(128)S(1)}, s32[8]{0:T(128)}, u32[]{:S(2)}) copy-start(s32[8]{0:T(128)} %param.17) | copy-start | bytes 100
  7.2 11.0 %copy-start.8 = (s32[1,8]{1,0:T(1,128)S(1)}, s32[1,8]{1,0:T(1,128)}, u32[]{:S(2)}) copy-start(s32[1,8]{1,0:T(1,128)} %param.18) | copy-start | bytes 100
  7.2 71.5 %collective-permute-start.2 = (bf16[8,512,576]{1,2,0:T(8,128)(2,1)}, bf16[8,512,576]{1,2,0:T(8,128)(2,1)}, u32[]{:S(2)}, u32[]{:S(2)}) collective-permute-start(bf16[8,512,576]{1,2,0:T(8,128)(2,1)} %param.15), channel_id=1, source_target_pairs={{0,8},{8,16},{16,24},{24,0},{1,9},{9,17},{17,25},{25,1},{2,10},{10... | collective-permute-start | bytes 14155784 | tf_op jit(solution)/shard_map/ppermute | solution.py:15
  7.7 68.4 %collective-permute-start.3 = (bf16[8,2,576]{2,1,0:T(2,128)(2,1)}, bf16[8,2,576]{2,1,0:T(2,128)(2,1)S(1)}, u32[]{:S(2)}, u32[]{:S(2)}) collective-permute-start(bf16[8,2,576]{2,1,0:T(2,128)(2,1)} %param.16), channel_id=1, source_target_pairs={{0,8},{8,16},{16,24},{24,0},{1,9},{9,17},{17,25},{25,1},{2,10},{10... | collective-permute-start | bytes 55304 | tf_op jit(solution)/shard_map/ppermute | solution.py:15
  10.3 65.9 %collective-permute-start.1 = (bf16[8,2,64,576]{3,2,1,0:T(8,128)(2,1)}, bf16[8,2,64,576]{3,2,1,0:T(8,128)(2,1)}, u32[]{:S(2)}, u32[]{:S(2)}) collective-permute-start(bf16[8,2,64,576]{3,2,1,0:T(8,128)(2,1)} %param.14), channel_id=1, source_target_pairs={{0,8},{8,16},{16,24},{24,0},{1,9},{9,17},{17,25},{25,1},{2,10},{10... | collective-permute-start | bytes 3538952 | tf_op jit(solution)/shard_map/ppermute | solution.py:15
  10.4 65.6 %collective-permute-start = (s32[8]{0:T(128)}, s32[8]{0:T(128)S(1)}, u32[]{:S(2)}, u32[]{:S(2)}) collective-permute-start(s32[8]{0:T(128)} %param.17), channel_id=1, source_target_pairs={{0,8},{8,16},{16,24},{24,0},{1,9},{9,17},{17,25},{25,1},{2,10},{10... | collective-permute-start | bytes 104 | tf_op jit(solution)/shard_map/ppermute | solution.py:15
  97.5 31.9 %all-to-all-start = ((bf16[8,2,64,512]{3,1,0,2:T(2,128)(2,1)}), bf16[8,2,64,512]{3,1,0,2:T(2,128)(2,1)S(1)}, u32[]{:S(2)}, u32[]{:S(2)}) async-start(bf16[8,2,64,512]{3,1,0,2:T(2,128)(2,1)} %copy.117), calls=%async_computation | async-start | bytes 2097152 | tf_op jit(solution)/shard_map/all_to_all | solution.py:85
  104.2 178.1 %all-reduce.4.cloned.1.call-start = ((), (), s32[]{:S(2)}) async-start(), calls=%async_computation.2 | async-start | bytes 7340032 | tf_op jit(solution)/shard_map/psum | solution.py:99
  130.2 9.0 %copy-start.3 = (bf16[8,2,7168]{2,1,0:T(2,128)(2,1)S(1)}, bf16[8,2,7168]{2,1,0:T(2,128)(2,1)}, u32[]{:S(2)}) copy-start(bf16[8,2,7168]{2,1,0:T(2,128)(2,1)} %param.19) | copy-start | bytes 688132
  139.2 2.1 copy-start.7
  141.0 143.8 %copy-start.5 = (f32[7168]{0:T(1024)S(1)}, f32[7168]{0:T(1024)}, u32[]{:S(2)}) copy-start(f32[7168]{0:T(1024)} %param.22) | copy-start | bytes 86020
  141.1 184.1 %all-gather.2.cloned.1.call-start = ((), (), s32[]{:S(2)}) async-start(), calls=%async_computation.3 | async-start | bytes 4587520 | tf_op jit(solution)/shard_map/all_gather | solution.py:126
  282.3 3.1 copy-start.2
  294.5 115.9 %reduce-scatter.2.cloned.1.call-start = ((), (), s32[]{:S(2)}) async-start(), calls=%async_computation.4 | async-start | bytes 9175040 | tf_op jit(solution)/shard_map/reduce_scatter | solution.py:131
  344.7 0.7 copy-start.10
  344.7 3.9 copy-start.4
  414.4 153.6 %copy-start.1 = (bf16[8,512,128]{2,1,0:T(8,128)(2,1)S(1)}, bf16[8,512,128]{2,1,0:T(8,128)(2,1)}, u32[]{:S(2)}) copy-start(bf16[8,512,128]{2,1,0:T(8,128)(2,1)} %param.20) | copy-start | bytes 3145732
Sparse Core Ops, SparseCore 0:
  141.2 141.0 all-reduce.3
  294.6 30.5 all-gather.1
  344.9 65.4 reduce-scatter.1
where the time goes:
time: 575 us
  waiting for transfers between devices  314 us (55%)
  blocking collectives  147 us (26%)
  matrix products  38.6 us (7%)
  local copies, waits for them, and re-layouts  36.8 us (6%)
  between operations  14.7 us (3%)
  other arithmetic  12.7 us (2%)
  starting transfers between devices  10.2 us (2%)
    unnamed x1, blocking collectives  147 us
    psum x1, waiting for transfers between devices, local(): state_rows = lax.psum(partial_out + placed_rows, 'ffn')  140 us
    reduce_scatter x1, waiting for transfers between devices, local(): lax.psum_scatter(jnp.dot(rows_in, down_local, preferred_element_type=jnp....  60.4 us
    ppermute x4, waiting for transfers between devices, shifted(): lax.ppermute(value, axis, [(i, (i + by) % count) for i in range(count)])  57.8 us
    all_gather x1, waiting for transfers between devices, local(): rows_in = lax.all_gather(expert_input, 'attn', axis=0, tiled=True)  30.6 us
    all_to_all x1, waiting for transfers between devices, local(): lax.all_to_all(latent_out, 'ffn', split_axis=2, concat_axis=0, tiled=True)  25.2 us
    dot_general x1, matrix products, local(): jnp.dot(rows_in, down_local, preferred_element_type=jnp.float32)  13.3 us
  transfers between devices with their start and end apart: 8, of which 5 were waited for; matrix products, arithmetic and copies ran while one was open for 3% of the time, Pallas kernels for 0%

commit v1 on v0

v1 whole, which is shorter than its diff:
```python
import functools

import jax
import jax.numpy as jnp
from jax import lax
from jax.experimental import pallas as pl
from jax.experimental.pallas import tpu as pltpu
from jax.sharding import PartitionSpec as P

KV_RANK = 512
SCORE_SCALE = 192.0 ** (-0.5)
NORM_EPSILON = 1e-06
IN_CHUNKS = 2
OUT_CHUNKS = 2

f32 = jnp.float32
bf16 = jnp.bfloat16


def swap(value, axis, mask):
    count = lax.axis_size(axis)
    return lax.ppermute(value, axis, [(i, i ^ mask) for i in range(count)])


def masks_of(count):
    return [1 << k for k in range(count.bit_length() - 1)]


def relative_order(count):
    order = [0]
    for mask in reversed(masks_of(count)):
        order = order + [mask ^ o for o in order]
    return order


def gather_rows(rows, axis):
    for mask in reversed(masks_of(lax.axis_size(axis))):
        rows = jnp.concatenate([rows, swap(rows, axis, mask)], axis=0)
    return rows


def reduce_rows(rows, axis, masks):
    for mask in masks:
        half = rows.shape[0] // 2
        rows = rows[:half] + swap(rows[half:].astype(bf16), axis, mask).astype(f32)
    return rows


def attend_kernel(heads_local, lengths_ref, q_ref, cache_ref, fresh_ref, out_ref):
    q = q_ref[0]
    row_count = q.shape[0]
    span = cache_ref.shape[1]
    steps = fresh_ref.shape[1]
    heads = row_count // steps
    live = lengths_ref[pl.program_id(0)]
    keys = cache_ref[0]
    contract = (((1,), (1,)), ((), ()))
    old = lax.dot_general(q, keys, contract, preferred_element_type=f32) * SCORE_SCALE
    position = lax.broadcasted_iota(jnp.int32, (row_count, span), 1)
    old = jnp.where(position < live, old, -jnp.inf)
    fresh = fresh_ref[0]
    new = lax.dot_general(q, fresh, contract, preferred_element_type=f32) * SCORE_SCALE
    row_step = lax.broadcasted_iota(jnp.int32, (row_count, steps), 0) // heads
    column = lax.broadcasted_iota(jnp.int32, (row_count, steps), 1)
    new = jnp.where(column <= row_step, new, -jnp.inf)
    peak = jnp.maximum(jnp.max(old, axis=1, keepdims=True), jnp.max(new, axis=1, keepdims=True))
    old_exp = jnp.exp(old - peak)
    new_exp = jnp.exp(new - peak)
    total = jnp.sum(old_exp, axis=1, keepdims=True) + jnp.sum(new_exp, axis=1, keepdims=True)
    inverse = 1.0 / total
    old_probs = (old_exp * inverse).astype(bf16)
    new_probs = (new_exp * inverse).astype(bf16).astype(f32)
    mix = jnp.dot(old_probs, keys[:, :KV_RANK], preferred_element_type=f32)
    fresh_values = fresh[:, :KV_RANK].astype(f32)
    for j in range(steps):
        mix = mix + new_probs[:, j : j + 1] * fresh_values[j : j + 1, :]
    if heads_local % 8 == 0:
        for dest in range(heads // heads_local):
            parts = [mix[t * heads + dest * heads_local :][:heads_local] for t in range(steps)]
            out_ref[dest, 0] = jnp.concatenate(parts, axis=0).astype(bf16)
    else:
        out_ref[0] = mix.astype(bf16)


def attend(queries, latent_cache, fresh_latent, lengths, heads_local):
    reqs, steps, heads, width = queries.shape
    span = latent_cache.shape[1]
    rows = steps * heads
    dests = heads // heads_local
    if heads_local % 8 == 0:
        out_shape = (dests, reqs, steps * heads_local, KV_RANK)
        out_spec = pl.BlockSpec(
            (dests, 1, steps * heads_local, KV_RANK), lambda r, n: (0, r, 0, 0)
        )
    else:
        out_shape = (reqs, rows, KV_RANK)
        out_spec = pl.BlockSpec((1, rows, KV_RANK), lambda r, n: (r, 0, 0))
    out = pl.pallas_call(
        functools.partial(attend_kernel, heads_local),
        out_shape=jax.ShapeDtypeStruct(out_shape, bf16),
        grid_spec=pltpu.PrefetchScalarGridSpec(
            num_scalar_prefetch=1,
            grid=(reqs,),
            in_specs=[
                pl.BlockSpec((1, rows, width), lambda r, n: (r, 0, 0)),
                pl.BlockSpec((1, span, width), lambda r, n: (r, 0, 0)),
                pl.BlockSpec((1, steps, width), lambda r, n: (r, 0, 0)),
            ],
            out_specs=out_spec,
        ),
        compiler_params=pltpu.CompilerParams(vmem_limit_bytes=24 * 1024 * 1024),
        name="attend",
    )(lengths, queries.reshape(reqs, rows, width), latent_cache, fresh_latent)
    if heads_local % 8 == 0:
        return out
    out = out.reshape(reqs, steps, dests, heads_local, KV_RANK)
    return out.transpose(2, 0, 1, 3, 4).reshape(dests, reqs, steps * heads_local, KV_RANK)


def value_kernel(order, place_ref, latent_ref, up_ref, out_ref):
    heads_local, _, v_head = up_ref.shape
    place = place_ref[0]
    rows = jnp.concatenate([latent_ref[place ^ o] for o in order], axis=0)
    tokens = rows.shape[0] // heads_local
    for h in range(heads_local):
        one = jnp.dot(rows, up_ref[h], preferred_element_type=f32)
        one = one.reshape(tokens, heads_local, v_head)
        head = lax.broadcasted_iota(jnp.int32, one.shape, 1)
        one = jnp.sum(jnp.where(head == h, one, 0.0), axis=1)
        out_ref[:, h * v_head : (h + 1) * v_head] = one.astype(bf16)


def values_of(latents, value_up, place, order):
    sources, reqs, rows, rank = latents.shape
    heads_local, _, v_head = value_up.shape
    steps = rows // heads_local
    tokens = sources * reqs * steps
    if heads_local % 8 == 0:
        return pl.pallas_call(
            functools.partial(value_kernel, order),
            out_shape=jax.ShapeDtypeStruct((tokens, heads_local * v_head), bf16),
            in_specs=[
                pl.BlockSpec(memory_space=pltpu.SMEM),
                pl.BlockSpec(memory_space=pltpu.VMEM),
                pl.BlockSpec(memory_space=pltpu.VMEM),
            ],
            out_specs=pl.BlockSpec(memory_space=pltpu.VMEM),
            compiler_params=pltpu.CompilerParams(vmem_limit_bytes=24 * 1024 * 1024),
            name="values",
        )(place[None], latents.reshape(sources, reqs * rows, rank), value_up)
    latents = latents[place ^ jnp.array(order, jnp.int32)]
    latents = latents.reshape(sources * reqs * steps, heads_local, rank)
    out = jnp.einsum("nhb,hbw->nhw", latents, value_up, preferred_element_type=f32)
    return out.astype(bf16).reshape(tokens, heads_local * v_head)


def local(
    queries,
    latent_cache,
    fresh_latent,
    lengths,
    handoff,
    residual,
    value_up_matrix,
    output_weight,
    norm_gain,
    router,
    expert_ids,
    gate_weight,
    up_weight,
    down_weight,
):
    n_attn = lax.axis_size("attn")
    n_ffn = lax.axis_size("ffn")
    attn_masks = masks_of(n_attn)
    ffn_masks = masks_of(n_ffn)
    order = relative_order(n_ffn)
    ffn_index = lax.axis_index("ffn").astype(jnp.int32)
    sources = ffn_index ^ jnp.array(order, jnp.int32)
    reqs, steps, model_width = residual.shape
    own_tokens = reqs * steps
    row_tokens = n_ffn * own_tokens
    heads_local = value_up_matrix.shape[0]

    ids = expert_ids.reshape(n_ffn, own_tokens, expert_ids.shape[2])[sources]
    ids = ids.reshape(row_tokens, expert_ids.shape[2])
    hit = jnp.sum((ids == ffn_index).astype(jnp.int32), axis=1)
    rank = jnp.cumsum(hit) - 1
    capacity = 4 * own_tokens
    slots = lax.broadcasted_iota(jnp.int32, (capacity, row_tokens), 0)
    chosen = (hit[None, :] == 1) & (rank[None, :] == slots)
    selector = chosen.astype(bf16)
    partner_id = jnp.sum(
        jnp.where(chosen, (jnp.sum(ids, axis=1) - ffn_index)[None, :], 0), axis=1
    )
    moved = lax.all_gather(handoff[0], "ffn", axis=0)[sources]
    moved = jnp.repeat(moved.reshape(n_ffn * reqs) == 1, steps)[:, None]

    latents = attend(queries, latent_cache, fresh_latent, lengths, heads_local)
    latents = lax.all_to_all(latents, "ffn", split_axis=0, concat_axis=0, tiled=True)
    values = values_of(latents, value_up_matrix, ffn_index, order)
    arrived = lax.ppermute(values, "attn", [(i, (i + 1) % n_attn) for i in range(n_attn)])
    values = jnp.where(moved, arrived, values)

    residual_rows = residual.reshape(own_tokens, model_width)
    half_tokens = row_tokens // 2
    width = model_width // IN_CHUNKS
    attended = []
    selected = []
    for c in range(IN_CHUNKS):
        columns = slice(c * width, (c + 1) * width)
        weight = output_weight[:, columns]
        outgoing = jnp.dot(values[half_tokens:], weight, preferred_element_type=f32).astype(bf16)
        incoming = swap(outgoing, "ffn", ffn_masks[0])
        part = jnp.dot(values[:half_tokens], weight, preferred_element_type=f32)
        part = reduce_rows(part + incoming.astype(f32), "ffn", ffn_masks[1:])
        state = residual_rows[:, columns].astype(f32) + part
        attended.append(state.astype(bf16))
        gained = (state * norm_gain[None, columns]).astype(bf16)
        gained = gather_rows(gained, "ffn")
        rows = jnp.dot(selector, gained, preferred_element_type=f32).astype(bf16)
        selected.append(gather_rows(rows, "attn"))
    attended = jnp.concatenate(attended, axis=1).reshape(reqs, steps, model_width)

    gate_part = up_part = squares = logits = 0.0
    for c in range(IN_CHUNKS):
        columns = slice(c * width, (c + 1) * width)
        rows = selected[c]
        gate_part += jnp.dot(rows, gate_weight[0, columns], preferred_element_type=f32)
        up_part += jnp.dot(rows, up_weight[0, columns], preferred_element_type=f32)
        inverse_gain = 1.0 / norm_gain[None, columns]
        squares += jnp.sum(jnp.square(rows.astype(f32) * inverse_gain), axis=1, keepdims=True)
        logits += jnp.dot(rows[:capacity], router[columns], preferred_element_type=f32)
    scale = lax.rsqrt(squares / model_width + NORM_EPSILON)
    hidden = (jax.nn.silu(gate_part * scale) * (up_part * scale)).astype(bf16)
    affinity = jax.nn.sigmoid(logits * scale[:capacity])
    expert = lax.broadcasted_iota(jnp.int32, affinity.shape, 1)
    mine = jnp.sum(jnp.where(expert == ffn_index, affinity, 0.0), axis=1, keepdims=True)
    other = jnp.sum(jnp.where(expert == partner_id[:, None], affinity, 0.0), axis=1, keepdims=True)
    share = 2.5 * mine / (mine + other)

    half_rows = hidden.shape[0] // 2
    width = model_width // OUT_CHUNKS
    spread = (((0,), (0,)), ((), ()))
    result = []
    for c in range(OUT_CHUNKS):
        columns = slice(c * width, (c + 1) * width)
        weight = down_weight[0][:, columns]
        outgoing = jnp.dot(hidden[half_rows:], weight, preferred_element_type=f32).astype(bf16)
        incoming = swap(outgoing, "attn", attn_masks[0])
        part = jnp.dot(hidden[:half_rows], weight, preferred_element_type=f32)
        part = reduce_rows(part + incoming.astype(f32), "attn", attn_masks[1:])
        rows = (part * share).astype(bf16)
        outgoing = lax.dot_general(
            selector[:, half_tokens:], rows, spread, preferred_element_type=f32
        ).astype(bf16)
        incoming = swap(outgoing, "ffn", ffn_masks[0])
        part = lax.dot_general(
            selector[:, :half_tokens], rows, spread, preferred_element_type=f32
        )
        part = reduce_rows(part + incoming.astype(f32), "ffn", ffn_masks[1:])
        result.append(part.astype(bf16))
    result = jnp.concatenate(result, axis=1).reshape(reqs, steps, model_width)
    return attended, result


def solution(mesh):
    return jax.shard_map(
        local,
        mesh=mesh,
        in_specs=(
            P(("attn", "ffn"), None, None, None),
            P(("attn", "ffn"), None, None),
            P(("attn", "ffn"), None, None),
            P(("attn", "ffn")),
            P("ffn", None),
            P(("attn", "ffn"), None, None),
            P("ffn", None, None),
            P("ffn", None),
            P(),
            P(),
            P("attn", None, None),
            P("ffn", None, "attn"),
            P("ffn", None, "attn"),
            P("ffn", "attn", None),
        ),
        out_specs=(P(("attn", "ffn"), None, None), P(("attn", "ffn"), None, None)),
        check_vma=False,
    )
```

time: 575 us -> 239 us (0.42)
  waiting for transfers between devices: 314 us -> 88.2 us
  blocking collectives: 147 us -> 31.4 us
  starting transfers between devices: 10.2 us -> 57.9 us
  local copies, waits for them, and re-layouts: 36.8 us -> 16.8 us
  between operations: 14.7 us -> 1.3 us
  other arithmetic: 12.7 us -> 2.57 us
  Pallas kernels: 0 us -> 10 us
  matrix products: 38.6 us -> 30.6 us
    unnamed x1 -> x0, blocking collectives: 147 us -> none
    psum x1 -> x0, waiting for transfers between devices: 140 us -> none  [local(): state_rows = lax.psum(partial_out + placed_rows, 'ffn')]
    reduce_scatter x1 -> x0, waiting for transfers between devices: 60.4 us -> none  [local(): lax.psum_scatter(jnp.dot(rows_in, down_local, preferred_element_type=jnp....]
    ppermute x4 -> x27, starting transfers between devices: 3.23 us -> 50.5 us  [the longest x26 50.3 us: swap(): return lax.ppermute(value, axis, [(i, i ^ mask) for i in range(count)])]
    all_gather x0 -> x1, blocking collectives: none -> 31.4 us  [local(): moved = lax.all_gather(handoff[0], 'ffn', axis=0)[sources]]
    all_gather x1 -> x0, waiting for transfers between devices: 30.6 us -> none  [local(): rows_in = lax.all_gather(expert_input, 'attn', axis=0, tiled=True)]
    ppermute x4 -> x27, waiting for transfers between devices: 57.8 us -> 88.2 us  [the longest x26 83 us: swap(): return lax.ppermute(value, axis, [(i, i ^ mask) for i in range(count)])]
    all_to_all x1, waiting for transfers between devices: 25.2 us -> 0.01 us  [local(): lax.all_to_all(latents, 'ffn', split_axis=0, concat_axis=0, tiled=True)]
  transfers between devices with their start and end apart: 8 -> 28, of which waited for: 5 -> 18; matrix products, arithmetic and copies ran while one was open for 3% -> 10% of each run, Pallas kernels for 0% -> 0%
where the time goes in v1:
time: 239 us
  waiting for transfers between devices  88.2 us (37%)
  starting transfers between devices  57.9 us (24%)
  blocking collectives  31.4 us (13%)
  matrix products  30.6 us (13%)
  local copies, waits for them, and re-layouts  16.8 us (7%)
  Pallas kernels  10 us (4%)
  other arithmetic  2.57 us (1%)
    ppermute x26, waiting for transfers between devices, swap(): return lax.ppermute(value, axis, [(i, i ^ mask) for i in range(count)])  83 us
    ppermute x26, starting transfers between devices, swap(): return lax.ppermute(value, axis, [(i, i ^ mask) for i in range(count)])  50.3 us
    all_gather x1, blocking collectives, local(): moved = lax.all_gather(handoff[0], 'ffn', axis=0)[sources]  31.4 us
    unnamed x44, local copies, waits for them, and re-layouts  13.1 us
    dot_general x2, matrix products, local(): jnp.dot(values[half_tokens:], weight, preferred_element_type=f32)  9.07 us
    pallas_call x1, Pallas kernels, attend(): pl.pallas_call(functools.partial(attend_kernel, heads_local), out_shape=j...  7.6 us
    all_to_all x1, starting transfers between devices, local(): lax.all_to_all(latents, 'ffn', split_axis=0, concat_axis=0, tiled=True)  7.42 us
    dot_general x2, matrix products, local(): part = jnp.dot(values[:half_tokens], weight, preferred_element_type=f32)  5.87 us
  transfers between devices with their start and end apart: 28, of which 18 were waited for; matrix products, arithmetic and copies ran while one was open for 10% of the time, Pallas kernels for 0%

profile of v1, /device:TPU:0, one launch (start us, length us, event | category | flops | bytes accessed | tf_op | source)
XLA Modules:
  0.0 238.8 jit_solution(2432364656452480273)
XLA Ops:
  0.7 7.8 %copy.30.cache_ref = bf16[8,512,576]{2,1,0:T(8,128)(2,1)} copy(bf16[8,512,576]{1,2,0:T(8,128)(2,1)} %param.16) | data formatting | bytes 9437184 | tf_op args[1]
  11.0 7.6 %attend.1 = bf16[8,8,16,512]{3,2,1,0:T(8,128)(2,1)} custom-call(s32[8]{0:T(128)S(1)} %copy-done.4, bf16[8,128,576]{2,1,0:T(8,128)(2,1)S(1)} %bitcast.37, bf16[8,512,576]{2,1,0:T(8,128)(2,1)S(1)} %copy-done, bf16[8,2,576]{2,1,0:T(2,128)(2,1)S(1)} %copy-done.3), custom_call_target="tpu_custom_call" | custom-call | tf_op jit(solution)/shard_map/attend/pallas_call | solution.py:98
  18.6 7.4 %all-to-all-start = ((bf16[8,8,16,512]{3,2,1,0:T(8,128)(2,1)}), bf16[8,8,16,512]{3,2,1,0:T(8,128)(2,1)S(1)}, u32[]{:S(2)}, u32[]{:S(2)}) async-start(bf16[8,8,16,512]{3,2,1,0:T(8,128)(2,1)} %attend.1), calls=%async_computation | async-start | bytes 2097152 | tf_op jit(solution)/shard_map/all_to_all | solution.py:200
  26.2 31.4 %all-gather = s32[8,1,8]{2,1,0:T(1,128)S(1)} all-gather(s32[1,1,8]{2,1,0:T(1,128)S(1)} %bitcast.45), channel_id=1, replica_groups=mesh['attn'=4,'ffn'=8] {'ffn'}, dimensions={0}, use_global_device_ids=true | all-gather | bytes 288 | tf_op jit(solution)/shard_map/all_gather | solution.py:196
  62.1 5.1 %collective-permute-done = bf16[128,1024]{1,0:T(8,128)(2,1)S(1)} collective-permute-done((bf16[128,1024]{1,0:T(8,128)(2,1)S(1)}, bf16[128,1024]{1,0:T(8,128)(2,1)S(1)}, u32[]{:S(2)}, u32[]{:S(2)}) %collective-permute-start) | collective-permute-done | bytes 262176 | tf_op jit(solution)/shard_map/ppermute | solution.py:202
  67.3 4.6 %fusion.17 = bf16[64,3584]{1,0:T(8,128)(2,1)S(1)} fusion(bf16[1024,7168]{1,0:T(8,128)(2,1)} %param.22, bf16[128,1024]{1,0:T(8,128)(2,1)S(1)} %broadcast_select_fusion), kind=kOutput, calls=%fused_computation.17 | convolution fusion | flops 469991424 | bytes 7929856 | tf_op jit(solution)/shard_map/dot_general | solution.py:213
  74.0 4.5 %fusion.14 = bf16[64,3584]{1,0:T(8,128)(2,1)S(1)} fusion(bf16[1024,7168]{1,0:T(8,128)(2,1)} %param.22, bf16[128,1024]{1,0:T(8,128)(2,1)S(1)} %broadcast_select_fusion), kind=kOutput, calls=%fused_computation.16 | convolution fusion | flops 469991424 | bytes 7929856 | tf_op jit(solution)/shard_map/dot_general | solution.py:213
  78.7 6.7 %collective-permute-done.4 = bf16[64,3584]{1,0:T(8,128)(2,1)S(1)} collective-permute-done((bf16[64,3584]{1,0:T(8,128)(2,1)S(1)}, bf16[64,3584]{1,0:T(8,128)(2,1)S(1)}, u32[]{:S(2)}, u32[]{:S(2)}) %collective-permute-start.4) | collective-permute-done | bytes 458784 | tf_op jit(solution)/shard_map/ppermute | solution.py:22
  85.5 4.5 %fusion.11 = f32[64,3584]{1,0:T(8,128)S(1)} fusion(bf16[1024,7168]{1,0:T(8,128)(2,1)} %param.22, bf16[64,3584]{1,0:T(8,128)(2,1)S(1)} %collective-permute-done.4, bf16[128,1024]{1,0:T(8,128)(2,1)S(1)} %broadcast_select_fusion), kind=kOutput, calls=%fused_computation.15 | convolution fusion | flops 470220800 | bytes 8847360 | tf_op jit(solution)/shard_map/dot_general | solution.py:215
  90.0 3.7 %collective-permute-start.5 = (bf16[32,3584]{1,0:T(8,128)(2,1)S(1)}, bf16[32,3584]{1,0:T(8,128)(2,1)S(1)}, u32[]{:S(2)}, u32[]{:S(2)}) collective-permute-start(bf16[32,3584]{1,0:T(8,128)(2,1)S(1)} %slice.363), channel_id=1, source_target_pairs={{0,2},{1,3},{2,0},{3,1},{4,6},{5,7},{6,4},{7,5},{8,10},{9,11},{10,... | collective-permute-start | bytes 688136 | tf_op jit(solution)/shard_map/ppermute | solution.py:22
  95.2 3.4 %collective-permute-start.2 = (bf16[32,3584]{1,0:T(8,128)(2,1)S(1)}, bf16[32,3584]{1,0:T(8,128)(2,1)S(1)}, u32[]{:S(2)}, u32[]{:S(2)}) collective-permute-start(bf16[32,3584]{1,0:T(8,128)(2,1)S(1)} %slice.364), channel_id=1, source_target_pairs={{0,2},{1,3},{2,0},{3,1},{4,6},{5,7},{6,4},{7,5},{8,10},{9,11},{10,... | collective-permute-start | bytes 688136 | tf_op jit(solution)/shard_map/ppermute | solution.py:22
  101.0 3.5 %collective-permute-done.2 = bf16[32,3584]{1,0:T(8,128)(2,1)S(1)} collective-permute-done((bf16[32,3584]{1,0:T(8,128)(2,1)S(1)}, bf16[32,3584]{1,0:T(8,128)(2,1)S(1)}, u32[]{:S(2)}, u32[]{:S(2)}) %collective-permute-start.2) | collective-permute-done | bytes 229408 | tf_op jit(solution)/shard_map/ppermute | solution.py:22
  104.6 2.6 %collective-permute-start.3 = (bf16[16,3584]{1,0:T(8,128)(2,1)S(1)}, bf16[16,3584]{1,0:T(8,128)(2,1)S(1)}, u32[]{:S(2)}, u32[]{:S(2)}) collective-permute-start(bf16[16,3584]{1,0:T(8,128)(2,1)S(1)} %slice.368), channel_id=1, source_target_pairs={{0,4},{1,5},{2,6},{3,7},{4,0},{5,1},{6,2},{7,3},{8,12},{9,13},{10,... | collective-permute-start | bytes 344072 | tf_op jit(solution)/shard_map/ppermute | solution.py:22
  107.3 4.3 %collective-permute-done.3 = bf16[16,3584]{1,0:T(8,128)(2,1)S(1)} collective-permute-done((bf16[16,3584]{1,0:T(8,128)(2,1)S(1)}, bf16[16,3584]{1,0:T(8,128)(2,1)S(1)}, u32[]{:S(2)}, u32[]{:S(2)}) %collective-permute-start.3) | collective-permute-done | bytes 114720 | tf_op jit(solution)/shard_map/ppermute | solution.py:22
  115.0 3.4 %collective-permute-done.12 = bf16[16,3584]{1,0:T(8,128)(2,1)S(1)} collective-permute-done((bf16[16,3584]{1,0:T(8,128)(2,1)S(1)}, bf16[16,3584]{1,0:T(8,128)(2,1)S(1)}, u32[]{:S(2)}, u32[]{:S(2)}) %collective-permute-start.12) | collective-permute-done | bytes 114720 | tf_op jit(solution)/shard_map/ppermute | solution.py:22
  118.5 4.7 %collective-permute-start.13 = (bf16[32,3584]{1,0:T(8,128)(2,1)S(1)}, bf16[32,3584]{1,0:T(8,128)(2,1)S(1)}, u32[]{:S(2)}, u32[]{:S(2)}) collective-permute-start(bf16[32,3584]{1,0:T(8,128)(2,1)S(1)} %pad_maximum_fusion.8), channel_id=1, source_target_pairs={{0,2},{1,3},{2,0},{3,1},{4,6},{5,7},{6,4},{7,5},{8,10},{9,11},{10,... | collective-permute-start | bytes 688136 | tf_op jit(solution)/shard_map/ppermute | solution.py:22
  123.2 3.6 %collective-permute-start.8 = (bf16[32,3584]{1,0:T(8,128)(2,1)S(1)}, bf16[32,3584]{1,0:T(8,128)(2,1)S(1)}, u32[]{:S(2)}, u32[]{:S(2)}) collective-permute-start(bf16[32,3584]{1,0:T(8,128)(2,1)S(1)} %pad_maximum_fusion.7), channel_id=1, source_target_pairs={{0,2},{1,3},{2,0},{3,1},{4,6},{5,7},{6,4},{7,5},{8,10},{9,11},{10,... | collective-permute-start | bytes 688136 | tf_op jit(solution)/shard_map/ppermute | solution.py:22
  127.8 3.0 %collective-permute-done.8 = bf16[32,3584]{1,0:T(8,128)(2,1)S(1)} collective-permute-done((bf16[32,3584]{1,0:T(8,128)(2,1)S(1)}, bf16[32,3584]{1,0:T(8,128)(2,1)S(1)}, u32[]{:S(2)}, u32[]{:S(2)}) %collective-permute-start.8) | collective-permute-done | bytes 229408 | tf_op jit(solution)/shard_map/ppermute | solution.py:22
  131.4 7.9 %collective-permute-done.14 = bf16[64,3584]{1,0:T(8,128)(2,1)S(1)} collective-permute-done((bf16[64,3584]{1,0:T(8,128)(2,1)S(1)}, bf16[64,3584]{1,0:T(8,128)(2,1)S(1)}, u32[]{:S(2)}, u32[]{:S(2)}) %collective-permute-start.14) | collective-permute-done | bytes 458784 | tf_op jit(solution)/shard_map/ppermute | solution.py:22
  139.6 4.8 %collective-permute-start.15 = (bf16[64,3584]{1,0:T(8,128)(2,1)S(1)}, bf16[64,3584]{1,0:T(8,128)(2,1)S(1)}, u32[]{:S(2)}, u32[]{:S(2)}) collective-permute-start(bf16[64,3584]{1,0:T(8,128)(2,1)S(1)} %convolution_convert_fusion.4), channel_id=1, source_target_pairs={{0,16},{8,24},{16,0},{24,8},{1,17},{9,25},{17,1},{25,9},{2,18},{10... | collective-permute-start | bytes 1376264 | tf_op jit(solution)/shard_map/ppermute | solution.py:22
  144.7 4.6 %collective-permute-start.10 = (bf16[64,3584]{1,0:T(8,128)(2,1)S(1)}, bf16[64,3584]{1,0:T(8,128)(2,1)S(1)}, u32[]{:S(2)}, u32[]{:S(2)}) collective-permute-start(bf16[64,3584]{1,0:T(8,128)(2,1)S(1)} %convolution_convert_fusion.5), channel_id=1, source_target_pairs={{0,16},{8,24},{16,0},{24,8},{1,17},{9,25},{17,1},{25,9},{2,18},{10... | collective-permute-start | bytes 1376264 | tf_op jit(solution)/shard_map/ppermute | solution.py:22
  149.3 4.4 %collective-permute-done.15 = bf16[64,3584]{1,0:T(8,128)(2,1)S(1)} collective-permute-done((bf16[64,3584]{1,0:T(8,128)(2,1)S(1)}, bf16[64,3584]{1,0:T(8,128)(2,1)S(1)}, u32[]{:S(2)}, u32[]{:S(2)}) %collective-permute-start.15) | collective-permute-done | bytes 458784 | tf_op jit(solution)/shard_map/ppermute | solution.py:22
  153.9 4.8 %collective-permute-done.10 = bf16[64,3584]{1,0:T(8,128)(2,1)S(1)} collective-permute-done((bf16[64,3584]{1,0:T(8,128)(2,1)S(1)}, bf16[64,3584]{1,0:T(8,128)(2,1)S(1)}, u32[]{:S(2)}, u32[]{:S(2)}) %collective-permute-start.10) | collective-permute-done | bytes 458784 | tf_op jit(solution)/shard_map/ppermute | solution.py:22
  173.4 2.7 %convert_add_fusion = f32[128,3584]{1,0:T(8,128)S(1)} fusion(bf16[128,3584]{1,0:T(8,128)(2,1)S(1)} %collective-permute-done.22, bf16[512,7168]{1,0:T(8,128)(2,1)} %bitcast.38, bf16[256,512]{1,0:T(8,128)(2,1)S(1)} %multiply_convert_fusion), kind=kOutput, calls=%fused_computation.44 | convolution fusion | flops 470679552 | bytes 6553600 | tf_op jit(solution)/shard_map/dot_general | solution.py:251
  178.2 2.8 %convert_add_fusion.1 = f32[128,3584]{1,0:T(8,128)S(1)} fusion(bf16[128,3584]{1,0:T(8,128)(2,1)S(1)} %collective-permute-done.17, bf16[512,7168]{1,0:T(8,128)(2,1)} %bitcast.39, bf16[256,512]{1,0:T(8,128)(2,1)S(1)} %multiply_convert_fusion), kind=kOutput, calls=%fused_computation.45 | convolution fusion | flops 470679552 | bytes 6553600 | tf_op jit(solution)/shard_map/dot_general | solution.py:251
  181.9 8.0 %collective-permute-done.23 = bf16[64,3584]{1,0:T(8,128)(2,1)S(1)} collective-permute-done((bf16[64,3584]{1,0:T(8,128)(2,1)S(1)}, bf16[64,3584]{1,0:T(8,128)(2,1)S(1)}, u32[]{:S(2)}, u32[]{:S(2)}) %collective-permute-start.23) | collective-permute-done | bytes 458784 | tf_op jit(solution)/shard_map/ppermute | solution.py:22
  189.9 9.0 %collective-permute-done.18 = bf16[64,3584]{1,0:T(8,128)(2,1)S(1)} collective-permute-done((bf16[64,3584]{1,0:T(8,128)(2,1)S(1)}, bf16[64,3584]{1,0:T(8,128)(2,1)S(1)}, u32[]{:S(2)}, u32[]{:S(2)}) %collective-permute-start.18) | collective-permute-done | bytes 458784 | tf_op jit(solution)/shard_map/ppermute | solution.py:22
  202.9 10.2 %collective-permute-done.19 = bf16[64,3584]{1,0:T(8,128)(2,1)S(1)} collective-permute-done((bf16[64,3584]{1,0:T(8,128)(2,1)S(1)}, bf16[64,3584]{1,0:T(8,128)(2,1)S(1)}, u32[]{:S(2)}, u32[]{:S(2)}) %collective-permute-start.19) | collective-permute-done | bytes 458784 | tf_op jit(solution)/shard_map/ppermute | solution.py:22
  213.6 7.7 %collective-permute-done.24 = bf16[64,3584]{1,0:T(8,128)(2,1)S(1)} collective-permute-done((bf16[64,3584]{1,0:T(8,128)(2,1)S(1)}, bf16[64,3584]{1,0:T(8,128)(2,1)S(1)}, u32[]{:S(2)}, u32[]{:S(2)}) %collective-permute-start.24) | collective-permute-done | bytes 458784 | tf_op jit(solution)/shard_map/ppermute | solution.py:22
  221.8 5.2 %collective-permute-start.21 = (bf16[16,3584]{1,0:T(8,128)(2,1)S(1)}, bf16[16,3584]{1,0:T(8,128)(2,1)S(1)}, u32[]{:S(2)}, u32[]{:S(2)}) collective-permute-start(bf16[16,3584]{1,0:T(8,128)(2,1)S(1)} %slice.366), channel_id=1, source_target_pairs={{0,4},{1,5},{2,6},{3,7},{4,0},{5,1},{6,2},{7,3},{8,12},{9,13},{10,... | collective-permute-start | bytes 344072 | tf_op jit(solution)/shard_map/ppermute | solution.py:22
  229.4 3.4 %collective-permute-start.26 = (bf16[16,3584]{1,0:T(8,128)(2,1)S(1)}, bf16[16,3584]{1,0:T(8,128)(2,1)S(1)}, u32[]{:S(2)}, u32[]{:S(2)}) collective-permute-start(bf16[16,3584]{1,0:T(8,128)(2,1)S(1)} %slice.365), channel_id=1, source_target_pairs={{0,4},{1,5},{2,6},{3,7},{4,0},{5,1},{6,2},{7,3},{8,12},{9,13},{10,... | collective-permute-start | bytes 344072 | tf_op jit(solution)/shard_map/ppermute | solution.py:22
  232.8 5.1 %collective-permute-done.26 = bf16[16,3584]{1,0:T(8,128)(2,1)S(1)} collective-permute-done((bf16[16,3584]{1,0:T(8,128)(2,1)S(1)}, bf16[16,3584]{1,0:T(8,128)(2,1)S(1)}, u32[]{:S(2)}, u32[]{:S(2)}) %collective-permute-start.26) | collective-permute-done | bytes 114720 | tf_op jit(solution)/shard_map/ppermute | solution.py:22
  (152 shorter events, 45.1 us)
Async XLA Ops:
  10.9 46.6 %copy-start.10 = (s32[8]{0:T(128)S(1)}, s32[8]{0:T(128)}, u32[]{:S(2)}) copy-start(s32[8]{0:T(128)} %constant.34.clone) | copy-start | bytes 100
  10.9 47.8 %copy-start.2 = (bf16[8,512,128]{2,1,0:T(8,128)(2,1)S(1)}, bf16[8,512,128]{2,1,0:T(8,128)(2,1)}, u32[]{:S(2)}) copy-start(bf16[8,512,128]{2,1,0:T(8,128)(2,1)} %up_ref.1) | copy-start | bytes 3145732
  18.6 43.2 %copy-start.5 = (bf16[8,2,7168]{2,1,0:T(2,128)(2,1)S(1)}, bf16[8,2,7168]{2,1,0:T(2,128)(2,1)}, u32[]{:S(2)}) copy-start(bf16[8,2,7168]{2,1,0:T(2,128)(2,1)} %param.20) | copy-start | bytes 688132
  18.6 40.2 %all-to-all-start = ((bf16[8,8,16,512]{3,2,1,0:T(8,128)(2,1)}), bf16[8,8,16,512]{3,2,1,0:T(8,128)(2,1)S(1)}, u32[]{:S(2)}, u32[]{:S(2)}) async-start(bf16[8,8,16,512]{3,2,1,0:T(8,128)(2,1)} %attend.1), calls=%async_computation | async-start | bytes 2097152 | tf_op jit(solution)/shard_map/all_to_all | solution.py:200
  61.2 6.0 %collective-permute-start = (bf16[128,1024]{1,0:T(8,128)(2,1)S(1)}, bf16[128,1024]{1,0:T(8,128)(2,1)S(1)}, u32[]{:S(2)}, u32[]{:S(2)}) collective-permute-start(bf16[128,1024]{1,0:T(8,128)(2,1)S(1)} %values.1), channel_id=1, source_target_pairs={{0,8},{8,16},{16,24},{24,0},{1,9},{9,17},{17,25},{25,1},{2,10},{10... | collective-permute-start | bytes 786440 | tf_op jit(solution)/shard_map/ppermute | solution.py:202
  71.9 13.5 %collective-permute-start.4 = (bf16[64,3584]{1,0:T(8,128)(2,1)S(1)}, bf16[64,3584]{1,0:T(8,128)(2,1)S(1)}, u32[]{:S(2)}, u32[]{:S(2)}) collective-permute-start(bf16[64,3584]{1,0:T(8,128)(2,1)S(1)} %fusion.17), channel_id=1, source_target_pairs={{0,1},{1,0},{2,3},{3,2},{4,5},{5,4},{6,7},{7,6},{8,9},{9,8},{10,11... | collective-permute-start | bytes 1376264 | tf_op jit(solution)/shard_map/ppermute | solution.py:22
  78.5 15.2 %collective-permute-start.1 = (bf16[64,3584]{1,0:T(8,128)(2,1)S(1)}, bf16[64,3584]{1,0:T(8,128)(2,1)S(1)}, u32[]{:S(2)}, u32[]{:S(2)}) collective-permute-start(bf16[64,3584]{1,0:T(8,128)(2,1)S(1)} %fusion.14), channel_id=1, source_target_pairs={{0,1},{1,0},{2,3},{3,2},{4,5},{5,4},{6,7},{7,6},{8,9},{9,8},{10,11... | collective-permute-start | bytes 1376264 | tf_op jit(solution)/shard_map/ppermute | solution.py:22
  90.0 8.6 %collective-permute-start.5 = (bf16[32,3584]{1,0:T(8,128)(2,1)S(1)}, bf16[32,3584]{1,0:T(8,128)(2,1)S(1)}, u32[]{:S(2)}, u32[]{:S(2)}) collective-permute-start(bf16[32,3584]{1,0:T(8,128)(2,1)S(1)} %slice.363), channel_id=1, source_target_pairs={{0,2},{1,3},{2,0},{3,1},{4,6},{5,7},{6,4},{7,5},{8,10},{9,11},{10,... | collective-permute-start | bytes 688136 | tf_op jit(solution)/shard_map/ppermute | solution.py:22
  95.2 9.3 %collective-permute-start.2 = (bf16[32,3584]{1,0:T(8,128)(2,1)S(1)}, bf16[32,3584]{1,0:T(8,128)(2,1)S(1)}, u32[]{:S(2)}, u32[]{:S(2)}) collective-permute-start(bf16[32,3584]{1,0:T(8,128)(2,1)S(1)} %slice.364), channel_id=1, source_target_pairs={{0,2},{1,3},{2,0},{3,1},{4,6},{5,7},{6,4},{7,5},{8,10},{9,11},{10,... | collective-permute-start | bytes 688136 | tf_op jit(solution)/shard_map/ppermute | solution.py:22
  98.7 8.6 %collective-permute-start.6 = (bf16[16,3584]{1,0:T(8,128)(2,1)S(1)}, bf16[16,3584]{1,0:T(8,128)(2,1)S(1)}, u32[]{:S(2)}, u32[]{:S(2)}) collective-permute-start(bf16[16,3584]{1,0:T(8,128)(2,1)S(1)} %slice.367), channel_id=1, source_target_pairs={{0,4},{1,5},{2,6},{3,7},{4,0},{5,1},{6,2},{7,3},{8,12},{9,13},{10,... | collective-permute-start | bytes 344072 | tf_op jit(solution)/shard_map/ppermute | solution.py:22
  104.6 7.0 %collective-permute-start.3 = (bf16[16,3584]{1,0:T(8,128)(2,1)S(1)}, bf16[16,3584]{1,0:T(8,128)(2,1)S(1)}, u32[]{:S(2)}, u32[]{:S(2)}) collective-permute-start(bf16[16,3584]{1,0:T(8,128)(2,1)S(1)} %slice.368), channel_id=1, source_target_pairs={{0,4},{1,5},{2,6},{3,7},{4,0},{5,1},{6,2},{7,3},{8,12},{9,13},{10,... | collective-permute-start | bytes 344072 | tf_op jit(solution)/shard_map/ppermute | solution.py:22
  111.7 6.8 %collective-permute-start.12 = (bf16[16,3584]{1,0:T(8,128)(2,1)S(1)}, bf16[16,3584]{1,0:T(8,128)(2,1)S(1)}, u32[]{:S(2)}, u32[]{:S(2)}) collective-permute-start(bf16[16,3584]{1,0:T(8,128)(2,1)S(1)} %get-tuple-element.11), channel_id=1, source_target_pairs={{0,4},{1,5},{2,6},{3,7},{4,0},{5,1},{6,2},{7,3},{8,12},{9,13},{10,... | collective-permute-start | bytes 344072 | tf_op jit(solution)/shard_map/ppermute | solution.py:22
  113.5 9.7 %collective-permute-start.7 = (bf16[16,3584]{1,0:T(8,128)(2,1)S(1)}, bf16[16,3584]{1,0:T(8,128)(2,1)S(1)}, u32[]{:S(2)}, u32[]{:S(2)}) collective-permute-start(bf16[16,3584]{1,0:T(8,128)(2,1)S(1)} %get-tuple-element.6), channel_id=1, source_target_pairs={{0,4},{1,5},{2,6},{3,7},{4,0},{5,1},{6,2},{7,3},{8,12},{9,13},{10,... | collective-permute-start | bytes 344072 | tf_op jit(solution)/shard_map/ppermute | solution.py:22
  118.5 8.7 %collective-permute-start.13 = (bf16[32,3584]{1,0:T(8,128)(2,1)S(1)}, bf16[32,3584]{1,0:T(8,128)(2,1)S(1)}, u32[]{:S(2)}, u32[]{:S(2)}) collective-permute-start(bf16[32,3584]{1,0:T(8,128)(2,1)S(1)} %pad_maximum_fusion.8), channel_id=1, source_target_pairs={{0,2},{1,3},{2,0},{3,1},{4,6},{5,7},{6,4},{7,5},{8,10},{9,11},{10,... | collective-permute-start | bytes 688136 | tf_op jit(solution)/shard_map/ppermute | solution.py:22
  123.2 7.6 %collective-permute-start.8 = (bf16[32,3584]{1,0:T(8,128)(2,1)S(1)}, bf16[32,3584]{1,0:T(8,128)(2,1)S(1)}, u32[]{:S(2)}, u32[]{:S(2)}) collective-permute-start(bf16[32,3584]{1,0:T(8,128)(2,1)S(1)} %pad_maximum_fusion.7), channel_id=1, source_target_pairs={{0,2},{1,3},{2,0},{3,1},{4,6},{5,7},{6,4},{7,5},{8,10},{9,11},{10,... | collective-permute-start | bytes 688136 | tf_op jit(solution)/shard_map/ppermute | solution.py:22
  127.2 34.7 %slice-start.8 = ((s8[7340032]{0:T(1024)(128)(4,1)}), s8[4194304]{0:T(1024)(128)(4,1)S(1)}, s32[]{:S(2)}) async-start(s8[7340032]{0:T(1024)(128)(4,1)} %bitcast.50), calls=%async_computation.9 | async-start | bytes 8388608
  127.2 12.1 %collective-permute-start.14 = (bf16[64,3584]{1,0:T(8,128)(2,1)S(1)}, bf16[64,3584]{1,0:T(8,128)(2,1)S(1)}, u32[]{:S(2)}, u32[]{:S(2)}) collective-permute-start(bf16[64,3584]{1,0:T(8,128)(2,1)S(1)} %pad_maximum_fusion.5), channel_id=1, source_target_pairs={{0,1},{1,0},{2,3},{3,2},{4,5},{5,4},{6,7},{7,6},{8,9},{9,8},{10,11... | collective-permute-start | bytes 1376264 | tf_op jit(solution)/shard_map/ppermute | solution.py:22
  130.8 13.6 %collective-permute-start.9 = (bf16[64,3584]{1,0:T(8,128)(2,1)S(1)}, bf16[64,3584]{1,0:T(8,128)(2,1)S(1)}, u32[]{:S(2)}, u32[]{:S(2)}) collective-permute-start(bf16[64,3584]{1,0:T(8,128)(2,1)S(1)} %pad_maximum_fusion.4), channel_id=1, source_target_pairs={{0,1},{1,0},{2,3},{3,2},{4,5},{5,4},{6,7},{7,6},{8,9},{9,8},{10,11... | collective-permute-start | bytes 1376264 | tf_op jit(solution)/shard_map/ppermute | solution.py:22
  139.6 14.2 %collective-permute-start.15 = (bf16[64,3584]{1,0:T(8,128)(2,1)S(1)}, bf16[64,3584]{1,0:T(8,128)(2,1)S(1)}, u32[]{:S(2)}, u32[]{:S(2)}) collective-permute-start(bf16[64,3584]{1,0:T(8,128)(2,1)S(1)} %convolution_convert_fusion.4), channel_id=1, source_target_pairs={{0,16},{8,24},{16,0},{24,8},{1,17},{9,25},{17,1},{25,9},{2,18},{10... | collective-permute-start | bytes 1376264 | tf_op jit(solution)/shard_map/ppermute | solution.py:22
  144.7 13.9 %collective-permute-start.10 = (bf16[64,3584]{1,0:T(8,128)(2,1)S(1)}, bf16[64,3584]{1,0:T(8,128)(2,1)S(1)}, u32[]{:S(2)}, u32[]{:S(2)}) collective-permute-start(bf16[64,3584]{1,0:T(8,128)(2,1)S(1)} %convolution_convert_fusion.5), channel_id=1, source_target_pairs={{0,16},{8,24},{16,0},{24,8},{1,17},{9,25},{17,1},{25,9},{2,18},{10... | collective-permute-start | bytes 1376264 | tf_op jit(solution)/shard_map/ppermute | solution.py:22
  153.8 5.0 %collective-permute-start.16 = (bf16[128,3584]{1,0:T(8,128)(2,1)S(1)}, bf16[128,3584]{1,0:T(8,128)(2,1)S(1)}, u32[]{:S(2)}, u32[]{:S(2)}) collective-permute-start(bf16[128,3584]{1,0:T(8,128)(2,1)S(1)} %pad_maximum_fusion.3), channel_id=1, source_target_pairs={{0,8},{8,0},{16,24},{24,16},{1,9},{9,1},{17,25},{25,17},{2,10},{10... | collective-permute-start | bytes 2752520 | tf_op jit(solution)/shard_map/ppermute | solution.py:22
  158.7 2.5 %collective-permute-start.11 = (bf16[128,3584]{1,0:T(8,128)(2,1)S(1)}, bf16[128,3584]{1,0:T(8,128)(2,1)S(1)}, u32[]{:S(2)}, u32[]{:S(2)}) collective-permute-start(bf16[128,3584]{1,0:T(8,128)(2,1)S(1)} %pad_maximum_fusion.2), channel_id=1, source_target_pairs={{0,8},{8,0},{16,24},{24,16},{1,9},{9,1},{17,25},{25,17},{2,10},{10... | collective-permute-start | bytes 2752520 | tf_op jit(solution)/shard_map/ppermute | solution.py:22
  170.7 2.7 %collective-permute-start.22 = (bf16[128,3584]{1,0:T(8,128)(2,1)}, bf16[128,3584]{1,0:T(8,128)(2,1)S(1)}, u32[]{:S(2)}, u32[]{:S(2)}) collective-permute-start(bf16[128,3584]{1,0:T(8,128)(2,1)} %convolution_convert_fusion), channel_id=1, source_target_pairs={{0,8},{8,0},{16,24},{24,16},{1,9},{9,1},{17,25},{25,17},{2,10},{10... | collective-permute-start | bytes 2752520 | tf_op jit(solution)/shard_map/ppermute | solution.py:22
  172.4 5.8 %collective-permute-start.17 = (bf16[128,3584]{1,0:T(8,128)(2,1)}, bf16[128,3584]{1,0:T(8,128)(2,1)S(1)}, u32[]{:S(2)}, u32[]{:S(2)}) collective-permute-start(bf16[128,3584]{1,0:T(8,128)(2,1)} %convolution_convert_fusion.1), channel_id=1, source_target_pairs={{0,8},{8,0},{16,24},{24,16},{1,9},{9,1},{17,25},{25,17},{2,10},{10... | collective-permute-start | bytes 2752520 | tf_op jit(solution)/shard_map/ppermute | solution.py:22
  176.2 13.6 %collective-permute-start.23 = (bf16[64,3584]{1,0:T(8,128)(2,1)S(1)}, bf16[64,3584]{1,0:T(8,128)(2,1)S(1)}, u32[]{:S(2)}, u32[]{:S(2)}) collective-permute-start(bf16[64,3584]{1,0:T(8,128)(2,1)S(1)} %slice.359), channel_id=1, source_target_pairs={{0,16},{8,24},{16,0},{24,8},{1,17},{9,25},{17,1},{25,9},{2,18},{10... | collective-permute-start | bytes 1376264 | tf_op jit(solution)/shard_map/ppermute | solution.py:22
  181.1 17.8 %collective-permute-start.18 = (bf16[64,3584]{1,0:T(8,128)(2,1)S(1)}, bf16[64,3584]{1,0:T(8,128)(2,1)S(1)}, u32[]{:S(2)}, u32[]{:S(2)}) collective-permute-start(bf16[64,3584]{1,0:T(8,128)(2,1)S(1)} %slice.360), channel_id=1, source_target_pairs={{0,16},{8,24},{16,0},{24,8},{1,17},{9,25},{17,1},{25,9},{2,18},{10... | collective-permute-start | bytes 1376264 | tf_op jit(solution)/shard_map/ppermute | solution.py:22
  199.6 13.5 %collective-permute-start.19 = (bf16[64,3584]{1,0:T(8,128)(2,1)S(1)}, bf16[64,3584]{1,0:T(8,128)(2,1)S(1)}, u32[]{:S(2)}, u32[]{:S(2)}) collective-permute-start(bf16[64,3584]{1,0:T(8,128)(2,1)S(1)} %convolution_convert_fusion.3), channel_id=1, source_target_pairs={{0,1},{1,0},{2,3},{3,2},{4,5},{5,4},{6,7},{7,6},{8,9},{9,8},{10,11... | collective-permute-start | bytes 1376264 | tf_op jit(solution)/shard_map/ppermute | solution.py:22
  200.6 20.6 %collective-permute-start.24 = (bf16[64,3584]{1,0:T(8,128)(2,1)S(1)}, bf16[64,3584]{1,0:T(8,128)(2,1)S(1)}, u32[]{:S(2)}, u32[]{:S(2)}) collective-permute-start(bf16[64,3584]{1,0:T(8,128)(2,1)S(1)} %convolution_convert_fusion.2), channel_id=1, source_target_pairs={{0,1},{1,0},{2,3},{3,2},{4,5},{5,4},{6,7},{7,6},{8,9},{9,8},{10,11... | collective-permute-start | bytes 1376264 | tf_op jit(solution)/shard_map/ppermute | solution.py:22
  213.5 8.2 %collective-permute-start.20 = (bf16[32,3584]{1,0:T(8,128)(2,1)S(1)}, bf16[32,3584]{1,0:T(8,128)(2,1)S(1)}, u32[]{:S(2)}, u32[]{:S(2)}) collective-permute-start(bf16[32,3584]{1,0:T(8,128)(2,1)S(1)} %slice.362), channel_id=1, source_target_pairs={{0,2},{1,3},{2,0},{3,1},{4,6},{5,7},{6,4},{7,5},{8,10},{9,11},{10,... | collective-permute-start | bytes 688136 | tf_op jit(solution)/shard_map/ppermute | solution.py:22
  221.6 7.7 %collective-permute-start.25 = (bf16[32,3584]{1,0:T(8,128)(2,1)S(1)}, bf16[32,3584]{1,0:T(8,128)(2,1)S(1)}, u32[]{:S(2)}, u32[]{:S(2)}) collective-permute-start(bf16[32,3584]{1,0:T(8,128)(2,1)S(1)} %slice.361), channel_id=1, source_target_pairs={{0,2},{1,3},{2,0},{3,1},{4,6},{5,7},{6,4},{7,5},{8,10},{9,11},{10,... | collective-permute-start | bytes 688136 | tf_op jit(solution)/shard_map/ppermute | solution.py:22
  221.8 11.1 %collective-permute-start.21 = (bf16[16,3584]{1,0:T(8,128)(2,1)S(1)}, bf16[16,3584]{1,0:T(8,128)(2,1)S(1)}, u32[]{:S(2)}, u32[]{:S(2)}) collective-permute-start(bf16[16,3584]{1,0:T(8,128)(2,1)S(1)} %slice.366), channel_id=1, source_target_pairs={{0,4},{1,5},{2,6},{3,7},{4,0},{5,1},{6,2},{7,3},{8,12},{9,13},{10,... | collective-permute-start | bytes 344072 | tf_op jit(solution)/shard_map/ppermute | solution.py:22
  229.4 8.6 %collective-permute-start.26 = (bf16[16,3584]{1,0:T(8,128)(2,1)S(1)}, bf16[16,3584]{1,0:T(8,128)(2,1)S(1)}, u32[]{:S(2)}, u32[]{:S(2)}) collective-permute-start(bf16[16,3584]{1,0:T(8,128)(2,1)S(1)} %slice.365), channel_id=1, source_target_pairs={{0,4},{1,5},{2,6},{3,7},{4,0},{5,1},{6,2},{7,3},{8,12},{9,13},{10,... | collective-permute-start | bytes 344072 | tf_op jit(solution)/shard_map/ppermute | solution.py:22
  (17 other events, 200.4 us)

commit v2 on v1

v2 whole, which is shorter than its diff:
```python
import functools
import math

import jax
import jax.numpy as jnp
from jax import lax
from jax.experimental import pallas as pl
from jax.experimental.pallas import tpu as pltpu
from jax.sharding import PartitionSpec as P

KV_RANK = 512
SCORE_SCALE = 192.0 ** (-0.5)
NORM_EPSILON = 1e-06
MIB = 1024 * 1024
STATE_WIDTHS = (28, 28)
IN_WIDTHS = (14, 14, 14, 14)
OUT_WIDTHS = (14, 14, 14, 14)
PROJECT_TILE = 896
PROJECT_SPLITS = 4

f32 = jnp.float32
bf16 = jnp.bfloat16


def swap(value, axis, mask):
    count = lax.axis_size(axis)
    return lax.ppermute(value, axis, [(i, i ^ mask) for i in range(count)])


def column_ranges(shares, model_width):
    unit = model_width // sum(shares)
    return [(sum(shares[:i]) * unit, share * unit) for i, share in enumerate(shares)]


def masks_of(count):
    return [1 << k for k in range(count.bit_length() - 1)]


def relative_order(count):
    order = [0]
    for mask in reversed(masks_of(count)):
        order = order + [mask ^ o for o in order]
    return order


def gather_rows(rows, axis):
    for mask in reversed(masks_of(lax.axis_size(axis))):
        rows = jnp.concatenate([rows, swap(rows, axis, mask)], axis=0)
    return rows


def reduce_rows(rows, axis, masks):
    for mask in masks:
        half = rows.shape[0] // 2
        rows = rows[:half] + swap(rows[half:].astype(bf16), axis, mask).astype(f32)
    return rows


def in_hbm(array):
    return pltpu.with_memory_space_constraint(array, pltpu.HBM)


def attend_request(q, keys, fresh, live):
    row_count = q.shape[0]
    span = keys.shape[1]
    steps = fresh.shape[0]
    heads = row_count // steps
    old = jnp.dot(q, keys, preferred_element_type=f32) * SCORE_SCALE
    position = lax.broadcasted_iota(jnp.int32, (row_count, span), 1)
    old = jnp.where(position < live, old, -jnp.inf)
    step = lax.broadcasted_iota(jnp.int32, (row_count, 1), 0) // heads
    fresh = fresh.astype(f32)
    wide = q.astype(f32)
    peak = jnp.max(old, axis=1, keepdims=True)
    new = []
    for j in range(steps):
        score = jnp.sum(wide * fresh[j : j + 1], axis=1, keepdims=True) * SCORE_SCALE
        new.append(jnp.where(step >= j, score, -jnp.inf))
        peak = jnp.maximum(peak, new[j])
    old = jnp.exp(old - peak)
    new = [jnp.exp(score - peak) for score in new]
    total = jnp.sum(old, axis=1, keepdims=True)
    contract = (((1,), (1,)), ((), ()))
    mix = lax.dot_general(old.astype(bf16), keys[:KV_RANK], contract, preferred_element_type=f32)
    for j in range(steps):
        total = total + new[j]
        mix = mix + new[j] * fresh[j : j + 1, :KV_RANK]
    return mix * (1.0 / total)


def attend_kernel(masks, heads_local, lengths_ref, place_ref, q_ref, cache_ref, fresh_ref, *refs):
    outs, mix_ref = refs[:-1], refs[-1]
    count, steps = q_ref.shape[0], fresh_ref.shape[1]
    heads = q_ref.shape[1] // steps
    place = place_ref[0]
    base = pl.program_id(0) * count
    for r in range(count):
        mix_ref[r] = attend_request(q_ref[r], cache_ref[r], fresh_ref[r], lengths_ref[base + r])
        if masks is None:
            outs[0][r] = mix_ref[r].astype(bf16)
            continue
        for out_ref, pair in zip(outs, masks):
            for far, mask in enumerate(pair):
                first = (place ^ mask) * heads_local
                parts = [
                    mix_ref[r, pl.ds(pl.multiple_of(t * heads + first, 8), heads_local)]
                    for t in range(steps)
                ]
                out_ref[far, r] = jnp.concatenate(parts, axis=0).astype(bf16)


def attend(queries, latent_cache, fresh_latent, lengths, place, masks, heads_local):
    reqs, steps, heads, width = queries.shape
    span = latent_cache.shape[1]
    rows = steps * heads
    group = 4 if reqs % 4 == 0 else 1
    if masks is not None:
        rows_local = steps * heads_local
        out_shape = [
            jax.ShapeDtypeStruct((len(pair), reqs, rows_local, KV_RANK), bf16) for pair in masks
        ]
        out_specs = [
            pl.BlockSpec((len(pair), group, rows_local, KV_RANK), lambda r, n, p: (0, r, 0, 0))
            for pair in masks
        ]
    else:
        out_shape = [jax.ShapeDtypeStruct((reqs, rows, KV_RANK), bf16)]
        out_specs = [pl.BlockSpec((group, rows, KV_RANK), lambda r, n, p: (r, 0, 0))]
    return pl.pallas_call(
        functools.partial(attend_kernel, masks, heads_local),
        out_shape=out_shape,
        grid_spec=pltpu.PrefetchScalarGridSpec(
            num_scalar_prefetch=2,
            grid=(reqs // group,),
            in_specs=[
                pl.BlockSpec((group, rows, width), lambda r, n, p: (r, 0, 0)),
                pl.BlockSpec((group, width, span), lambda r, n, p: (r, 0, 0)),
                pl.BlockSpec((group, steps, width), lambda r, n, p: (r, 0, 0)),
            ],
            out_specs=out_specs,
            scratch_shapes=[pltpu.VMEM((group, rows, KV_RANK), f32)],
        ),
        compiler_params=pltpu.CompilerParams(vmem_limit_bytes=24 * MIB),
        cost_estimate=pl.CostEstimate(
            flops=4 * reqs * rows * span * width,
            bytes_accessed=2 * reqs * span * width,
            transcendentals=reqs * rows * span,
        ),
        name="attend",
    )(
        lengths,
        place[None],
        in_hbm(queries.reshape(reqs, rows, width)),
        in_hbm(latent_cache.transpose(0, 2, 1)),
        fresh_latent,
    )


def value_kernel(far, order, place_ref, *refs):
    latent_refs, up_ref, out_ref = refs[:-2], refs[-2], refs[-1]
    heads_local, _, v_head = up_ref.shape
    share = heads_local // len(order)
    place = place_ref[0]
    rows = jnp.concatenate([latent_ref[far] for latent_ref in latent_refs], axis=0)
    tokens = rows.shape[0] // heads_local
    for i in range(heads_local):
        own = (place ^ order[i // share]) * share + i % share if len(order) > 1 else i
        one = jnp.dot(rows, up_ref[i], preferred_element_type=f32)
        one = one.reshape(tokens, heads_local, v_head)
        head = lax.broadcasted_iota(jnp.int32, one.shape, 1)
        one = jnp.sum(jnp.where(head == own, one, 0.0), axis=1)
        first = own * v_head
        if len(order) > 1:
            first = pl.multiple_of(first, 128)
        out_ref[:, pl.ds(first, v_head)] = one.astype(bf16)


def values_of(latents, far, value_up, place, order):
    heads_local, _, v_head = value_up.shape
    pairs, reqs, rows, rank = latents[0].shape
    tokens = len(latents) * reqs * rows // heads_local
    whole = pl.BlockSpec(memory_space=pltpu.VMEM)
    return pl.pallas_call(
        functools.partial(value_kernel, far, order),
        out_shape=jax.ShapeDtypeStruct((tokens, heads_local * v_head), bf16),
        in_specs=[pl.BlockSpec(memory_space=pltpu.SMEM)] + [whole] * (len(latents) + 1),
        out_specs=whole,
        compiler_params=pltpu.CompilerParams(vmem_limit_bytes=12 * MIB),
        cost_estimate=pl.CostEstimate(
            flops=2 * tokens * heads_local * heads_local * rank * v_head,
            bytes_accessed=2 * value_up.size,
            transcendentals=0,
        ),
        name="values",
    )(place[None], *[x.reshape(pairs, reqs * rows, rank) for x in latents], value_up)


def values_here(queries, latent_cache, fresh_latent, lengths, value_up):
    n_attn, n_ffn = lax.axis_size("attn"), lax.axis_size("ffn")
    attn_index = lax.axis_index("attn").astype(jnp.int32)
    ffn_index = lax.axis_index("ffn").astype(jnp.int32)
    far = n_ffn // 2
    near = relative_order(far)
    heads_local, rank, v_head = value_up.shape
    reqs, steps = queries.shape[:2]
    if heads_local % 8 == 0 and heads_local % n_attn == 0:
        share = heads_local // n_attn
        part = lax.dynamic_slice_in_dim(value_up, attn_index * share, share, 0)
        partner_up = gather_rows(swap(part, "ffn", far), "attn")
        masks = [(m, m ^ far) for m in near]
        latents = attend(
            queries, latent_cache, fresh_latent, lengths, ffn_index, masks, heads_local
        )
        latents = [x if m == 0 else swap(x, "ffn", m) for x, m in zip(latents, near)]
        partner = values_of(latents, 1, partner_up, attn_index, relative_order(n_attn))
        arrived = swap(partner, "ffn", far)
        latents[0], _ = lax.optimization_barrier((latents[0], partner))
        return values_of(latents, 0, value_up, attn_index, [0]), arrived
    (latents,) = attend(queries, latent_cache, fresh_latent, lengths, ffn_index, None, heads_local)
    latents = latents.reshape(reqs, steps, n_ffn, heads_local, rank)
    latents = lax.all_to_all(latents, "ffn", split_axis=2, concat_axis=0, tiled=True)
    latents = latents.reshape(n_ffn, reqs * steps, heads_local, rank)
    values = []
    for flip in (0, far):
        rows = latents[ffn_index ^ jnp.array([m ^ flip for m in near], jnp.int32)]
        rows = rows.reshape(-1, heads_local, rank)
        rows = jnp.einsum("nhb,hbw->nhw", rows, value_up, preferred_element_type=f32)
        values.append(rows.astype(bf16).reshape(-1, heads_local * v_head))
    return values


def project_kernel(values_ref, *refs):
    weight_refs, (kept_ref, sent_ref) = refs[:-2], refs[-2:]
    half = kept_ref.shape[0]
    depth = weight_refs[0].shape[0]
    out = 0.0
    for i, weight_ref in enumerate(weight_refs):
        rows = values_ref[:, i * depth : (i + 1) * depth]
        out = out + jnp.dot(rows, weight_ref[...], preferred_element_type=f32)
    kept_ref[...] = out[:half]
    sent_ref[...] = out[half:].astype(bf16)


def project(values, weight, first, width):
    tokens, depth = values.shape
    tile = math.gcd(math.gcd(first, width), PROJECT_TILE)
    half = tokens // 2
    offset = first // tile
    splits = PROJECT_SPLITS
    weight_specs = [
        pl.BlockSpec((depth // splits, tile), lambda j, i=i: (i, offset + j)) for i in range(splits)
    ]
    return pl.pallas_call(
        project_kernel,
        out_shape=(
            jax.ShapeDtypeStruct((half, width), f32),
            jax.ShapeDtypeStruct((half, width), bf16),
        ),
        grid=(width // tile,),
        in_specs=[pl.BlockSpec((tokens, depth), lambda j: (0, 0)), *weight_specs],
        out_specs=(
            pl.BlockSpec((half, tile), lambda j: (0, j)),
            pl.BlockSpec((half, tile), lambda j: (0, j)),
        ),
        compiler_params=pltpu.CompilerParams(vmem_limit_bytes=12 * MIB),
        cost_estimate=pl.CostEstimate(
            flops=2 * tokens * depth * width, bytes_accessed=2 * depth * width, transcendentals=0
        ),
        name="project",
    )(values, *[in_hbm(weight)] * splits)


def local(
    queries,
    latent_cache,
    fresh_latent,
    lengths,
    handoff,
    residual,
    value_up_matrix,
    output_weight,
    norm_gain,
    router,
    expert_ids,
    gate_weight,
    up_weight,
    down_weight,
):
    n_attn = lax.axis_size("attn")
    n_ffn = lax.axis_size("ffn")
    attn_masks = masks_of(n_attn)
    ffn_masks = masks_of(n_ffn)
    order = relative_order(n_ffn)
    ffn_index = lax.axis_index("ffn").astype(jnp.int32)
    sources = ffn_index ^ jnp.array(order, jnp.int32)
    reqs, steps, model_width = residual.shape
    own_tokens = reqs * steps
    row_tokens = n_ffn * own_tokens
    heads_local = value_up_matrix.shape[0]

    ids = expert_ids.reshape(n_ffn, own_tokens, expert_ids.shape[2])[sources]
    ids = ids.reshape(row_tokens, expert_ids.shape[2])
    hit = jnp.sum((ids == ffn_index).astype(jnp.int32), axis=1)
    rank = jnp.cumsum(hit) - 1
    capacity = 4 * own_tokens
    slots = lax.broadcasted_iota(jnp.int32, (capacity, row_tokens), 0)
    chosen = (hit[None, :] == 1) & (rank[None, :] == slots)
    selector = chosen.astype(bf16)
    partner_id = jnp.sum(
        jnp.where(chosen, (jnp.sum(ids, axis=1) - ffn_index)[None, :], 0), axis=1
    )

    residual_rows = residual.reshape(own_tokens, model_width)
    half_tokens = row_tokens // 2
    moved = jnp.repeat(handoff[0] == 1, steps)[:, None]
    onward = [(i, (i + 1) % n_attn) for i in range(n_attn)]
    near_values, far_values = values_here(
        queries, latent_cache, fresh_latent, lengths, value_up_matrix
    )

    def near_sum(values, first, width):
        part, outgoing = project(values, output_weight, first, width)
        part = part + swap(outgoing, "ffn", ffn_masks[0]).astype(f32)
        return reduce_rows(part, "ffn", ffn_masks[1:-1])

    state_ranges = column_ranges(STATE_WIDTHS, model_width)
    near_sums = [near_sum(near_values, *columns) for columns in state_ranges]
    sums = []
    for part, columns in zip(near_sums, state_ranges):
        outgoing = near_sum(far_values, *columns).astype(bf16)
        part = part + swap(outgoing, "ffn", ffn_masks[-1]).astype(f32)
        arrived = lax.ppermute(part.astype(bf16), "attn", onward).astype(f32)
        sums.append(jnp.where(moved, arrived, part))

    def total_of(first, width):
        pieces = []
        for (start, wide), piece in zip(state_ranges, sums):
            low, high = max(first, start), min(first + width, start + wide)
            if low < high:
                pieces.append(piece[:, low - start : high - start])
        return pieces[0] if len(pieces) == 1 else jnp.concatenate(pieces, axis=1)

    attended = []
    selected = []
    for first, width in column_ranges(IN_WIDTHS, model_width):
        columns = slice(first, first + width)
        state = residual_rows[:, columns].astype(f32) + total_of(first, width)
        attended.append(state.astype(bf16))
        gained = (state * norm_gain[None, columns]).astype(bf16)
        gained = gather_rows(gained, "ffn")
        rows = jnp.dot(selector, gained, preferred_element_type=f32).astype(bf16)
        selected.append(gather_rows(rows, "attn"))
    attended = jnp.concatenate(attended, axis=1).reshape(reqs, steps, model_width)

    gate_part = up_part = squares = logits = 0.0
    for rows, (first, width) in zip(selected, column_ranges(IN_WIDTHS, model_width)):
        columns = slice(first, first + width)
        gate_part += jnp.dot(rows, gate_weight[0, columns], preferred_element_type=f32)
        up_part += jnp.dot(rows, up_weight[0, columns], preferred_element_type=f32)
        inverse_gain = 1.0 / norm_gain[None, columns]
        squares += jnp.sum(jnp.square(rows.astype(f32) * inverse_gain), axis=1, keepdims=True)
        logits += jnp.dot(rows[:capacity], router[columns], preferred_element_type=f32)
    scale = lax.rsqrt(squares / model_width + NORM_EPSILON)
    hidden = (jax.nn.silu(gate_part * scale) * (up_part * scale)).astype(bf16)
    affinity = jax.nn.sigmoid(logits * scale[:capacity])
    expert = lax.broadcasted_iota(jnp.int32, affinity.shape, 1)
    mine = jnp.sum(jnp.where(expert == ffn_index, affinity, 0.0), axis=1, keepdims=True)
    other = jnp.sum(jnp.where(expert == partner_id[:, None], affinity, 0.0), axis=1, keepdims=True)
    share = 2.5 * mine / (mine + other)
    weights = jnp.sum(jnp.where(chosen, share, 0.0), axis=0)[:, None]

    half_rows = hidden.shape[0] // 2
    spread = (((0,), (0,)), ((), ()))
    result = []
    for first, width in column_ranges(OUT_WIDTHS, model_width):
        weight = down_weight[0][:, first : first + width]
        outgoing = jnp.dot(hidden[half_rows:], weight, preferred_element_type=f32).astype(bf16)
        incoming = swap(outgoing, "attn", attn_masks[0])
        part = jnp.dot(hidden[:half_rows], weight, preferred_element_type=f32)
        part = reduce_rows(part + incoming.astype(f32), "attn", attn_masks[1:])
        rows = part.astype(bf16)
        outgoing = lax.dot_general(
            selector[:, half_tokens:], rows, spread, preferred_element_type=f32
        )
        outgoing = (outgoing * weights[half_tokens:]).astype(bf16)
        incoming = swap(outgoing, "ffn", ffn_masks[0])
        part = lax.dot_general(
            selector[:, :half_tokens], rows, spread, preferred_element_type=f32
        )
        part = part * weights[:half_tokens]
        part = reduce_rows(part + incoming.astype(f32), "ffn", ffn_masks[1:])
        result.append(part.astype(bf16))
    result = jnp.concatenate(result, axis=1).reshape(reqs, steps, model_width)
    return attended, result


def solution(mesh):
    return jax.shard_map(
        local,
        mesh=mesh,
        in_specs=(
            P(("attn", "ffn"), None, None, None),
            P(("attn", "ffn"), None, None),
            P(("attn", "ffn"), None, None),
            P(("attn", "ffn")),
            P("ffn", None),
            P(("attn", "ffn"), None, None),
            P("ffn", None, None),
            P("ffn", None),
            P(),
            P(),
            P("attn", None, None),
            P("ffn", None, "attn"),
            P("ffn", None, "attn"),
            P("ffn", "attn", None),
        ),
        out_specs=(P(("attn", "ffn"), None, None), P(("attn", "ffn"), None, None)),
        check_vma=False,
    )
```

time: 239 us -> 185 us (0.77)
  blocking collectives: 31.4 us -> 0 us
  Pallas kernels: 10 us -> 26.9 us
  matrix products: 30.6 us -> 14.2 us
  waiting for transfers between devices: 88.2 us -> 78.8 us
  local copies, waits for them, and re-layouts: 16.8 us -> 7.49 us
  starting transfers between devices: 57.9 us -> 53.2 us
    all_gather x1 -> x0, blocking collectives: 31.4 us -> none  [local(): moved = lax.all_gather(handoff[0], 'ffn', axis=0)[sources]]
    pallas_call x2 -> x7, Pallas kernels: 10 us -> 26.9 us  [the longest x4 17.9 us: project(): pl.pallas_call(project_kernel, out_shape=(jax.ShapeDtypeStruct((half, wid...]
    dot_general x4 -> x0, matrix products: 14.9 us -> none  [the longest x2 9.07 us: local(): jnp.dot(values[half_tokens:], weight, preferred_element_type=f32)]
    unnamed x44 -> x33, local copies, waits for them, and re-layouts: 13.1 us -> 3.46 us
    ppermute x26 -> x57, waiting for transfers between devices: 83 us -> 75.1 us  [swap(): return lax.ppermute(value, axis, [(i, i ^ mask) for i in range(count)])]
    all_to_all x1 -> x0, starting transfers between devices: 7.42 us -> none  [local(): lax.all_to_all(latents, 'ffn', split_axis=0, concat_axis=0, tiled=True)]
    dot_general x2 -> x4, matrix products: 5.51 us -> 1.68 us  [local(): part = jnp.dot(hidden[:half_rows], weight, preferred_element_type=f32)]
    ppermute x26 -> x57, starting transfers between devices: 50.3 us -> 52.9 us  [swap(): return lax.ppermute(value, axis, [(i, i ^ mask) for i in range(count)])]
  transfers between devices with their start and end apart: 28 -> 59, of which waited for: 18 -> 37; matrix products, arithmetic and copies ran while one was open for 10% -> 6% of each run, Pallas kernels for 0% -> 14%
where the time goes in v2:
time: 185 us
  waiting for transfers between devices  78.8 us (43%)
  starting transfers between devices  53.2 us (29%)
  Pallas kernels  26.9 us (15%)
  matrix products  14.2 us (8%)
  local copies, waits for them, and re-layouts  7.49 us (4%)
  other arithmetic  2.96 us (2%)
    ppermute x57, waiting for transfers between devices, swap(): return lax.ppermute(value, axis, [(i, i ^ mask) for i in range(count)])  75.1 us
    ppermute x57, starting transfers between devices, swap(): return lax.ppermute(value, axis, [(i, i ^ mask) for i in range(count)])  52.9 us
    pallas_call x4, Pallas kernels, project(): pl.pallas_call(project_kernel, out_shape=(jax.ShapeDtypeStruct((half, wid...  17.9 us
    pallas_call x1, Pallas kernels, attend(): pl.pallas_call(functools.partial(attend_kernel, masks, heads_local), out_...  6.38 us
    dot_general x4, matrix products, local(): up_part += jnp.dot(rows, up_weight[0, columns], preferred_element_type=f32)  4.27 us
    ppermute x2, waiting for transfers between devices, local(): arrived = lax.ppermute(part.astype(bf16), 'attn', onward).astype(f32)  3.73 us
  transfers between devices with their start and end apart: 59, of which 37 were waited for; matrix products, arithmetic and copies ran while one was open for 6% of the time, Pallas kernels for 14%

profile of v2, /device:TPU:0, one launch (start us, length us, event | category | flops | bytes accessed | tf_op | source)
XLA Modules:
  0.0 185.1 jit_solution(4716920245245923052)
XLA Ops:
  1.6 4.1 %collective-permute-start.3 = (bf16[2,512,128]{2,1,0:T(8,128)(2,1)S(1)}, bf16[2,512,128]{2,1,0:T(8,128)(2,1)S(1)}, u32[]{:S(2)}, u32[]{:S(2)}) collective-permute-start(bf16[2,512,128]{2,1,0:T(8,128)(2,1)S(1)} %constant_dynamic-slice_fusion), channel_id=1, source_target_pairs={{0,4},{1,5},{2,6},{3,7},{4,0},{5,1},{6,2},{7,3},{8,12},{9,13},{10,... | collective-permute-start | bytes 786440 | tf_op jit(solution)/shard_map/ppermute | solution.py:27
  7.1 6.4 %attend.1 = (bf16[2,8,16,512]{3,2,1,0:T(8,128)(2,1)S(1)}, bf16[2,8,16,512]{3,2,1,0:T(8,128)(2,1)S(1)}, bf16[2,8,16,512]{3,2,1,0:T(8,128)(2,1)S(1)}, bf16[2,8,16,512]{3,2,1,0:T(8,128)(2,1)S(1)}) custom-call(s32[8]{0:T(128)S(1)} %copy-done.2, s32[1]{0:T(128)} %bitcast.2.place_ref, bf16[8,128,576]{2,1,0:T(8,128)(2,1)} %bitcast.79, ...), custom_call_target="tpu_custom_call" | custom-call | flops 1207959552 | bytes 4718592 | tf_op jit(solution)/shard_map/attend/pallas_call | solution.py:129
  19.9 5.2 %collective-permute-done.4 = bf16[2,512,128]{2,1,0:T(8,128)(2,1)S(1)} collective-permute-done((bf16[2,512,128]{2,1,0:T(8,128)(2,1)S(1)}, bf16[2,512,128]{2,1,0:T(8,128)(2,1)S(1)}, u32[]{:S(2)}, u32[]{:S(2)}) %collective-permute-start.4) | collective-permute-done | bytes 262176 | tf_op jit(solution)/shard_map/ppermute | solution.py:27
  27.3 2.6 %collective-permute-done.2 = bf16[2,8,16,512]{3,2,1,0:T(8,128)(2,1)S(1)} collective-permute-done((bf16[2,8,16,512]{3,2,1,0:T(8,128)(2,1)S(1)}, bf16[2,8,16,512]{3,2,1,0:T(8,128)(2,1)S(1)}, u32[]{:S(2)}, u32[]{:S(2)}) %collective-permute-start.2) | collective-permute-done | bytes 262176 | tf_op jit(solution)/shard_map/ppermute | solution.py:27
  33.2 4.5 %project.6 = (f32[32,3584]{1,0:T(8,128)S(1)}, bf16[32,3584]{1,0:T(8,128)(2,1)S(1)}) custom-call(bf16[64,1024]{1,0:T(8,128)(2,1)S(1)} %values.3.values_ref, bf16[1024,7168]{1,0:T(8,128)(2,1)} %refs_3_.7, bf16[1024,7168]{1,0:T(8,128)(2,1)} %refs_3_.7, bf16[1024,7168]{1,0:T(8,128)(2,1)} %refs_3_.7, bf16[1024,7168]{1,0:T(8,128)(2,1)} %refs_3_.7), custom_call_target="tpu_custom_call" | custom-call | flops 469762048 | bytes 7340032 | tf_op jit(solution)/shard_map/project/pallas_call | solution.py:253
  39.3 4.5 %project.4 = (f32[32,3584]{1,0:T(8,128)S(1)}, bf16[32,3584]{1,0:T(8,128)(2,1)S(1)}) custom-call(bf16[64,1024]{1,0:T(8,128)(2,1)S(1)} %values.3.values_ref, bf16[1024,7168]{1,0:T(8,128)(2,1)} %refs_3_.7, bf16[1024,7168]{1,0:T(8,128)(2,1)} %refs_3_.7, bf16[1024,7168]{1,0:T(8,128)(2,1)} %refs_3_.7, bf16[1024,7168]{1,0:T(8,128)(2,1)} %refs_3_.7), custom_call_target="tpu_custom_call" | custom-call | flops 469762048 | bytes 7340032 | tf_op jit(solution)/shard_map/project/pallas_call | solution.py:253
  44.4 4.5 %project.7 = (f32[32,3584]{1,0:T(8,128)S(1)}, bf16[32,3584]{1,0:T(8,128)(2,1)S(1)}) custom-call(bf16[64,1024]{1,0:T(8,128)(2,1)S(1)} %collective-permute-done.8.values_ref, bf16[1024,7168]{1,0:T(8,128)(2,1)} %refs_3_.7, bf16[1024,7168]{1,0:T(8,128)(2,1)} %refs_3_.7, bf16[1024,7168]{1,0:T(8,128)(2,1)} %refs_3_.7, bf16[1024,7168]{1,0:T(8,128)(2,1)} %refs_3_.7), custom_call_target="tpu_custom_call" | custom-call | flops 469762048 | bytes 7340032 | tf_op jit(solution)/shard_map/project/pallas_call | solution.py:253
  50.4 4.4 %project.5 = (f32[32,3584]{1,0:T(8,128)S(1)}, bf16[32,3584]{1,0:T(8,128)(2,1)S(1)}) custom-call(bf16[64,1024]{1,0:T(8,128)(2,1)S(1)} %collective-permute-done.8.values_ref, bf16[1024,7168]{1,0:T(8,128)(2,1)} %refs_3_.7, bf16[1024,7168]{1,0:T(8,128)(2,1)} %refs_3_.7, bf16[1024,7168]{1,0:T(8,128)(2,1)} %refs_3_.7, bf16[1024,7168]{1,0:T(8,128)(2,1)} %refs_3_.7), custom_call_target="tpu_custom_call" | custom-call | flops 469762048 | bytes 7340032 | tf_op jit(solution)/shard_map/project/pallas_call | solution.py:253
  55.5 3.5 %collective-permute-start.14 = (bf16[16,3584]{1,0:T(8,128)(2,1)S(1)}, bf16[16,3584]{1,0:T(8,128)(2,1)S(1)}, u32[]{:S(2)}, u32[]{:S(2)}) collective-permute-start(bf16[16,3584]{1,0:T(8,128)(2,1)S(1)} %slice.594), channel_id=1, source_target_pairs={{0,2},{1,3},{2,0},{3,1},{4,6},{5,7},{6,4},{7,5},{8,10},{9,11},{10,... | collective-permute-start | bytes 344072 | tf_op jit(solution)/shard_map/ppermute | solution.py:27
  59.3 2.1 %collective-permute-start.16 = (bf16[16,3584]{1,0:T(8,128)(2,1)S(1)}, bf16[16,3584]{1,0:T(8,128)(2,1)S(1)}, u32[]{:S(2)}, u32[]{:S(2)}) collective-permute-start(bf16[16,3584]{1,0:T(8,128)(2,1)S(1)} %slice.593), channel_id=1, source_target_pairs={{0,2},{1,3},{2,0},{3,1},{4,6},{5,7},{6,4},{7,5},{8,10},{9,11},{10,... | collective-permute-start | bytes 344072 | tf_op jit(solution)/shard_map/ppermute | solution.py:27
  61.4 2.7 %collective-permute-start.10 = (bf16[16,3584]{1,0:T(8,128)(2,1)S(1)}, bf16[16,3584]{1,0:T(8,128)(2,1)S(1)}, u32[]{:S(2)}, u32[]{:S(2)}) collective-permute-start(bf16[16,3584]{1,0:T(8,128)(2,1)S(1)} %slice.595), channel_id=1, source_target_pairs={{0,2},{1,3},{2,0},{3,1},{4,6},{5,7},{6,4},{7,5},{8,10},{9,11},{10,... | collective-permute-start | bytes 344072 | tf_op jit(solution)/shard_map/ppermute | solution.py:27
  64.1 3.4 %collective-permute-done.16 = bf16[16,3584]{1,0:T(8,128)(2,1)S(1)} collective-permute-done((bf16[16,3584]{1,0:T(8,128)(2,1)S(1)}, bf16[16,3584]{1,0:T(8,128)(2,1)S(1)}, u32[]{:S(2)}, u32[]{:S(2)}) %collective-permute-start.16) | collective-permute-done | bytes 114720 | tf_op jit(solution)/shard_map/ppermute | solution.py:27
  67.8 2.0 %collective-permute-done.10 = bf16[16,3584]{1,0:T(8,128)(2,1)S(1)} collective-permute-done((bf16[16,3584]{1,0:T(8,128)(2,1)S(1)}, bf16[16,3584]{1,0:T(8,128)(2,1)S(1)}, u32[]{:S(2)}, u32[]{:S(2)}) %collective-permute-start.10) | collective-permute-done | bytes 114720 | tf_op jit(solution)/shard_map/ppermute | solution.py:27
  70.6 5.1 %collective-permute-done.17 = bf16[16,3584]{1,0:T(8,128)(2,1)S(1)} collective-permute-done((bf16[16,3584]{1,0:T(8,128)(2,1)S(1)}, bf16[16,3584]{1,0:T(8,128)(2,1)S(1)}, u32[]{:S(2)}, u32[]{:S(2)}) %collective-permute-start.17) | collective-permute-done | bytes 114720 | tf_op jit(solution)/shard_map/ppermute | solution.py:27
  75.8 2.3 %collective-permute-done.11 = bf16[16,3584]{1,0:T(8,128)(2,1)S(1)} collective-permute-done((bf16[16,3584]{1,0:T(8,128)(2,1)S(1)}, bf16[16,3584]{1,0:T(8,128)(2,1)S(1)}, u32[]{:S(2)}, u32[]{:S(2)}) %collective-permute-start.11) | collective-permute-done | bytes 114720 | tf_op jit(solution)/shard_map/ppermute | solution.py:27
  80.0 2.6 %collective-permute-done.12 = bf16[16,3584]{1,0:T(8,128)(2,1)S(1)} collective-permute-done((bf16[16,3584]{1,0:T(8,128)(2,1)S(1)}, bf16[16,3584]{1,0:T(8,128)(2,1)S(1)}, u32[]{:S(2)}, u32[]{:S(2)}) %collective-permute-start.12) | collective-permute-done | bytes 114720 | tf_op jit(solution)/shard_map/ppermute | solution.py:332
  83.7 2.9 %collective-permute-start.19 = (bf16[16,1792]{1,0:T(8,128)(2,1)S(1)}, bf16[16,1792]{1,0:T(8,128)(2,1)S(1)}, u32[]{:S(2)}, u32[]{:S(2)}) collective-permute-start(bf16[16,1792]{1,0:T(8,128)(2,1)S(1)} %get-tuple-element.37), channel_id=1, source_target_pairs={{0,4},{1,5},{2,6},{3,7},{4,0},{5,1},{6,2},{7,3},{8,12},{9,13},{10,... | collective-permute-start | bytes 172040 | tf_op jit(solution)/shard_map/ppermute | solution.py:27
  86.6 2.9 %collective-permute-start.29 = (bf16[16,1792]{1,0:T(8,128)(2,1)S(1)}, bf16[16,1792]{1,0:T(8,128)(2,1)S(1)}, u32[]{:S(2)}, u32[]{:S(2)}) collective-permute-start(bf16[16,1792]{1,0:T(8,128)(2,1)S(1)} %get-tuple-element.33), channel_id=1, source_target_pairs={{0,4},{1,5},{2,6},{3,7},{4,0},{5,1},{6,2},{7,3},{8,12},{9,13},{10,... | collective-permute-start | bytes 172040 | tf_op jit(solution)/shard_map/ppermute | solution.py:27
  89.5 2.2 %collective-permute-done.24 = bf16[16,1792]{1,0:T(8,128)(2,1)S(1)} collective-permute-done((bf16[16,1792]{1,0:T(8,128)(2,1)S(1)}, bf16[16,1792]{1,0:T(8,128)(2,1)S(1)}, u32[]{:S(2)}, u32[]{:S(2)}) %collective-permute-start.24) | collective-permute-done | bytes 57376 | tf_op jit(solution)/shard_map/ppermute | solution.py:27
  98.3 2.1 %collective-permute-done.20 = bf16[32,1792]{1,0:T(8,128)(2,1)S(1)} collective-permute-done((bf16[32,1792]{1,0:T(8,128)(2,1)S(1)}, bf16[32,1792]{1,0:T(8,128)(2,1)S(1)}, u32[]{:S(2)}, u32[]{:S(2)}) %collective-permute-start.20) | collective-permute-done | bytes 114720 | tf_op jit(solution)/shard_map/ppermute | solution.py:27
  104.5 2.1 %collective-permute-done.26 = bf16[64,1792]{1,0:T(8,128)(2,1)S(1)} collective-permute-done((bf16[64,1792]{1,0:T(8,128)(2,1)S(1)}, bf16[64,1792]{1,0:T(8,128)(2,1)S(1)}, u32[]{:S(2)}, u32[]{:S(2)}) %collective-permute-start.26) | collective-permute-done | bytes 229408 | tf_op jit(solution)/shard_map/ppermute | solution.py:27
  107.2 4.3 %collective-permute-done.21 = bf16[64,1792]{1,0:T(8,128)(2,1)S(1)} collective-permute-done((bf16[64,1792]{1,0:T(8,128)(2,1)S(1)}, bf16[64,1792]{1,0:T(8,128)(2,1)S(1)}, u32[]{:S(2)}, u32[]{:S(2)}) %collective-permute-start.21) | collective-permute-done | bytes 229408 | tf_op jit(solution)/shard_map/ppermute | solution.py:27
  117.6 2.5 %collective-permute-done.22 = bf16[64,1792]{1,0:T(8,128)(2,1)S(1)} collective-permute-done((bf16[64,1792]{1,0:T(8,128)(2,1)S(1)}, bf16[64,1792]{1,0:T(8,128)(2,1)S(1)}, u32[]{:S(2)}, u32[]{:S(2)}) %collective-permute-start.22) | collective-permute-done | bytes 229408 | tf_op jit(solution)/shard_map/ppermute | solution.py:27
  120.2 2.3 %collective-permute-done.37 = bf16[64,1792]{1,0:T(8,128)(2,1)S(1)} collective-permute-done((bf16[64,1792]{1,0:T(8,128)(2,1)S(1)}, bf16[64,1792]{1,0:T(8,128)(2,1)S(1)}, u32[]{:S(2)}, u32[]{:S(2)}) %collective-permute-start.37) | collective-permute-done | bytes 229408 | tf_op jit(solution)/shard_map/ppermute | solution.py:27
  122.7 2.3 %collective-permute-done.32 = bf16[64,1792]{1,0:T(8,128)(2,1)S(1)} collective-permute-done((bf16[64,1792]{1,0:T(8,128)(2,1)S(1)}, bf16[64,1792]{1,0:T(8,128)(2,1)S(1)}, u32[]{:S(2)}, u32[]{:S(2)}) %collective-permute-start.32) | collective-permute-done | bytes 229408 | tf_op jit(solution)/shard_map/ppermute | solution.py:27
  127.3 2.3 %fusion.10 = f32[256,512]{1,0:T(8,128)S(1)} fusion(bf16[1,7168,512]{2,1,0:T(8,128)(2,1)} %param.27, bf16[128,1792]{1,0:T(8,128)(2,1)S(1)} %collective-permute-done.33, bf16[64,1792]{1,0:T(8,128)(2,1)S(1)} %collective-permute-done.32, bf16[64,1792]{1,0:T(8,128)(2,1)S(1)} %convolution_convert_fusion.5), kind=kOutput, calls=%fused_computation.27 | convolution fusion | flops 472514560 | bytes 3276800 | tf_op jit(solution)/shard_map/dot_general | solution.py:359
  145.9 2.8 %collective-permute-done.40 = bf16[64,1792]{1,0:T(8,128)(2,1)S(1)} collective-permute-done((bf16[64,1792]{1,0:T(8,128)(2,1)S(1)}, bf16[64,1792]{1,0:T(8,128)(2,1)S(1)}, u32[]{:S(2)}, u32[]{:S(2)}) %collective-permute-start.40) | collective-permute-done | bytes 229408 | tf_op jit(solution)/shard_map/ppermute | solution.py:27
  150.3 3.4 %collective-permute-done.55 = bf16[64,1792]{1,0:T(8,128)(2,1)S(1)} collective-permute-done((bf16[64,1792]{1,0:T(8,128)(2,1)S(1)}, bf16[64,1792]{1,0:T(8,128)(2,1)S(1)}, u32[]{:S(2)}, u32[]{:S(2)}) %collective-permute-start.55) | collective-permute-done | bytes 229408 | tf_op jit(solution)/shard_map/ppermute | solution.py:27
  155.2 3.4 %collective-permute-done.50 = bf16[64,1792]{1,0:T(8,128)(2,1)S(1)} collective-permute-done((bf16[64,1792]{1,0:T(8,128)(2,1)S(1)}, bf16[64,1792]{1,0:T(8,128)(2,1)S(1)}, u32[]{:S(2)}, u32[]{:S(2)}) %collective-permute-start.50) | collective-permute-done | bytes 229408 | tf_op jit(solution)/shard_map/ppermute | solution.py:27
  160.1 2.6 %collective-permute-done.45 = bf16[64,1792]{1,0:T(8,128)(2,1)S(1)} collective-permute-done((bf16[64,1792]{1,0:T(8,128)(2,1)S(1)}, bf16[64,1792]{1,0:T(8,128)(2,1)S(1)}, u32[]{:S(2)}, u32[]{:S(2)}) %collective-permute-start.45) | collective-permute-done | bytes 229408 | tf_op jit(solution)/shard_map/ppermute | solution.py:27
  167.8 2.1 %collective-permute-done.46 = bf16[64,1792]{1,0:T(8,128)(2,1)S(1)} collective-permute-done((bf16[64,1792]{1,0:T(8,128)(2,1)S(1)}, bf16[64,1792]{1,0:T(8,128)(2,1)S(1)}, u32[]{:S(2)}, u32[]{:S(2)}) %collective-permute-start.46) | collective-permute-done | bytes 229408 | tf_op jit(solution)/shard_map/ppermute | solution.py:27
  174.4 2.6 %collective-permute-done.52 = bf16[32,1792]{1,0:T(8,128)(2,1)S(1)} collective-permute-done((bf16[32,1792]{1,0:T(8,128)(2,1)S(1)}, bf16[32,1792]{1,0:T(8,128)(2,1)S(1)}, u32[]{:S(2)}, u32[]{:S(2)}) %collective-permute-start.52) | collective-permute-done | bytes 114720 | tf_op jit(solution)/shard_map/ppermute | solution.py:27
  (246 shorter events, 80.9 us)
Async XLA Ops:
  1.6 16.4 %collective-permute-start.3 = (bf16[2,512,128]{2,1,0:T(8,128)(2,1)S(1)}, bf16[2,512,128]{2,1,0:T(8,128)(2,1)S(1)}, u32[]{:S(2)}, u32[]{:S(2)}) collective-permute-start(bf16[2,512,128]{2,1,0:T(8,128)(2,1)S(1)} %constant_dynamic-slice_fusion), channel_id=1, source_target_pairs={{0,4},{1,5},{2,6},{3,7},{4,0},{5,1},{6,2},{7,3},{8,12},{9,13},{10,... | collective-permute-start | bytes 786440 | tf_op jit(solution)/shard_map/ppermute | solution.py:27
  13.5 13.8 %collective-permute-start = (bf16[2,8,16,512]{3,2,1,0:T(8,128)(2,1)S(1)}, bf16[2,8,16,512]{3,2,1,0:T(8,128)(2,1)S(1)}, u32[]{:S(2)}, u32[]{:S(2)}) collective-permute-start(bf16[2,8,16,512]{3,2,1,0:T(8,128)(2,1)S(1)} %get-tuple-element.16), channel_id=1, source_target_pairs={{0,2},{1,3},{2,0},{3,1},{4,6},{5,7},{6,4},{7,5},{8,10},{9,11},{10,... | collective-permute-start | bytes 786440 | tf_op jit(solution)/shard_map/ppermute | solution.py:27
  15.1 12.1 %collective-permute-start.1 = (bf16[2,8,16,512]{3,2,1,0:T(8,128)(2,1)S(1)}, bf16[2,8,16,512]{3,2,1,0:T(8,128)(2,1)S(1)}, u32[]{:S(2)}, u32[]{:S(2)}) collective-permute-start(bf16[2,8,16,512]{3,2,1,0:T(8,128)(2,1)S(1)} %get-tuple-element.17), channel_id=1, source_target_pairs={{0,1},{1,0},{2,3},{3,2},{4,5},{5,4},{6,7},{7,6},{8,9},{9,8},{10,11... | collective-permute-start | bytes 786440 | tf_op jit(solution)/shard_map/ppermute | solution.py:27
  16.7 13.2 %collective-permute-start.2 = (bf16[2,8,16,512]{3,2,1,0:T(8,128)(2,1)S(1)}, bf16[2,8,16,512]{3,2,1,0:T(8,128)(2,1)S(1)}, u32[]{:S(2)}, u32[]{:S(2)}) collective-permute-start(bf16[2,8,16,512]{3,2,1,0:T(8,128)(2,1)S(1)} %get-tuple-element.18), channel_id=1, source_target_pairs={{0,3},{1,2},{2,1},{3,0},{4,7},{5,6},{6,5},{7,4},{8,11},{9,10},{10,... | collective-permute-start | bytes 786440 | tf_op jit(solution)/shard_map/ppermute | solution.py:27
  31.2 13.2 %collective-permute-start.8 = (bf16[64,1024]{1,0:T(8,128)(2,1)S(1)}, bf16[64,1024]{1,0:T(8,128)(2,1)S(1)}, u32[]{:S(2)}, u32[]{:S(2)}) collective-permute-start(bf16[64,1024]{1,0:T(8,128)(2,1)S(1)} %values.2), channel_id=1, source_target_pairs={{0,4},{1,5},{2,6},{3,7},{4,0},{5,1},{6,2},{7,3},{8,12},{9,13},{10,... | collective-permute-start | bytes 393224 | tf_op jit(solution)/shard_map/ppermute | solution.py:27
  37.7 17.7 %collective-permute-start.13 = (bf16[32,3584]{1,0:T(8,128)(2,1)S(1)}, bf16[32,3584]{1,0:T(8,128)(2,1)S(1)}, u32[]{:S(2)}, u32[]{:S(2)}) collective-permute-start(bf16[32,3584]{1,0:T(8,128)(2,1)S(1)} %get-tuple-element.25), channel_id=1, source_target_pairs={{0,1},{1,0},{2,3},{3,2},{4,5},{5,4},{6,7},{7,6},{8,9},{9,8},{10,11... | collective-permute-start | bytes 688136 | tf_op jit(solution)/shard_map/ppermute | solution.py:27
  43.8 15.2 %collective-permute-start.6 = (bf16[32,3584]{1,0:T(8,128)(2,1)S(1)}, bf16[32,3584]{1,0:T(8,128)(2,1)S(1)}, u32[]{:S(2)}, u32[]{:S(2)}) collective-permute-start(bf16[32,3584]{1,0:T(8,128)(2,1)S(1)} %get-tuple-element.21), channel_id=1, source_target_pairs={{0,1},{1,0},{2,3},{3,2},{4,5},{5,4},{6,7},{7,6},{8,9},{9,8},{10,11... | collective-permute-start | bytes 688136 | tf_op jit(solution)/shard_map/ppermute | solution.py:27
  48.8 10.3 %collective-permute-start.15 = (bf16[32,3584]{1,0:T(8,128)(2,1)S(1)}, bf16[32,3584]{1,0:T(8,128)(2,1)S(1)}, u32[]{:S(2)}, u32[]{:S(2)}) collective-permute-start(bf16[32,3584]{1,0:T(8,128)(2,1)S(1)} %get-tuple-element.27), channel_id=1, source_target_pairs={{0,1},{1,0},{2,3},{3,2},{4,5},{5,4},{6,7},{7,6},{8,9},{9,8},{10,11... | collective-permute-start | bytes 688136 | tf_op jit(solution)/shard_map/ppermute | solution.py:27
  55.5 15.1 %collective-permute-start.14 = (bf16[16,3584]{1,0:T(8,128)(2,1)S(1)}, bf16[16,3584]{1,0:T(8,128)(2,1)S(1)}, u32[]{:S(2)}, u32[]{:S(2)}) collective-permute-start(bf16[16,3584]{1,0:T(8,128)(2,1)S(1)} %slice.594), channel_id=1, source_target_pairs={{0,2},{1,3},{2,0},{3,1},{4,6},{5,7},{6,4},{7,5},{8,10},{9,11},{10,... | collective-permute-start | bytes 344072 | tf_op jit(solution)/shard_map/ppermute | solution.py:27
  59.1 16.7 %collective-permute-start.7 = (bf16[16,3584]{1,0:T(8,128)(2,1)S(1)}, bf16[16,3584]{1,0:T(8,128)(2,1)S(1)}, u32[]{:S(2)}, u32[]{:S(2)}) collective-permute-start(bf16[16,3584]{1,0:T(8,128)(2,1)S(1)} %slice.596), channel_id=1, source_target_pairs={{0,2},{1,3},{2,0},{3,1},{4,6},{5,7},{6,4},{7,5},{8,10},{9,11},{10,... | collective-permute-start | bytes 344072 | tf_op jit(solution)/shard_map/ppermute | solution.py:27
  61.4 8.5 %collective-permute-start.10 = (bf16[16,3584]{1,0:T(8,128)(2,1)S(1)}, bf16[16,3584]{1,0:T(8,128)(2,1)S(1)}, u32[]{:S(2)}, u32[]{:S(2)}) collective-permute-start(bf16[16,3584]{1,0:T(8,128)(2,1)S(1)} %slice.595), channel_id=1, source_target_pairs={{0,2},{1,3},{2,0},{3,1},{4,6},{5,7},{6,4},{7,5},{8,10},{9,11},{10,... | collective-permute-start | bytes 344072 | tf_op jit(solution)/shard_map/ppermute | solution.py:27
  69.9 8.2 %collective-permute-start.11 = (bf16[16,3584]{1,0:T(8,128)(2,1)S(1)}, bf16[16,3584]{1,0:T(8,128)(2,1)S(1)}, u32[]{:S(2)}, u32[]{:S(2)}) collective-permute-start(bf16[16,3584]{1,0:T(8,128)(2,1)S(1)} %fusion.109), channel_id=1, source_target_pairs={{0,4},{1,5},{2,6},{3,7},{4,0},{5,1},{6,2},{7,3},{8,12},{9,13},{10,... | collective-permute-start | bytes 344072 | tf_op jit(solution)/shard_map/ppermute | solution.py:27
  82.8 9.0 %collective-permute-start.24 = (bf16[16,1792]{1,0:T(8,128)(2,1)S(1)}, bf16[16,1792]{1,0:T(8,128)(2,1)S(1)}, u32[]{:S(2)}, u32[]{:S(2)}) collective-permute-start(bf16[16,1792]{1,0:T(8,128)(2,1)S(1)} %get-tuple-element.36), channel_id=1, source_target_pairs={{0,4},{1,5},{2,6},{3,7},{4,0},{5,1},{6,2},{7,3},{8,12},{9,13},{10,... | collective-permute-start | bytes 172040 | tf_op jit(solution)/shard_map/ppermute | solution.py:27
  83.7 10.0 %collective-permute-start.19 = (bf16[16,1792]{1,0:T(8,128)(2,1)S(1)}, bf16[16,1792]{1,0:T(8,128)(2,1)S(1)}, u32[]{:S(2)}, u32[]{:S(2)}) collective-permute-start(bf16[16,1792]{1,0:T(8,128)(2,1)S(1)} %get-tuple-element.37), channel_id=1, source_target_pairs={{0,4},{1,5},{2,6},{3,7},{4,0},{5,1},{6,2},{7,3},{8,12},{9,13},{10,... | collective-permute-start | bytes 172040 | tf_op jit(solution)/shard_map/ppermute | solution.py:27
  86.6 9.3 %collective-permute-start.29 = (bf16[16,1792]{1,0:T(8,128)(2,1)S(1)}, bf16[16,1792]{1,0:T(8,128)(2,1)S(1)}, u32[]{:S(2)}, u32[]{:S(2)}) collective-permute-start(bf16[16,1792]{1,0:T(8,128)(2,1)S(1)} %get-tuple-element.33), channel_id=1, source_target_pairs={{0,4},{1,5},{2,6},{3,7},{4,0},{5,1},{6,2},{7,3},{8,12},{9,13},{10,... | collective-permute-start | bytes 172040 | tf_op jit(solution)/shard_map/ppermute | solution.py:27
  98.0 8.6 %collective-permute-start.26 = (bf16[64,1792]{1,0:T(8,128)(2,1)S(1)}, bf16[64,1792]{1,0:T(8,128)(2,1)S(1)}, u32[]{:S(2)}, u32[]{:S(2)}) collective-permute-start(bf16[64,1792]{1,0:T(8,128)(2,1)S(1)} %pad_maximum_fusion.12), channel_id=1, source_target_pairs={{0,1},{1,0},{2,3},{3,2},{4,5},{5,4},{6,7},{7,6},{8,9},{9,8},{10,11... | collective-permute-start | bytes 688136 | tf_op jit(solution)/shard_map/ppermute | solution.py:27
  100.4 11.1 %collective-permute-start.21 = (bf16[64,1792]{1,0:T(8,128)(2,1)S(1)}, bf16[64,1792]{1,0:T(8,128)(2,1)S(1)}, u32[]{:S(2)}, u32[]{:S(2)}) collective-permute-start(bf16[64,1792]{1,0:T(8,128)(2,1)S(1)} %pad_maximum_fusion.11), channel_id=1, source_target_pairs={{0,1},{1,0},{2,3},{3,2},{4,5},{5,4},{6,7},{7,6},{8,9},{9,8},{10,11... | collective-permute-start | bytes 688136 | tf_op jit(solution)/shard_map/ppermute | solution.py:27
  102.3 12.0 %collective-permute-start.36 = (bf16[64,1792]{1,0:T(8,128)(2,1)S(1)}, bf16[64,1792]{1,0:T(8,128)(2,1)S(1)}, u32[]{:S(2)}, u32[]{:S(2)}) collective-permute-start(bf16[64,1792]{1,0:T(8,128)(2,1)S(1)} %pad_maximum_fusion.14), channel_id=1, source_target_pairs={{0,1},{1,0},{2,3},{3,2},{4,5},{5,4},{6,7},{7,6},{8,9},{9,8},{10,11... | collective-permute-start | bytes 688136 | tf_op jit(solution)/shard_map/ppermute | solution.py:27
  103.5 13.2 %collective-permute-start.31 = (bf16[64,1792]{1,0:T(8,128)(2,1)S(1)}, bf16[64,1792]{1,0:T(8,128)(2,1)S(1)}, u32[]{:S(2)}, u32[]{:S(2)}) collective-permute-start(bf16[64,1792]{1,0:T(8,128)(2,1)S(1)} %pad_maximum_fusion.13), channel_id=1, source_target_pairs={{0,1},{1,0},{2,3},{3,2},{4,5},{5,4},{6,7},{7,6},{8,9},{9,8},{10,11... | collective-permute-start | bytes 688136 | tf_op jit(solution)/shard_map/ppermute | solution.py:27
  106.8 10.7 %collective-permute-start.27 = (bf16[64,1792]{1,0:T(8,128)(2,1)S(1)}, bf16[64,1792]{1,0:T(8,128)(2,1)S(1)}, u32[]{:S(2)}, u32[]{:S(2)}) collective-permute-start(bf16[64,1792]{1,0:T(8,128)(2,1)S(1)} %convolution_convert_fusion.6), channel_id=1, source_target_pairs={{0,16},{8,24},{16,0},{24,8},{1,17},{9,25},{17,1},{25,9},{2,18},{10... | collective-permute-start | bytes 688136 | tf_op jit(solution)/shard_map/ppermute | solution.py:27
  111.7 8.4 %collective-permute-start.22 = (bf16[64,1792]{1,0:T(8,128)(2,1)S(1)}, bf16[64,1792]{1,0:T(8,128)(2,1)S(1)}, u32[]{:S(2)}, u32[]{:S(2)}) collective-permute-start(bf16[64,1792]{1,0:T(8,128)(2,1)S(1)} %convolution_convert_fusion.7), channel_id=1, source_target_pairs={{0,16},{8,24},{16,0},{24,8},{1,17},{9,25},{17,1},{25,9},{2,18},{10... | collective-permute-start | bytes 688136 | tf_op jit(solution)/shard_map/ppermute | solution.py:27
  140.2 8.5 %collective-permute-start.40 = (bf16[64,1792]{1,0:T(8,128)(2,1)S(1)}, bf16[64,1792]{1,0:T(8,128)(2,1)S(1)}, u32[]{:S(2)}, u32[]{:S(2)}) collective-permute-start(bf16[64,1792]{1,0:T(8,128)(2,1)S(1)} %slice.588), channel_id=1, source_target_pairs={{0,16},{8,24},{16,0},{24,8},{1,17},{9,25},{17,1},{25,9},{2,18},{10... | collective-permute-start | bytes 688136 | tf_op jit(solution)/shard_map/ppermute | solution.py:27
  141.0 12.6 %collective-permute-start.55 = (bf16[64,1792]{1,0:T(8,128)(2,1)S(1)}, bf16[64,1792]{1,0:T(8,128)(2,1)S(1)}, u32[]{:S(2)}, u32[]{:S(2)}) collective-permute-start(bf16[64,1792]{1,0:T(8,128)(2,1)S(1)} %slice.585), channel_id=1, source_target_pairs={{0,16},{8,24},{16,0},{24,8},{1,17},{9,25},{17,1},{25,9},{2,18},{10... | collective-permute-start | bytes 688136 | tf_op jit(solution)/shard_map/ppermute | solution.py:27
  143.3 15.2 %collective-permute-start.50 = (bf16[64,1792]{1,0:T(8,128)(2,1)S(1)}, bf16[64,1792]{1,0:T(8,128)(2,1)S(1)}, u32[]{:S(2)}, u32[]{:S(2)}) collective-permute-start(bf16[64,1792]{1,0:T(8,128)(2,1)S(1)} %slice.586), channel_id=1, source_target_pairs={{0,16},{8,24},{16,0},{24,8},{1,17},{9,25},{17,1},{25,9},{2,18},{10... | collective-permute-start | bytes 688136 | tf_op jit(solution)/shard_map/ppermute | solution.py:27
  144.1 18.6 %collective-permute-start.45 = (bf16[64,1792]{1,0:T(8,128)(2,1)S(1)}, bf16[64,1792]{1,0:T(8,128)(2,1)S(1)}, u32[]{:S(2)}, u32[]{:S(2)}) collective-permute-start(bf16[64,1792]{1,0:T(8,128)(2,1)S(1)} %slice.587), channel_id=1, source_target_pairs={{0,16},{8,24},{16,0},{24,8},{1,17},{9,25},{17,1},{25,9},{2,18},{10... | collective-permute-start | bytes 688136 | tf_op jit(solution)/shard_map/ppermute | solution.py:27
  149.1 15.2 %collective-permute-start.41 = (bf16[64,1792]{1,0:T(8,128)(2,1)S(1)}, bf16[64,1792]{1,0:T(8,128)(2,1)S(1)}, u32[]{:S(2)}, u32[]{:S(2)}) collective-permute-start(bf16[64,1792]{1,0:T(8,128)(2,1)S(1)} %fusion.4), channel_id=1, source_target_pairs={{0,1},{1,0},{2,3},{3,2},{4,5},{5,4},{6,7},{7,6},{8,9},{9,8},{10,11... | collective-permute-start | bytes 688136 | tf_op jit(solution)/shard_map/ppermute | solution.py:27
  154.0 11.0 %collective-permute-start.56 = (bf16[64,1792]{1,0:T(8,128)(2,1)S(1)}, bf16[64,1792]{1,0:T(8,128)(2,1)S(1)}, u32[]{:S(2)}, u32[]{:S(2)}) collective-permute-start(bf16[64,1792]{1,0:T(8,128)(2,1)S(1)} %fusion.7), channel_id=1, source_target_pairs={{0,1},{1,0},{2,3},{3,2},{4,5},{5,4},{6,7},{7,6},{8,9},{9,8},{10,11... | collective-permute-start | bytes 688136 | tf_op jit(solution)/shard_map/ppermute | solution.py:27
  165.3 8.4 %collective-permute-start.57 = (bf16[32,1792]{1,0:T(8,128)(2,1)S(1)}, bf16[32,1792]{1,0:T(8,128)(2,1)S(1)}, u32[]{:S(2)}, u32[]{:S(2)}) collective-permute-start(bf16[32,1792]{1,0:T(8,128)(2,1)S(1)} %slice.589), channel_id=1, source_target_pairs={{0,2},{1,3},{2,0},{3,1},{4,6},{5,7},{6,4},{7,5},{8,10},{9,11},{10,... | collective-permute-start | bytes 344072 | tf_op jit(solution)/shard_map/ppermute | solution.py:27
  167.3 9.7 %collective-permute-start.52 = (bf16[32,1792]{1,0:T(8,128)(2,1)S(1)}, bf16[32,1792]{1,0:T(8,128)(2,1)S(1)}, u32[]{:S(2)}, u32[]{:S(2)}) collective-permute-start(bf16[32,1792]{1,0:T(8,128)(2,1)S(1)} %slice.590), channel_id=1, source_target_pairs={{0,2},{1,3},{2,0},{3,1},{4,6},{5,7},{6,4},{7,5},{8,10},{9,11},{10,... | collective-permute-start | bytes 344072 | tf_op jit(solution)/shard_map/ppermute | solution.py:27
  170.2 8.5 %collective-permute-start.47 = (bf16[32,1792]{1,0:T(8,128)(2,1)S(1)}, bf16[32,1792]{1,0:T(8,128)(2,1)S(1)}, u32[]{:S(2)}, u32[]{:S(2)}) collective-permute-start(bf16[32,1792]{1,0:T(8,128)(2,1)S(1)} %slice.591), channel_id=1, source_target_pairs={{0,2},{1,3},{2,0},{3,1},{4,6},{5,7},{6,4},{7,5},{8,10},{9,11},{10,... | collective-permute-start | bytes 344072 | tf_op jit(solution)/shard_map/ppermute | solution.py:27
  170.7 9.4 %collective-permute-start.43 = (bf16[16,1792]{1,0:T(8,128)(2,1)S(1)}, bf16[16,1792]{1,0:T(8,128)(2,1)S(1)}, u32[]{:S(2)}, u32[]{:S(2)}) collective-permute-start(bf16[16,1792]{1,0:T(8,128)(2,1)S(1)} %slice.600), channel_id=1, source_target_pairs={{0,4},{1,5},{2,6},{3,7},{4,0},{5,1},{6,2},{7,3},{8,12},{9,13},{10,... | collective-permute-start | bytes 172040 | tf_op jit(solution)/shard_map/ppermute | solution.py:27
  173.8 8.3 %collective-permute-start.58 = (bf16[16,1792]{1,0:T(8,128)(2,1)S(1)}, bf16[16,1792]{1,0:T(8,128)(2,1)S(1)}, u32[]{:S(2)}, u32[]{:S(2)}) collective-permute-start(bf16[16,1792]{1,0:T(8,128)(2,1)S(1)} %slice.597), channel_id=1, source_target_pairs={{0,4},{1,5},{2,6},{3,7},{4,0},{5,1},{6,2},{7,3},{8,12},{9,13},{10,... | collective-permute-start | bytes 172040 | tf_op jit(solution)/shard_map/ppermute | solution.py:27
  (44 other events, 290.1 us)

commit v3 on v2

--- a/solution.py
+++ b/solution.py
@@ -15,7 +15,7 @@
 STATE_WIDTHS = (28, 28)
 IN_WIDTHS = (14, 14, 14, 14)
 OUT_WIDTHS = (14, 14, 14, 14)
-PROJECT_TILE = 896
+PROJECT_TILE = 1792
 PROJECT_SPLITS = 4
 
 f32 = jnp.float32
@@ -43,8 +43,8 @@
     return order
 
 
-def gather_rows(rows, axis):
-    for mask in reversed(masks_of(lax.axis_size(axis))):
+def gather_rows(rows, axis, masks=None):
+    for mask in reversed(masks or masks_of(lax.axis_size(axis))):
         rows = jnp.concatenate([rows, swap(rows, axis, mask)], axis=0)
     return rows
 
@@ -152,7 +152,7 @@
         place[None],
         in_hbm(queries.reshape(reqs, rows, width)),
         in_hbm(latent_cache.transpose(0, 2, 1)),
-        fresh_latent,
+        in_hbm(fresh_latent),
     )
 
 
@@ -195,7 +195,7 @@
     )(place[None], *[x.reshape(pairs, reqs * rows, rank) for x in latents], value_up)
 
 
-def values_here(queries, latent_cache, fresh_latent, lengths, value_up):
+def values_here(queries, latent_cache, fresh_latent, lengths, handoff, value_up):
     n_attn, n_ffn = lax.axis_size("attn"), lax.axis_size("ffn")
     attn_index = lax.axis_index("attn").astype(jnp.int32)
     ffn_index = lax.axis_index("ffn").astype(jnp.int32)
@@ -203,6 +203,11 @@
     near = relative_order(far)
     heads_local, rank, v_head = value_up.shape
     reqs, steps = queries.shape[:2]
+    onward = [(i, (i + 1) % n_attn) for i in range(n_attn)]
+
+    def hand_off(values, moved):
+        return jnp.where(moved, lax.ppermute(values, "attn", onward), values)
+
     if heads_local % 8 == 0 and heads_local % n_attn == 0:
         share = heads_local // n_attn
         part = lax.dynamic_slice_in_dim(value_up, attn_index * share, share, 0)
@@ -212,62 +217,84 @@
             queries, latent_cache, fresh_latent, lengths, ffn_index, masks, heads_local
         )
         latents = [x if m == 0 else swap(x, "ffn", m) for x, m in zip(latents, near)]
+        moved = gather_rows(handoff, "ffn", masks_of(far))
+        moved = jnp.repeat(moved.reshape(-1) == 1, steps)[:, None]
         partner = values_of(latents, 1, partner_up, attn_index, relative_order(n_attn))
-        arrived = swap(partner, "ffn", far)
         latents[0], _ = lax.optimization_barrier((latents[0], partner))
-        return values_of(latents, 0, value_up, attn_index, [0]), arrived
+        arrived = swap(hand_off(partner, moved), "ffn", far)
+        return hand_off(values_of(latents, 0, value_up, attn_index, [0]), moved), arrived
     (latents,) = attend(queries, latent_cache, fresh_latent, lengths, ffn_index, None, heads_local)
     latents = latents.reshape(reqs, steps, n_ffn, heads_local, rank)
     latents = lax.all_to_all(latents, "ffn", split_axis=2, concat_axis=0, tiled=True)
     latents = latents.reshape(n_ffn, reqs * steps, heads_local, rank)
+    flags = lax.all_gather(handoff[0], "ffn", axis=0)
     values = []
     for flip in (0, far):
-        rows = latents[ffn_index ^ jnp.array([m ^ flip for m in near], jnp.int32)]
+        sources = ffn_index ^ jnp.array([m ^ flip for m in near], jnp.int32)
+        moved = jnp.repeat(flags[sources].reshape(-1) == 1, steps)[:, None]
+        rows = latents[sources]
         rows = rows.reshape(-1, heads_local, rank)
         rows = jnp.einsum("nhb,hbw->nhw", rows, value_up, preferred_element_type=f32)
-        values.append(rows.astype(bf16).reshape(-1, heads_local * v_head))
+        values.append(hand_off(rows.astype(bf16).reshape(-1, heads_local * v_head), moved))
     return values
 
 
-def project_kernel(values_ref, *refs):
-    weight_refs, (kept_ref, sent_ref) = refs[:-2], refs[-2:]
+def project_kernel(first, values_ref, weight_ref, kept_ref, sent_ref, held, sems):
+    tiles, depth, tile = held.shape
+    splits = sems.shape[1]
+    rows = depth // splits
     half = kept_ref.shape[0]
-    depth = weight_refs[0].shape[0]
-    out = 0.0
-    for i, weight_ref in enumerate(weight_refs):
-        rows = values_ref[:, i * depth : (i + 1) * depth]
-        out = out + jnp.dot(rows, weight_ref[...], preferred_element_type=f32)
-    kept_ref[...] = out[:half]
-    sent_ref[...] = out[half:].astype(bf16)
+    copies = []
+    for i in range(tiles):
+        columns = pl.ds(first + i * tile, tile)
+        for s in range(splits):
+            block = pl.ds(s * rows, rows)
+            copies.append(
+                pltpu.make_async_copy(
+                    weight_ref.at[block, columns], held.at[i, block], sems.at[i, s]
+                )
+            )
+    for copy in copies:
+        copy.start()
+    values = values_ref[...]
+    for i in range(tiles):
+        for copy in copies[i * splits : (i + 1) * splits]:
+            copy.wait()
+        out = jnp.dot(values, held[i], preferred_element_type=f32)
+        columns = pl.ds(i * tile, tile)
+        kept_ref[:, columns] = out[:half]
+        sent_ref[:, columns] = out[half:].astype(bf16)
 
 
 def project(values, weight, first, width):
     tokens, depth = values.shape
-    tile = math.gcd(math.gcd(first, width), PROJECT_TILE)
+    tile = math.gcd(width, PROJECT_TILE)
     half = tokens // 2
-    offset = first // tile
-    splits = PROJECT_SPLITS
-    weight_specs = [
-        pl.BlockSpec((depth // splits, tile), lambda j, i=i: (i, offset + j)) for i in range(splits)
-    ]
+    tiles = width // tile
     return pl.pallas_call(
-        project_kernel,
+        functools.partial(project_kernel, first),
         out_shape=(
             jax.ShapeDtypeStruct((half, width), f32),
             jax.ShapeDtypeStruct((half, width), bf16),
         ),
-        grid=(width // tile,),
-        in_specs=[pl.BlockSpec((tokens, depth), lambda j: (0, 0)), *weight_specs],
+        in_specs=[
+            pl.BlockSpec((tokens, depth), lambda: (0, 0)),
+            pl.BlockSpec(memory_space=pl.ANY),
+        ],
         out_specs=(
-            pl.BlockSpec((half, tile), lambda j: (0, j)),
-            pl.BlockSpec((half, tile), lambda j: (0, j)),
-        ),
-        compiler_params=pltpu.CompilerParams(vmem_limit_bytes=12 * MIB),
+            pl.BlockSpec((half, width), lambda: (0, 0)),
+            pl.BlockSpec((half, width), lambda: (0, 0)),
+        ),
+        scratch_shapes=[
+            pltpu.VMEM((tiles, depth, tile), bf16),
+            pltpu.SemaphoreType.DMA((tiles, PROJECT_SPLITS)),
+        ],
+        compiler_params=pltpu.CompilerParams(vmem_limit_bytes=16 * MIB),
         cost_estimate=pl.CostEstimate(
             flops=2 * tokens * depth * width, bytes_accessed=2 * depth * width, transcendentals=0
         ),
         name="project",
-    )(values, *[in_hbm(weight)] * splits)
+    )(values, in_hbm(weight))
 
 
 def local(
@@ -312,10 +339,8 @@
 
     residual_rows = residual.reshape(own_tokens, model_width)
     half_tokens = row_tokens // 2
-    moved = jnp.repeat(handoff[0] == 1, steps)[:, None]
-    onward = [(i, (i + 1) % n_attn) for i in range(n_attn)]
     near_values, far_values = values_here(
-        queries, latent_cache, fresh_latent, lengths, value_up_matrix
+        queries, latent_cache, fresh_latent, lengths, handoff, value_up_matrix
     )
 
     def near_sum(values, first, width):
@@ -328,9 +353,7 @@
     sums = []
     for part, columns in zip(near_sums, state_ranges):
         outgoing = near_sum(far_values, *columns).astype(bf16)
-        part = part + swap(outgoing, "ffn", ffn_masks[-1]).astype(f32)
-        arrived = lax.ppermute(part.astype(bf16), "attn", onward).astype(f32)
-        sums.append(jnp.where(moved, arrived, part))
+        sums.append(part + swap(outgoing, "ffn", ffn_masks[-1]).astype(f32))
 
     def total_of(first, width):
         pieces = []

time: 185 us -> 175 us (0.946)
  waiting for transfers between devices: 78.8 us -> 60.6 us
  starting transfers between devices: 53.2 us -> 64.7 us
  Pallas kernels: 26.9 us -> 24.9 us
    ppermute x57 -> x59, waiting for transfers between devices: 75.1 us -> 60.6 us  [swap(): return lax.ppermute(value, axis, [(i, i ^ mask) for i in range(count)])]
    ppermute x57 -> x59, starting transfers between devices: 52.9 us -> 62.8 us  [swap(): return lax.ppermute(value, axis, [(i, i ^ mask) for i in range(count)])]
    ppermute x2, waiting for transfers between devices: 3.73 us -> 0.01 us  [hand_off(): return jnp.where(moved, lax.ppermute(values, 'attn', onward), values)]
    pallas_call x4, Pallas kernels: 17.9 us -> 16 us  [project(): pl.pallas_call(functools.partial(project_kernel, first), out_shape=(jax.S...]
  transfers between devices with their start and end apart: 59 -> 61, of which waited for: 37 -> 33; matrix products, arithmetic and copies ran while one was open for 6% -> 7% of each run, Pallas kernels for 14% -> 14%
where the time goes in v3:
time: 175 us
  starting transfers between devices  64.7 us (37%)
  waiting for transfers between devices  60.6 us (35%)
  Pallas kernels  24.9 us (14%)
  matrix products  12.8 us (7%)
  local copies, waits for them, and re-layouts  7.39 us (4%)
  other arithmetic  2.97 us (2%)
    ppermute x59, starting transfers between devices, swap(): return lax.ppermute(value, axis, [(i, i ^ mask) for i in range(count)])  62.8 us
    ppermute x59, waiting for transfers between devices, swap(): return lax.ppermute(value, axis, [(i, i ^ mask) for i in range(count)])  60.6 us
    pallas_call x4, Pallas kernels, project(): pl.pallas_call(functools.partial(project_kernel, first), out_shape=(jax.S...  16 us
    pallas_call x1, Pallas kernels, attend(): pl.pallas_call(functools.partial(attend_kernel, masks, heads_local), out_...  6.3 us
  transfers between devices with their start and end apart: 61, of which 33 were waited for; matrix products, arithmetic and copies ran while one was open for 7% of the time, Pallas kernels for 14%

profile of v3, /device:TPU:0, one launch (start us, length us, event | category | flops | bytes accessed | tf_op | source)
XLA Modules:
  0.0 174.9 jit_solution(2203422921513267675)
XLA Ops:
  0.6 3.1 %collective-permute-start = (s32[1,8]{1,0:T(1,128)}, s32[1,8]{1,0:T(1,128)S(1)}, u32[]{:S(2)}, u32[]{:S(2)}) collective-permute-start(s32[1,8]{1,0:T(1,128)} %param.19), channel_id=1, source_target_pairs={{0,2},{1,3},{2,0},{3,1},{4,6},{5,7},{6,4},{7,5},{8,10},{9,11},{10,... | collective-permute-start | bytes 104 | tf_op jit(solution)/shard_map/ppermute | solution.py:27
  4.7 2.7 %collective-permute-start.5 = (bf16[2,512,128]{2,1,0:T(8,128)(2,1)S(1)}, bf16[2,512,128]{2,1,0:T(8,128)(2,1)S(1)}, u32[]{:S(2)}, u32[]{:S(2)}) collective-permute-start(bf16[2,512,128]{2,1,0:T(8,128)(2,1)S(1)} %constant_dynamic-slice_fusion), channel_id=1, source_target_pairs={{0,4},{1,5},{2,6},{3,7},{4,0},{5,1},{6,2},{7,3},{8,12},{9,13},{10,... | collective-permute-start | bytes 786440 | tf_op jit(solution)/shard_map/ppermute | solution.py:27
  8.0 6.3 %attend.1 = (bf16[2,8,16,512]{3,2,1,0:T(8,128)(2,1)S(1)}, bf16[2,8,16,512]{3,2,1,0:T(8,128)(2,1)S(1)}, bf16[2,8,16,512]{3,2,1,0:T(8,128)(2,1)S(1)}, bf16[2,8,16,512]{3,2,1,0:T(8,128)(2,1)S(1)}) custom-call(s32[8]{0:T(128)S(1)} %copy-done.1, s32[1]{0:T(128)} %bitcast.1.place_ref, bf16[8,128,576]{2,1,0:T(8,128)(2,1)} %bitcast.77, ...), custom_call_target="tpu_custom_call" | custom-call | flops 1207959552 | bytes 4718592 | tf_op jit(solution)/shard_map/attend/pallas_call | solution.py:129
  20.8 6.4 %collective-permute-done.6 = bf16[2,512,128]{2,1,0:T(8,128)(2,1)S(1)} collective-permute-done((bf16[2,512,128]{2,1,0:T(8,128)(2,1)S(1)}, bf16[2,512,128]{2,1,0:T(8,128)(2,1)S(1)}, u32[]{:S(2)}, u32[]{:S(2)}) %collective-permute-start.6) | collective-permute-done | bytes 262176 | tf_op jit(solution)/shard_map/ppermute | solution.py:27
  33.8 1.8 %collective-permute-start.8 = (bf16[64,1024]{1,0:T(8,128)(2,1)S(1)}, bf16[64,1024]{1,0:T(8,128)(2,1)S(1)}, u32[]{:S(2)}, u32[]{:S(2)}) collective-permute-start(bf16[64,1024]{1,0:T(8,128)(2,1)S(1)} %values.3), channel_id=1, source_target_pairs={{0,8},{8,16},{16,24},{24,0},{1,9},{9,17},{17,25},{25,1},{2,10},{10... | collective-permute-start | bytes 393224 | tf_op jit(solution)/shard_map/ppermute | solution.py:209
  36.3 3.0 %collective-permute-done.1 = s32[2,8]{1,0:T(2,128)S(1)} collective-permute-done((s32[2,8]{1,0:T(2,128)S(1)}, s32[2,8]{1,0:T(2,128)S(1)}, u32[]{:S(2)}, u32[]{:S(2)}) %collective-permute-start.1) | collective-permute-done | bytes 96 | tf_op jit(solution)/shard_map/ppermute | solution.py:27
  39.8 4.0 %project.6 = (f32[32,3584]{1,0:T(8,128)S(1)}, bf16[32,3584]{1,0:T(8,128)(2,1)S(1)}) custom-call(bf16[64,1024]{1,0:T(8,128)(2,1)S(1)} %get-tuple-element.51.values_ref, bf16[1024,7168]{1,0:T(8,128)(2,1)} %weight_ref.7), custom_call_target="tpu_custom_call" | custom-call | flops 469762048 | bytes 7340032 | tf_op jit(solution)/shard_map/project/pallas_call | solution.py:274
  44.6 4.0 %project.4 = (f32[32,3584]{1,0:T(8,128)S(1)}, bf16[32,3584]{1,0:T(8,128)(2,1)S(1)}) custom-call(bf16[64,1024]{1,0:T(8,128)(2,1)S(1)} %get-tuple-element.51.values_ref, bf16[1024,7168]{1,0:T(8,128)(2,1)} %weight_ref.7), custom_call_target="tpu_custom_call" | custom-call | flops 469762048 | bytes 7340032 | tf_op jit(solution)/shard_map/project/pallas_call | solution.py:274
  50.0 4.0 %project.7 = (f32[32,3584]{1,0:T(8,128)S(1)}, bf16[32,3584]{1,0:T(8,128)(2,1)S(1)}) custom-call(bf16[64,1024]{1,0:T(8,128)(2,1)S(1)} %collective-permute-done.12.values_ref, bf16[1024,7168]{1,0:T(8,128)(2,1)} %weight_ref.7), custom_call_target="tpu_custom_call" | custom-call | flops 469762048 | bytes 7340032 | tf_op jit(solution)/shard_map/project/pallas_call | solution.py:274
  54.7 4.0 %project.5 = (f32[32,3584]{1,0:T(8,128)S(1)}, bf16[32,3584]{1,0:T(8,128)(2,1)S(1)}) custom-call(bf16[64,1024]{1,0:T(8,128)(2,1)S(1)} %collective-permute-done.12.values_ref, bf16[1024,7168]{1,0:T(8,128)(2,1)} %weight_ref.7), custom_call_target="tpu_custom_call" | custom-call | flops 469762048 | bytes 7340032 | tf_op jit(solution)/shard_map/project/pallas_call | solution.py:274
  60.2 2.7 %collective-permute-start.17 = (bf16[16,3584]{1,0:T(8,128)(2,1)S(1)}, bf16[16,3584]{1,0:T(8,128)(2,1)S(1)}, u32[]{:S(2)}, u32[]{:S(2)}) collective-permute-start(bf16[16,3584]{1,0:T(8,128)(2,1)S(1)} %slice.586), channel_id=1, source_target_pairs={{0,2},{1,3},{2,0},{3,1},{4,6},{5,7},{6,4},{7,5},{8,10},{9,11},{10,... | collective-permute-start | bytes 344072 | tf_op jit(solution)/shard_map/ppermute | solution.py:27
  63.1 2.1 %collective-permute-start.19 = (bf16[16,3584]{1,0:T(8,128)(2,1)S(1)}, bf16[16,3584]{1,0:T(8,128)(2,1)S(1)}, u32[]{:S(2)}, u32[]{:S(2)}) collective-permute-start(bf16[16,3584]{1,0:T(8,128)(2,1)S(1)} %slice.585), channel_id=1, source_target_pairs={{0,2},{1,3},{2,0},{3,1},{4,6},{5,7},{6,4},{7,5},{8,10},{9,11},{10,... | collective-permute-start | bytes 344072 | tf_op jit(solution)/shard_map/ppermute | solution.py:27
  65.4 2.4 %collective-permute-start.14 = (bf16[16,3584]{1,0:T(8,128)(2,1)S(1)}, bf16[16,3584]{1,0:T(8,128)(2,1)S(1)}, u32[]{:S(2)}, u32[]{:S(2)}) collective-permute-start(bf16[16,3584]{1,0:T(8,128)(2,1)S(1)} %slice.587), channel_id=1, source_target_pairs={{0,2},{1,3},{2,0},{3,1},{4,6},{5,7},{6,4},{7,5},{8,10},{9,11},{10,... | collective-permute-start | bytes 344072 | tf_op jit(solution)/shard_map/ppermute | solution.py:27
  67.8 3.1 %collective-permute-done.19 = bf16[16,3584]{1,0:T(8,128)(2,1)S(1)} collective-permute-done((bf16[16,3584]{1,0:T(8,128)(2,1)S(1)}, bf16[16,3584]{1,0:T(8,128)(2,1)S(1)}, u32[]{:S(2)}, u32[]{:S(2)}) %collective-permute-start.19) | collective-permute-done | bytes 114720 | tf_op jit(solution)/shard_map/ppermute | solution.py:27
  70.9 2.4 %collective-permute-start.20 = (bf16[16,3584]{1,0:T(8,128)(2,1)S(1)}, bf16[16,3584]{1,0:T(8,128)(2,1)S(1)}, u32[]{:S(2)}, u32[]{:S(2)}) collective-permute-start(bf16[16,3584]{1,0:T(8,128)(2,1)S(1)} %fusion.107), channel_id=1, source_target_pairs={{0,4},{1,5},{2,6},{3,7},{4,0},{5,1},{6,2},{7,3},{8,12},{9,13},{10,... | collective-permute-start | bytes 344072 | tf_op jit(solution)/shard_map/ppermute | solution.py:27
  74.7 7.5 %collective-permute-done.20 = bf16[16,3584]{1,0:T(8,128)(2,1)S(1)} collective-permute-done((bf16[16,3584]{1,0:T(8,128)(2,1)S(1)}, bf16[16,3584]{1,0:T(8,128)(2,1)S(1)}, u32[]{:S(2)}, u32[]{:S(2)}) %collective-permute-start.20) | collective-permute-done | bytes 114720 | tf_op jit(solution)/shard_map/ppermute | solution.py:27
  82.3 2.9 %collective-permute-start.31 = (bf16[16,1792]{1,0:T(8,128)(2,1)S(1)}, bf16[16,1792]{1,0:T(8,128)(2,1)S(1)}, u32[]{:S(2)}, u32[]{:S(2)}) collective-permute-start(bf16[16,1792]{1,0:T(8,128)(2,1)S(1)} %get-tuple-element.33), channel_id=1, source_target_pairs={{0,4},{1,5},{2,6},{3,7},{4,0},{5,1},{6,2},{7,3},{8,12},{9,13},{10,... | collective-permute-start | bytes 172040 | tf_op jit(solution)/shard_map/ppermute | solution.py:27
  86.2 2.8 %collective-permute-start.21 = (bf16[16,1792]{1,0:T(8,128)(2,1)S(1)}, bf16[16,1792]{1,0:T(8,128)(2,1)S(1)}, u32[]{:S(2)}, u32[]{:S(2)}) collective-permute-start(bf16[16,1792]{1,0:T(8,128)(2,1)S(1)} %get-tuple-element.37), channel_id=1, source_target_pairs={{0,4},{1,5},{2,6},{3,7},{4,0},{5,1},{6,2},{7,3},{8,12},{9,13},{10,... | collective-permute-start | bytes 172040 | tf_op jit(solution)/shard_map/ppermute | solution.py:27
  89.6 1.8 %collective-permute-start.32 = (bf16[32,1792]{1,0:T(8,128)(2,1)S(1)}, bf16[32,1792]{1,0:T(8,128)(2,1)S(1)}, u32[]{:S(2)}, u32[]{:S(2)}) collective-permute-start(bf16[32,1792]{1,0:T(8,128)(2,1)S(1)} %pad_maximum_fusion.18), channel_id=1, source_target_pairs={{0,2},{1,3},{2,0},{3,1},{4,6},{5,7},{6,4},{7,5},{8,10},{9,11},{10,... | collective-permute-start | bytes 344072 | tf_op jit(solution)/shard_map/ppermute | solution.py:27
  92.6 2.0 %collective-permute-start.22 = (bf16[32,1792]{1,0:T(8,128)(2,1)S(1)}, bf16[32,1792]{1,0:T(8,128)(2,1)S(1)}, u32[]{:S(2)}, u32[]{:S(2)}) collective-permute-start(bf16[32,1792]{1,0:T(8,128)(2,1)S(1)} %pad_maximum_fusion.16), channel_id=1, source_target_pairs={{0,2},{1,3},{2,0},{3,1},{4,6},{5,7},{6,4},{7,5},{8,10},{9,11},{10,... | collective-permute-start | bytes 344072 | tf_op jit(solution)/shard_map/ppermute | solution.py:27
  99.0 2.3 %collective-permute-done.38 = bf16[64,1792]{1,0:T(8,128)(2,1)S(1)} collective-permute-done((bf16[64,1792]{1,0:T(8,128)(2,1)S(1)}, bf16[64,1792]{1,0:T(8,128)(2,1)S(1)}, u32[]{:S(2)}, u32[]{:S(2)}) %collective-permute-start.38) | collective-permute-done | bytes 229408 | tf_op jit(solution)/shard_map/ppermute | solution.py:27
  110.8 2.1 %collective-permute-done.29 = bf16[64,1792]{1,0:T(8,128)(2,1)S(1)} collective-permute-done((bf16[64,1792]{1,0:T(8,128)(2,1)S(1)}, bf16[64,1792]{1,0:T(8,128)(2,1)S(1)}, u32[]{:S(2)}, u32[]{:S(2)}) %collective-permute-start.29) | collective-permute-done | bytes 229408 | tf_op jit(solution)/shard_map/ppermute | solution.py:27
  113.0 2.3 %collective-permute-done.24 = bf16[64,1792]{1,0:T(8,128)(2,1)S(1)} collective-permute-done((bf16[64,1792]{1,0:T(8,128)(2,1)S(1)}, bf16[64,1792]{1,0:T(8,128)(2,1)S(1)}, u32[]{:S(2)}, u32[]{:S(2)}) %collective-permute-start.24) | collective-permute-done | bytes 229408 | tf_op jit(solution)/shard_map/ppermute | solution.py:27
  135.3 2.8 %collective-permute-done.42 = bf16[64,1792]{1,0:T(8,128)(2,1)S(1)} collective-permute-done((bf16[64,1792]{1,0:T(8,128)(2,1)S(1)}, bf16[64,1792]{1,0:T(8,128)(2,1)S(1)}, u32[]{:S(2)}, u32[]{:S(2)}) %collective-permute-start.42) | collective-permute-done | bytes 229408 | tf_op jit(solution)/shard_map/ppermute | solution.py:27
  140.2 2.8 %collective-permute-done.57 = bf16[64,1792]{1,0:T(8,128)(2,1)S(1)} collective-permute-done((bf16[64,1792]{1,0:T(8,128)(2,1)S(1)}, bf16[64,1792]{1,0:T(8,128)(2,1)S(1)}, u32[]{:S(2)}, u32[]{:S(2)}) %collective-permute-start.57) | collective-permute-done | bytes 229408 | tf_op jit(solution)/shard_map/ppermute | solution.py:27
  145.1 2.8 %collective-permute-done.52 = bf16[64,1792]{1,0:T(8,128)(2,1)S(1)} collective-permute-done((bf16[64,1792]{1,0:T(8,128)(2,1)S(1)}, bf16[64,1792]{1,0:T(8,128)(2,1)S(1)}, u32[]{:S(2)}, u32[]{:S(2)}) %collective-permute-start.52) | collective-permute-done | bytes 229408 | tf_op jit(solution)/shard_map/ppermute | solution.py:27
  150.0 2.2 %collective-permute-done.47 = bf16[64,1792]{1,0:T(8,128)(2,1)S(1)} collective-permute-done((bf16[64,1792]{1,0:T(8,128)(2,1)S(1)}, bf16[64,1792]{1,0:T(8,128)(2,1)S(1)}, u32[]{:S(2)}, u32[]{:S(2)}) %collective-permute-start.47) | collective-permute-done | bytes 229408 | tf_op jit(solution)/shard_map/ppermute | solution.py:27
  155.1 2.1 %collective-permute-start.59 = (bf16[32,1792]{1,0:T(8,128)(2,1)S(1)}, bf16[32,1792]{1,0:T(8,128)(2,1)S(1)}, u32[]{:S(2)}, u32[]{:S(2)}) collective-permute-start(bf16[32,1792]{1,0:T(8,128)(2,1)S(1)} %slice.581), channel_id=1, source_target_pairs={{0,2},{1,3},{2,0},{3,1},{4,6},{5,7},{6,4},{7,5},{8,10},{9,11},{10,... | collective-permute-start | bytes 344072 | tf_op jit(solution)/shard_map/ppermute | solution.py:27
  157.5 2.1 %collective-permute-done.48 = bf16[64,1792]{1,0:T(8,128)(2,1)S(1)} collective-permute-done((bf16[64,1792]{1,0:T(8,128)(2,1)S(1)}, bf16[64,1792]{1,0:T(8,128)(2,1)S(1)}, u32[]{:S(2)}, u32[]{:S(2)}) %collective-permute-start.48) | collective-permute-done | bytes 229408 | tf_op jit(solution)/shard_map/ppermute | solution.py:27
  160.9 1.9 %collective-permute-start.45 = (bf16[16,1792]{1,0:T(8,128)(2,1)S(1)}, bf16[16,1792]{1,0:T(8,128)(2,1)S(1)}, u32[]{:S(2)}, u32[]{:S(2)}) collective-permute-start(bf16[16,1792]{1,0:T(8,128)(2,1)S(1)} %slice.592), channel_id=1, source_target_pairs={{0,4},{1,5},{2,6},{3,7},{4,0},{5,1},{6,2},{7,3},{8,12},{9,13},{10,... | collective-permute-start | bytes 172040 | tf_op jit(solution)/shard_map/ppermute | solution.py:27
  164.2 3.4 %collective-permute-done.54 = bf16[32,1792]{1,0:T(8,128)(2,1)S(1)} collective-permute-done((bf16[32,1792]{1,0:T(8,128)(2,1)S(1)}, bf16[32,1792]{1,0:T(8,128)(2,1)S(1)}, u32[]{:S(2)}, u32[]{:S(2)}) %collective-permute-start.54) | collective-permute-done | bytes 114720 | tf_op jit(solution)/shard_map/ppermute | solution.py:27
  168.9 1.8 %collective-permute-start.50 = (bf16[16,1792]{1,0:T(8,128)(2,1)S(1)}, bf16[16,1792]{1,0:T(8,128)(2,1)S(1)}, u32[]{:S(2)}, u32[]{:S(2)}) collective-permute-start(bf16[16,1792]{1,0:T(8,128)(2,1)S(1)} %slice.591), channel_id=1, source_target_pairs={{0,4},{1,5},{2,6},{3,7},{4,0},{5,1},{6,2},{7,3},{8,12},{9,13},{10,... | collective-permute-start | bytes 172040 | tf_op jit(solution)/shard_map/ppermute | solution.py:27
  (250 shorter events, 76.0 us)
Async XLA Ops:
  0.6 35.0 %collective-permute-start = (s32[1,8]{1,0:T(1,128)}, s32[1,8]{1,0:T(1,128)S(1)}, u32[]{:S(2)}, u32[]{:S(2)}) collective-permute-start(s32[1,8]{1,0:T(1,128)} %param.19), channel_id=1, source_target_pairs={{0,2},{1,3},{2,0},{3,1},{4,6},{5,7},{6,4},{7,5},{8,10},{9,11},{10,... | collective-permute-start | bytes 104 | tf_op jit(solution)/shard_map/ppermute | solution.py:27
  4.7 14.3 %collective-permute-start.5 = (bf16[2,512,128]{2,1,0:T(8,128)(2,1)S(1)}, bf16[2,512,128]{2,1,0:T(8,128)(2,1)S(1)}, u32[]{:S(2)}, u32[]{:S(2)}) collective-permute-start(bf16[2,512,128]{2,1,0:T(8,128)(2,1)S(1)} %constant_dynamic-slice_fusion), channel_id=1, source_target_pairs={{0,4},{1,5},{2,6},{3,7},{4,0},{5,1},{6,2},{7,3},{8,12},{9,13},{10,... | collective-permute-start | bytes 786440 | tf_op jit(solution)/shard_map/ppermute | solution.py:27
  14.3 15.0 %collective-permute-start.2 = (bf16[2,8,16,512]{3,2,1,0:T(8,128)(2,1)S(1)}, bf16[2,8,16,512]{3,2,1,0:T(8,128)(2,1)S(1)}, u32[]{:S(2)}, u32[]{:S(2)}) collective-permute-start(bf16[2,8,16,512]{3,2,1,0:T(8,128)(2,1)S(1)} %get-tuple-element.16), channel_id=1, source_target_pairs={{0,2},{1,3},{2,0},{3,1},{4,6},{5,7},{6,4},{7,5},{8,10},{9,11},{10,... | collective-permute-start | bytes 786440 | tf_op jit(solution)/shard_map/ppermute | solution.py:27
  14.8 14.5 %collective-permute-start.3 = (bf16[2,8,16,512]{3,2,1,0:T(8,128)(2,1)S(1)}, bf16[2,8,16,512]{3,2,1,0:T(8,128)(2,1)S(1)}, u32[]{:S(2)}, u32[]{:S(2)}) collective-permute-start(bf16[2,8,16,512]{3,2,1,0:T(8,128)(2,1)S(1)} %get-tuple-element.17), channel_id=1, source_target_pairs={{0,1},{1,0},{2,3},{3,2},{4,5},{5,4},{6,7},{7,6},{8,9},{9,8},{10,11... | collective-permute-start | bytes 786440 | tf_op jit(solution)/shard_map/ppermute | solution.py:27
  16.4 14.8 %collective-permute-start.4 = (bf16[2,8,16,512]{3,2,1,0:T(8,128)(2,1)S(1)}, bf16[2,8,16,512]{3,2,1,0:T(8,128)(2,1)S(1)}, u32[]{:S(2)}, u32[]{:S(2)}) collective-permute-start(bf16[2,8,16,512]{3,2,1,0:T(8,128)(2,1)S(1)} %get-tuple-element.18), channel_id=1, source_target_pairs={{0,3},{1,2},{2,1},{3,0},{4,7},{5,6},{6,5},{7,4},{8,11},{9,10},{10,... | collective-permute-start | bytes 786440 | tf_op jit(solution)/shard_map/ppermute | solution.py:27
  19.0 8.2 %collective-permute-start.6 = (bf16[2,512,128]{2,1,0:T(8,128)(2,1)S(1)}, bf16[2,512,128]{2,1,0:T(8,128)(2,1)S(1)}, u32[]{:S(2)}, u32[]{:S(2)}) collective-permute-start(bf16[2,512,128]{2,1,0:T(8,128)(2,1)S(1)} %collective-permute-done.5), channel_id=1, source_target_pairs={{0,16},{8,24},{16,0},{24,8},{1,17},{9,25},{17,1},{25,9},{2,18},{10... | collective-permute-start | bytes 786440 | tf_op jit(solution)/shard_map/ppermute | solution.py:27
  39.7 10.2 %collective-permute-start.12 = (bf16[64,1024]{1,0:T(8,128)(2,1)S(1)}, bf16[64,1024]{1,0:T(8,128)(2,1)S(1)}, u32[]{:S(2)}, u32[]{:S(2)}) collective-permute-start(bf16[64,1024]{1,0:T(8,128)(2,1)S(1)} %get-tuple-element.50), channel_id=1, source_target_pairs={{0,4},{1,5},{2,6},{3,7},{4,0},{5,1},{6,2},{7,3},{8,12},{9,13},{10,... | collective-permute-start | bytes 393224 | tf_op jit(solution)/shard_map/ppermute | solution.py:27
  43.8 16.3 %collective-permute-start.16 = (bf16[32,3584]{1,0:T(8,128)(2,1)S(1)}, bf16[32,3584]{1,0:T(8,128)(2,1)S(1)}, u32[]{:S(2)}, u32[]{:S(2)}) collective-permute-start(bf16[32,3584]{1,0:T(8,128)(2,1)S(1)} %get-tuple-element.25), channel_id=1, source_target_pairs={{0,1},{1,0},{2,3},{3,2},{4,5},{5,4},{6,7},{7,6},{8,9},{9,8},{10,11... | collective-permute-start | bytes 688136 | tf_op jit(solution)/shard_map/ppermute | solution.py:27
  48.6 14.3 %collective-permute-start.9 = (bf16[32,3584]{1,0:T(8,128)(2,1)S(1)}, bf16[32,3584]{1,0:T(8,128)(2,1)S(1)}, u32[]{:S(2)}, u32[]{:S(2)}) collective-permute-start(bf16[32,3584]{1,0:T(8,128)(2,1)S(1)} %get-tuple-element.21), channel_id=1, source_target_pairs={{0,1},{1,0},{2,3},{3,2},{4,5},{5,4},{6,7},{7,6},{8,9},{9,8},{10,11... | collective-permute-start | bytes 688136 | tf_op jit(solution)/shard_map/ppermute | solution.py:27
  54.0 9.1 %collective-permute-start.18 = (bf16[32,3584]{1,0:T(8,128)(2,1)S(1)}, bf16[32,3584]{1,0:T(8,128)(2,1)S(1)}, u32[]{:S(2)}, u32[]{:S(2)}) collective-permute-start(bf16[32,3584]{1,0:T(8,128)(2,1)S(1)} %get-tuple-element.27), channel_id=1, source_target_pairs={{0,1},{1,0},{2,3},{3,2},{4,5},{5,4},{6,7},{7,6},{8,9},{9,8},{10,11... | collective-permute-start | bytes 688136 | tf_op jit(solution)/shard_map/ppermute | solution.py:27
  60.2 14.5 %collective-permute-start.17 = (bf16[16,3584]{1,0:T(8,128)(2,1)S(1)}, bf16[16,3584]{1,0:T(8,128)(2,1)S(1)}, u32[]{:S(2)}, u32[]{:S(2)}) collective-permute-start(bf16[16,3584]{1,0:T(8,128)(2,1)S(1)} %slice.586), channel_id=1, source_target_pairs={{0,2},{1,3},{2,0},{3,1},{4,6},{5,7},{6,4},{7,5},{8,10},{9,11},{10,... | collective-permute-start | bytes 344072 | tf_op jit(solution)/shard_map/ppermute | solution.py:27
  62.9 22.3 %collective-permute-start.10 = (bf16[16,3584]{1,0:T(8,128)(2,1)S(1)}, bf16[16,3584]{1,0:T(8,128)(2,1)S(1)}, u32[]{:S(2)}, u32[]{:S(2)}) collective-permute-start(bf16[16,3584]{1,0:T(8,128)(2,1)S(1)} %slice.588), channel_id=1, source_target_pairs={{0,2},{1,3},{2,0},{3,1},{4,6},{5,7},{6,4},{7,5},{8,10},{9,11},{10,... | collective-permute-start | bytes 344072 | tf_op jit(solution)/shard_map/ppermute | solution.py:27
  63.1 7.7 %collective-permute-start.19 = (bf16[16,3584]{1,0:T(8,128)(2,1)S(1)}, bf16[16,3584]{1,0:T(8,128)(2,1)S(1)}, u32[]{:S(2)}, u32[]{:S(2)}) collective-permute-start(bf16[16,3584]{1,0:T(8,128)(2,1)S(1)} %slice.585), channel_id=1, source_target_pairs={{0,2},{1,3},{2,0},{3,1},{4,6},{5,7},{6,4},{7,5},{8,10},{9,11},{10,... | collective-permute-start | bytes 344072 | tf_op jit(solution)/shard_map/ppermute | solution.py:27
  65.4 7.8 %collective-permute-start.14 = (bf16[16,3584]{1,0:T(8,128)(2,1)S(1)}, bf16[16,3584]{1,0:T(8,128)(2,1)S(1)}, u32[]{:S(2)}, u32[]{:S(2)}) collective-permute-start(bf16[16,3584]{1,0:T(8,128)(2,1)S(1)} %slice.587), channel_id=1, source_target_pairs={{0,2},{1,3},{2,0},{3,1},{4,6},{5,7},{6,4},{7,5},{8,10},{9,11},{10,... | collective-permute-start | bytes 344072 | tf_op jit(solution)/shard_map/ppermute | solution.py:27
  70.9 11.3 %collective-permute-start.20 = (bf16[16,3584]{1,0:T(8,128)(2,1)S(1)}, bf16[16,3584]{1,0:T(8,128)(2,1)S(1)}, u32[]{:S(2)}, u32[]{:S(2)}) collective-permute-start(bf16[16,3584]{1,0:T(8,128)(2,1)S(1)} %fusion.107), channel_id=1, source_target_pairs={{0,4},{1,5},{2,6},{3,7},{4,0},{5,1},{6,2},{7,3},{8,12},{9,13},{10,... | collective-permute-start | bytes 344072 | tf_op jit(solution)/shard_map/ppermute | solution.py:27
  73.2 12.0 %collective-permute-start.15 = (bf16[16,3584]{1,0:T(8,128)(2,1)S(1)}, bf16[16,3584]{1,0:T(8,128)(2,1)S(1)}, u32[]{:S(2)}, u32[]{:S(2)}) collective-permute-start(bf16[16,3584]{1,0:T(8,128)(2,1)S(1)} %fusion.109), channel_id=1, source_target_pairs={{0,4},{1,5},{2,6},{3,7},{4,0},{5,1},{6,2},{7,3},{8,12},{9,13},{10,... | collective-permute-start | bytes 344072 | tf_op jit(solution)/shard_map/ppermute | solution.py:27
  95.2 8.6 %collective-permute-start.33 = (bf16[64,1792]{1,0:T(8,128)(2,1)S(1)}, bf16[64,1792]{1,0:T(8,128)(2,1)S(1)}, u32[]{:S(2)}, u32[]{:S(2)}) collective-permute-start(bf16[64,1792]{1,0:T(8,128)(2,1)S(1)} %pad_maximum_fusion.13), channel_id=1, source_target_pairs={{0,1},{1,0},{2,3},{3,2},{4,5},{5,4},{6,7},{7,6},{8,9},{9,8},{10,11... | collective-permute-start | bytes 688136 | tf_op jit(solution)/shard_map/ppermute | solution.py:27
  96.8 9.4 %collective-permute-start.28 = (bf16[64,1792]{1,0:T(8,128)(2,1)S(1)}, bf16[64,1792]{1,0:T(8,128)(2,1)S(1)}, u32[]{:S(2)}, u32[]{:S(2)}) collective-permute-start(bf16[64,1792]{1,0:T(8,128)(2,1)S(1)} %pad_maximum_fusion.12), channel_id=1, source_target_pairs={{0,1},{1,0},{2,3},{3,2},{4,5},{5,4},{6,7},{7,6},{8,9},{9,8},{10,11... | collective-permute-start | bytes 688136 | tf_op jit(solution)/shard_map/ppermute | solution.py:27
  98.1 10.6 %collective-permute-start.23 = (bf16[64,1792]{1,0:T(8,128)(2,1)S(1)}, bf16[64,1792]{1,0:T(8,128)(2,1)S(1)}, u32[]{:S(2)}, u32[]{:S(2)}) collective-permute-start(bf16[64,1792]{1,0:T(8,128)(2,1)S(1)} %pad_maximum_fusion.11), channel_id=1, source_target_pairs={{0,1},{1,0},{2,3},{3,2},{4,5},{5,4},{6,7},{7,6},{8,9},{9,8},{10,11... | collective-permute-start | bytes 688136 | tf_op jit(solution)/shard_map/ppermute | solution.py:27
  101.5 8.5 %collective-permute-start.39 = (bf16[64,1792]{1,0:T(8,128)(2,1)S(1)}, bf16[64,1792]{1,0:T(8,128)(2,1)S(1)}, u32[]{:S(2)}, u32[]{:S(2)}) collective-permute-start(bf16[64,1792]{1,0:T(8,128)(2,1)S(1)} %convolution_convert_fusion.4), channel_id=1, source_target_pairs={{0,16},{8,24},{16,0},{24,8},{1,17},{9,25},{17,1},{25,9},{2,18},{10... | collective-permute-start | bytes 688136 | tf_op jit(solution)/shard_map/ppermute | solution.py:27
  129.6 8.5 %collective-permute-start.42 = (bf16[64,1792]{1,0:T(8,128)(2,1)S(1)}, bf16[64,1792]{1,0:T(8,128)(2,1)S(1)}, u32[]{:S(2)}, u32[]{:S(2)}) collective-permute-start(bf16[64,1792]{1,0:T(8,128)(2,1)S(1)} %slice.580), channel_id=1, source_target_pairs={{0,16},{8,24},{16,0},{24,8},{1,17},{9,25},{17,1},{25,9},{2,18},{10... | collective-permute-start | bytes 688136 | tf_op jit(solution)/shard_map/ppermute | solution.py:27
  130.6 12.4 %collective-permute-start.57 = (bf16[64,1792]{1,0:T(8,128)(2,1)S(1)}, bf16[64,1792]{1,0:T(8,128)(2,1)S(1)}, u32[]{:S(2)}, u32[]{:S(2)}) collective-permute-start(bf16[64,1792]{1,0:T(8,128)(2,1)S(1)} %slice.577), channel_id=1, source_target_pairs={{0,16},{8,24},{16,0},{24,8},{1,17},{9,25},{17,1},{25,9},{2,18},{10... | collective-permute-start | bytes 688136 | tf_op jit(solution)/shard_map/ppermute | solution.py:27
  132.7 15.2 %collective-permute-start.52 = (bf16[64,1792]{1,0:T(8,128)(2,1)S(1)}, bf16[64,1792]{1,0:T(8,128)(2,1)S(1)}, u32[]{:S(2)}, u32[]{:S(2)}) collective-permute-start(bf16[64,1792]{1,0:T(8,128)(2,1)S(1)} %slice.578), channel_id=1, source_target_pairs={{0,16},{8,24},{16,0},{24,8},{1,17},{9,25},{17,1},{25,9},{2,18},{10... | collective-permute-start | bytes 688136 | tf_op jit(solution)/shard_map/ppermute | solution.py:27
  133.7 18.6 %collective-permute-start.47 = (bf16[64,1792]{1,0:T(8,128)(2,1)S(1)}, bf16[64,1792]{1,0:T(8,128)(2,1)S(1)}, u32[]{:S(2)}, u32[]{:S(2)}) collective-permute-start(bf16[64,1792]{1,0:T(8,128)(2,1)S(1)} %slice.579), channel_id=1, source_target_pairs={{0,16},{8,24},{16,0},{24,8},{1,17},{9,25},{17,1},{25,9},{2,18},{10... | collective-permute-start | bytes 688136 | tf_op jit(solution)/shard_map/ppermute | solution.py:27
  138.4 15.9 %collective-permute-start.43 = (bf16[64,1792]{1,0:T(8,128)(2,1)S(1)}, bf16[64,1792]{1,0:T(8,128)(2,1)S(1)}, u32[]{:S(2)}, u32[]{:S(2)}) collective-permute-start(bf16[64,1792]{1,0:T(8,128)(2,1)S(1)} %fusion.4), channel_id=1, source_target_pairs={{0,1},{1,0},{2,3},{3,2},{4,5},{5,4},{6,7},{7,6},{8,9},{9,8},{10,11... | collective-permute-start | bytes 688136 | tf_op jit(solution)/shard_map/ppermute | solution.py:27
  143.3 11.4 %collective-permute-start.58 = (bf16[64,1792]{1,0:T(8,128)(2,1)S(1)}, bf16[64,1792]{1,0:T(8,128)(2,1)S(1)}, u32[]{:S(2)}, u32[]{:S(2)}) collective-permute-start(bf16[64,1792]{1,0:T(8,128)(2,1)S(1)} %fusion.7), channel_id=1, source_target_pairs={{0,1},{1,0},{2,3},{3,2},{4,5},{5,4},{6,7},{7,6},{8,9},{9,8},{10,11... | collective-permute-start | bytes 688136 | tf_op jit(solution)/shard_map/ppermute | solution.py:27
  148.2 8.9 %collective-permute-start.53 = (bf16[64,1792]{1,0:T(8,128)(2,1)S(1)}, bf16[64,1792]{1,0:T(8,128)(2,1)S(1)}, u32[]{:S(2)}, u32[]{:S(2)}) collective-permute-start(bf16[64,1792]{1,0:T(8,128)(2,1)S(1)} %fusion.6), channel_id=1, source_target_pairs={{0,1},{1,0},{2,3},{3,2},{4,5},{5,4},{6,7},{7,6},{8,9},{9,8},{10,11... | collective-permute-start | bytes 688136 | tf_op jit(solution)/shard_map/ppermute | solution.py:27
  155.1 8.8 %collective-permute-start.59 = (bf16[32,1792]{1,0:T(8,128)(2,1)S(1)}, bf16[32,1792]{1,0:T(8,128)(2,1)S(1)}, u32[]{:S(2)}, u32[]{:S(2)}) collective-permute-start(bf16[32,1792]{1,0:T(8,128)(2,1)S(1)} %slice.581), channel_id=1, source_target_pairs={{0,2},{1,3},{2,0},{3,1},{4,6},{5,7},{6,4},{7,5},{8,10},{9,11},{10,... | collective-permute-start | bytes 344072 | tf_op jit(solution)/shard_map/ppermute | solution.py:27
  157.5 10.2 %collective-permute-start.54 = (bf16[32,1792]{1,0:T(8,128)(2,1)S(1)}, bf16[32,1792]{1,0:T(8,128)(2,1)S(1)}, u32[]{:S(2)}, u32[]{:S(2)}) collective-permute-start(bf16[32,1792]{1,0:T(8,128)(2,1)S(1)} %slice.582), channel_id=1, source_target_pairs={{0,2},{1,3},{2,0},{3,1},{4,6},{5,7},{6,4},{7,5},{8,10},{9,11},{10,... | collective-permute-start | bytes 344072 | tf_op jit(solution)/shard_map/ppermute | solution.py:27
  160.0 8.9 %collective-permute-start.49 = (bf16[32,1792]{1,0:T(8,128)(2,1)S(1)}, bf16[32,1792]{1,0:T(8,128)(2,1)S(1)}, u32[]{:S(2)}, u32[]{:S(2)}) collective-permute-start(bf16[32,1792]{1,0:T(8,128)(2,1)S(1)} %slice.583), channel_id=1, source_target_pairs={{0,2},{1,3},{2,0},{3,1},{4,6},{5,7},{6,4},{7,5},{8,10},{9,11},{10,... | collective-permute-start | bytes 344072 | tf_op jit(solution)/shard_map/ppermute | solution.py:27
  160.9 9.9 %collective-permute-start.45 = (bf16[16,1792]{1,0:T(8,128)(2,1)S(1)}, bf16[16,1792]{1,0:T(8,128)(2,1)S(1)}, u32[]{:S(2)}, u32[]{:S(2)}) collective-permute-start(bf16[16,1792]{1,0:T(8,128)(2,1)S(1)} %slice.592), channel_id=1, source_target_pairs={{0,4},{1,5},{2,6},{3,7},{4,0},{5,1},{6,2},{7,3},{8,12},{9,13},{10,... | collective-permute-start | bytes 172040 | tf_op jit(solution)/shard_map/ppermute | solution.py:27
  163.9 8.5 %collective-permute-start.60 = (bf16[16,1792]{1,0:T(8,128)(2,1)S(1)}, bf16[16,1792]{1,0:T(8,128)(2,1)S(1)}, u32[]{:S(2)}, u32[]{:S(2)}) collective-permute-start(bf16[16,1792]{1,0:T(8,128)(2,1)S(1)} %slice.589), channel_id=1, source_target_pairs={{0,4},{1,5},{2,6},{3,7},{4,0},{5,1},{6,2},{7,3},{8,12},{9,13},{10,... | collective-permute-start | bytes 172040 | tf_op jit(solution)/shard_map/ppermute | solution.py:27
  (45 other events, 253.0 us)

commit v4 on v3

--- a/solution.py
+++ b/solution.py
@@ -16,7 +16,7 @@
 IN_WIDTHS = (14, 14, 14, 14)
 OUT_WIDTHS = (14, 14, 14, 14)
 PROJECT_TILE = 1792
-PROJECT_SPLITS = 4
+PROJECT_SPLITS = 8
 
 f32 = jnp.float32
 bf16 = jnp.bfloat16

time: 175 us -> 175 us (level)
  transfers between devices with their start and end apart: 61 -> 61, of which waited for: 33 -> 32; matrix products, arithmetic and copies ran while one was open for 7% -> 7% of each run, Pallas kernels for 14% -> 14%
where the time goes in v4:
time: 175 us
  starting transfers between devices  65.7 us (38%)
  waiting for transfers between devices  59.2 us (34%)
  Pallas kernels  25.1 us (14%)
  matrix products  12.6 us (7%)
  local copies, waits for them, and re-layouts  7.45 us (4%)
  other arithmetic  2.97 us (2%)
  between operations  1.75 us (1%)
    ppermute x59, starting transfers between devices, swap(): return lax.ppermute(value, axis, [(i, i ^ mask) for i in range(count)])  63.9 us
    ppermute x59, waiting for transfers between devices, swap(): return lax.ppermute(value, axis, [(i, i ^ mask) for i in range(count)])  59.2 us
    pallas_call x4, Pallas kernels, project(): pl.pallas_call(functools.partial(project_kernel, first), out_shape=(jax.S...  16.2 us
    pallas_call x1, Pallas kernels, attend(): pl.pallas_call(functools.partial(attend_kernel, masks, heads_local), out_...  6.3 us
  transfers between devices with their start and end apart: 61, of which 32 were waited for; matrix products, arithmetic and copies ran while one was open for 7% of the time, Pallas kernels for 14%

profile of v4, /device:TPU:0, one launch (start us, length us, event | category | flops | bytes accessed | tf_op | source)
XLA Modules:
  0.0 174.7 jit_solution(16523048475341844828)
XLA Ops:
  0.6 3.1 %collective-permute-start = (s32[1,8]{1,0:T(1,128)}, s32[1,8]{1,0:T(1,128)S(1)}, u32[]{:S(2)}, u32[]{:S(2)}) collective-permute-start(s32[1,8]{1,0:T(1,128)} %param.19), channel_id=1, source_target_pairs={{0,2},{1,3},{2,0},{3,1},{4,6},{5,7},{6,4},{7,5},{8,10},{9,11},{10,... | collective-permute-start | bytes 104 | tf_op jit(solution)/shard_map/ppermute | solution.py:27
  4.7 2.7 %collective-permute-start.5 = (bf16[2,512,128]{2,1,0:T(8,128)(2,1)S(1)}, bf16[2,512,128]{2,1,0:T(8,128)(2,1)S(1)}, u32[]{:S(2)}, u32[]{:S(2)}) collective-permute-start(bf16[2,512,128]{2,1,0:T(8,128)(2,1)S(1)} %constant_dynamic-slice_fusion), channel_id=1, source_target_pairs={{0,4},{1,5},{2,6},{3,7},{4,0},{5,1},{6,2},{7,3},{8,12},{9,13},{10,... | collective-permute-start | bytes 786440 | tf_op jit(solution)/shard_map/ppermute | solution.py:27
  8.0 6.3 %attend.1 = (bf16[2,8,16,512]{3,2,1,0:T(8,128)(2,1)S(1)}, bf16[2,8,16,512]{3,2,1,0:T(8,128)(2,1)S(1)}, bf16[2,8,16,512]{3,2,1,0:T(8,128)(2,1)S(1)}, bf16[2,8,16,512]{3,2,1,0:T(8,128)(2,1)S(1)}) custom-call(s32[8]{0:T(128)S(1)} %copy-done.1, s32[1]{0:T(128)} %bitcast.1.place_ref, bf16[8,128,576]{2,1,0:T(8,128)(2,1)} %bitcast.77, ...), custom_call_target="tpu_custom_call" | custom-call | flops 1207959552 | bytes 4718592 | tf_op jit(solution)/shard_map/attend/pallas_call | solution.py:129
  20.8 6.4 %collective-permute-done.6 = bf16[2,512,128]{2,1,0:T(8,128)(2,1)S(1)} collective-permute-done((bf16[2,512,128]{2,1,0:T(8,128)(2,1)S(1)}, bf16[2,512,128]{2,1,0:T(8,128)(2,1)S(1)}, u32[]{:S(2)}, u32[]{:S(2)}) %collective-permute-start.6) | collective-permute-done | bytes 262176 | tf_op jit(solution)/shard_map/ppermute | solution.py:27
  29.3 1.8 %collective-permute-done.4 = bf16[2,8,16,512]{3,2,1,0:T(8,128)(2,1)S(1)} collective-permute-done((bf16[2,8,16,512]{3,2,1,0:T(8,128)(2,1)S(1)}, bf16[2,8,16,512]{3,2,1,0:T(8,128)(2,1)S(1)}, u32[]{:S(2)}, u32[]{:S(2)}) %collective-permute-start.4) | collective-permute-done | bytes 262176 | tf_op jit(solution)/shard_map/ppermute | solution.py:27
  33.8 1.8 %collective-permute-start.8 = (bf16[64,1024]{1,0:T(8,128)(2,1)S(1)}, bf16[64,1024]{1,0:T(8,128)(2,1)S(1)}, u32[]{:S(2)}, u32[]{:S(2)}) collective-permute-start(bf16[64,1024]{1,0:T(8,128)(2,1)S(1)} %values.3), channel_id=1, source_target_pairs={{0,8},{8,16},{16,24},{24,0},{1,9},{9,17},{17,25},{25,1},{2,10},{10... | collective-permute-start | bytes 393224 | tf_op jit(solution)/shard_map/ppermute | solution.py:209
  36.3 3.0 %collective-permute-done.1 = s32[2,8]{1,0:T(2,128)S(1)} collective-permute-done((s32[2,8]{1,0:T(2,128)S(1)}, s32[2,8]{1,0:T(2,128)S(1)}, u32[]{:S(2)}, u32[]{:S(2)}) %collective-permute-start.1) | collective-permute-done | bytes 96 | tf_op jit(solution)/shard_map/ppermute | solution.py:27
  39.8 4.0 %project.6 = (f32[32,3584]{1,0:T(8,128)S(1)}, bf16[32,3584]{1,0:T(8,128)(2,1)S(1)}) custom-call(bf16[64,1024]{1,0:T(8,128)(2,1)S(1)} %get-tuple-element.51.values_ref, bf16[1024,7168]{1,0:T(8,128)(2,1)} %weight_ref.7), custom_call_target="tpu_custom_call" | custom-call | flops 469762048 | bytes 7340032 | tf_op jit(solution)/shard_map/project/pallas_call | solution.py:274
  44.6 4.0 %project.4 = (f32[32,3584]{1,0:T(8,128)S(1)}, bf16[32,3584]{1,0:T(8,128)(2,1)S(1)}) custom-call(bf16[64,1024]{1,0:T(8,128)(2,1)S(1)} %get-tuple-element.51.values_ref, bf16[1024,7168]{1,0:T(8,128)(2,1)} %weight_ref.7), custom_call_target="tpu_custom_call" | custom-call | flops 469762048 | bytes 7340032 | tf_op jit(solution)/shard_map/project/pallas_call | solution.py:274
  50.1 4.0 %project.7 = (f32[32,3584]{1,0:T(8,128)S(1)}, bf16[32,3584]{1,0:T(8,128)(2,1)S(1)}) custom-call(bf16[64,1024]{1,0:T(8,128)(2,1)S(1)} %collective-permute-done.12.values_ref, bf16[1024,7168]{1,0:T(8,128)(2,1)} %weight_ref.7), custom_call_target="tpu_custom_call" | custom-call | flops 469762048 | bytes 7340032 | tf_op jit(solution)/shard_map/project/pallas_call | solution.py:274
  54.9 4.0 %project.5 = (f32[32,3584]{1,0:T(8,128)S(1)}, bf16[32,3584]{1,0:T(8,128)(2,1)S(1)}) custom-call(bf16[64,1024]{1,0:T(8,128)(2,1)S(1)} %collective-permute-done.12.values_ref, bf16[1024,7168]{1,0:T(8,128)(2,1)} %weight_ref.7), custom_call_target="tpu_custom_call" | custom-call | flops 469762048 | bytes 7340032 | tf_op jit(solution)/shard_map/project/pallas_call | solution.py:274
  60.4 2.7 %collective-permute-start.17 = (bf16[16,3584]{1,0:T(8,128)(2,1)S(1)}, bf16[16,3584]{1,0:T(8,128)(2,1)S(1)}, u32[]{:S(2)}, u32[]{:S(2)}) collective-permute-start(bf16[16,3584]{1,0:T(8,128)(2,1)S(1)} %slice.586), channel_id=1, source_target_pairs={{0,2},{1,3},{2,0},{3,1},{4,6},{5,7},{6,4},{7,5},{8,10},{9,11},{10,... | collective-permute-start | bytes 344072 | tf_op jit(solution)/shard_map/ppermute | solution.py:27
  63.3 2.1 %collective-permute-start.19 = (bf16[16,3584]{1,0:T(8,128)(2,1)S(1)}, bf16[16,3584]{1,0:T(8,128)(2,1)S(1)}, u32[]{:S(2)}, u32[]{:S(2)}) collective-permute-start(bf16[16,3584]{1,0:T(8,128)(2,1)S(1)} %slice.585), channel_id=1, source_target_pairs={{0,2},{1,3},{2,0},{3,1},{4,6},{5,7},{6,4},{7,5},{8,10},{9,11},{10,... | collective-permute-start | bytes 344072 | tf_op jit(solution)/shard_map/ppermute | solution.py:27
  65.4 2.4 %collective-permute-start.14 = (bf16[16,3584]{1,0:T(8,128)(2,1)S(1)}, bf16[16,3584]{1,0:T(8,128)(2,1)S(1)}, u32[]{:S(2)}, u32[]{:S(2)}) collective-permute-start(bf16[16,3584]{1,0:T(8,128)(2,1)S(1)} %slice.587), channel_id=1, source_target_pairs={{0,2},{1,3},{2,0},{3,1},{4,6},{5,7},{6,4},{7,5},{8,10},{9,11},{10,... | collective-permute-start | bytes 344072 | tf_op jit(solution)/shard_map/ppermute | solution.py:27
  67.8 3.1 %collective-permute-done.19 = bf16[16,3584]{1,0:T(8,128)(2,1)S(1)} collective-permute-done((bf16[16,3584]{1,0:T(8,128)(2,1)S(1)}, bf16[16,3584]{1,0:T(8,128)(2,1)S(1)}, u32[]{:S(2)}, u32[]{:S(2)}) %collective-permute-start.19) | collective-permute-done | bytes 114720 | tf_op jit(solution)/shard_map/ppermute | solution.py:27
  71.0 2.4 %collective-permute-start.20 = (bf16[16,3584]{1,0:T(8,128)(2,1)S(1)}, bf16[16,3584]{1,0:T(8,128)(2,1)S(1)}, u32[]{:S(2)}, u32[]{:S(2)}) collective-permute-start(bf16[16,3584]{1,0:T(8,128)(2,1)S(1)} %fusion.107), channel_id=1, source_target_pairs={{0,4},{1,5},{2,6},{3,7},{4,0},{5,1},{6,2},{7,3},{8,12},{9,13},{10,... | collective-permute-start | bytes 344072 | tf_op jit(solution)/shard_map/ppermute | solution.py:27
  75.0 7.3 %collective-permute-done.20 = bf16[16,3584]{1,0:T(8,128)(2,1)S(1)} collective-permute-done((bf16[16,3584]{1,0:T(8,128)(2,1)S(1)}, bf16[16,3584]{1,0:T(8,128)(2,1)S(1)}, u32[]{:S(2)}, u32[]{:S(2)}) %collective-permute-start.20) | collective-permute-done | bytes 114720 | tf_op jit(solution)/shard_map/ppermute | solution.py:27
  82.4 2.9 %collective-permute-start.31 = (bf16[16,1792]{1,0:T(8,128)(2,1)S(1)}, bf16[16,1792]{1,0:T(8,128)(2,1)S(1)}, u32[]{:S(2)}, u32[]{:S(2)}) collective-permute-start(bf16[16,1792]{1,0:T(8,128)(2,1)S(1)} %get-tuple-element.33), channel_id=1, source_target_pairs={{0,4},{1,5},{2,6},{3,7},{4,0},{5,1},{6,2},{7,3},{8,12},{9,13},{10,... | collective-permute-start | bytes 172040 | tf_op jit(solution)/shard_map/ppermute | solution.py:27
  86.3 2.8 %collective-permute-start.21 = (bf16[16,1792]{1,0:T(8,128)(2,1)S(1)}, bf16[16,1792]{1,0:T(8,128)(2,1)S(1)}, u32[]{:S(2)}, u32[]{:S(2)}) collective-permute-start(bf16[16,1792]{1,0:T(8,128)(2,1)S(1)} %get-tuple-element.37), channel_id=1, source_target_pairs={{0,4},{1,5},{2,6},{3,7},{4,0},{5,1},{6,2},{7,3},{8,12},{9,13},{10,... | collective-permute-start | bytes 172040 | tf_op jit(solution)/shard_map/ppermute | solution.py:27
  89.3 2.1 %collective-permute-start.32 = (bf16[32,1792]{1,0:T(8,128)(2,1)S(1)}, bf16[32,1792]{1,0:T(8,128)(2,1)S(1)}, u32[]{:S(2)}, u32[]{:S(2)}) collective-permute-start(bf16[32,1792]{1,0:T(8,128)(2,1)S(1)} %pad_maximum_fusion.18), channel_id=1, source_target_pairs={{0,2},{1,3},{2,0},{3,1},{4,6},{5,7},{6,4},{7,5},{8,10},{9,11},{10,... | collective-permute-start | bytes 344072 | tf_op jit(solution)/shard_map/ppermute | solution.py:27
  92.5 1.7 collective-permute-start.22
  99.0 2.4 %collective-permute-done.38 = bf16[64,1792]{1,0:T(8,128)(2,1)S(1)} collective-permute-done((bf16[64,1792]{1,0:T(8,128)(2,1)S(1)}, bf16[64,1792]{1,0:T(8,128)(2,1)S(1)}, u32[]{:S(2)}, u32[]{:S(2)}) %collective-permute-start.38) | collective-permute-done | bytes 229408 | tf_op jit(solution)/shard_map/ppermute | solution.py:27
  110.9 2.0 %collective-permute-done.29 = bf16[64,1792]{1,0:T(8,128)(2,1)S(1)} collective-permute-done((bf16[64,1792]{1,0:T(8,128)(2,1)S(1)}, bf16[64,1792]{1,0:T(8,128)(2,1)S(1)}, u32[]{:S(2)}, u32[]{:S(2)}) %collective-permute-start.29) | collective-permute-done | bytes 229408 | tf_op jit(solution)/shard_map/ppermute | solution.py:27
  113.1 2.3 %collective-permute-done.24 = bf16[64,1792]{1,0:T(8,128)(2,1)S(1)} collective-permute-done((bf16[64,1792]{1,0:T(8,128)(2,1)S(1)}, bf16[64,1792]{1,0:T(8,128)(2,1)S(1)}, u32[]{:S(2)}, u32[]{:S(2)}) %collective-permute-start.24) | collective-permute-done | bytes 229408 | tf_op jit(solution)/shard_map/ppermute | solution.py:27
  135.5 2.8 %collective-permute-done.42 = bf16[64,1792]{1,0:T(8,128)(2,1)S(1)} collective-permute-done((bf16[64,1792]{1,0:T(8,128)(2,1)S(1)}, bf16[64,1792]{1,0:T(8,128)(2,1)S(1)}, u32[]{:S(2)}, u32[]{:S(2)}) %collective-permute-start.42) | collective-permute-done | bytes 229408 | tf_op jit(solution)/shard_map/ppermute | solution.py:27
  140.2 3.0 %collective-permute-done.57 = bf16[64,1792]{1,0:T(8,128)(2,1)S(1)} collective-permute-done((bf16[64,1792]{1,0:T(8,128)(2,1)S(1)}, bf16[64,1792]{1,0:T(8,128)(2,1)S(1)}, u32[]{:S(2)}, u32[]{:S(2)}) %collective-permute-start.57) | collective-permute-done | bytes 229408 | tf_op jit(solution)/shard_map/ppermute | solution.py:27
  145.1 3.0 %collective-permute-done.52 = bf16[64,1792]{1,0:T(8,128)(2,1)S(1)} collective-permute-done((bf16[64,1792]{1,0:T(8,128)(2,1)S(1)}, bf16[64,1792]{1,0:T(8,128)(2,1)S(1)}, u32[]{:S(2)}, u32[]{:S(2)}) %collective-permute-start.52) | collective-permute-done | bytes 229408 | tf_op jit(solution)/shard_map/ppermute | solution.py:27
  150.0 2.4 %collective-permute-done.47 = bf16[64,1792]{1,0:T(8,128)(2,1)S(1)} collective-permute-done((bf16[64,1792]{1,0:T(8,128)(2,1)S(1)}, bf16[64,1792]{1,0:T(8,128)(2,1)S(1)}, u32[]{:S(2)}, u32[]{:S(2)}) %collective-permute-start.47) | collective-permute-done | bytes 229408 | tf_op jit(solution)/shard_map/ppermute | solution.py:27
  155.3 1.8 %collective-permute-start.59 = (bf16[32,1792]{1,0:T(8,128)(2,1)S(1)}, bf16[32,1792]{1,0:T(8,128)(2,1)S(1)}, u32[]{:S(2)}, u32[]{:S(2)}) collective-permute-start(bf16[32,1792]{1,0:T(8,128)(2,1)S(1)} %slice.581), channel_id=1, source_target_pairs={{0,2},{1,3},{2,0},{3,1},{4,6},{5,7},{6,4},{7,5},{8,10},{9,11},{10,... | collective-permute-start | bytes 344072 | tf_op jit(solution)/shard_map/ppermute | solution.py:27
  157.8 2.0 %collective-permute-done.48 = bf16[64,1792]{1,0:T(8,128)(2,1)S(1)} collective-permute-done((bf16[64,1792]{1,0:T(8,128)(2,1)S(1)}, bf16[64,1792]{1,0:T(8,128)(2,1)S(1)}, u32[]{:S(2)}, u32[]{:S(2)}) %collective-permute-start.48) | collective-permute-done | bytes 229408 | tf_op jit(solution)/shard_map/ppermute | solution.py:27
  164.6 2.1 %collective-permute-done.54 = bf16[32,1792]{1,0:T(8,128)(2,1)S(1)} collective-permute-done((bf16[32,1792]{1,0:T(8,128)(2,1)S(1)}, bf16[32,1792]{1,0:T(8,128)(2,1)S(1)}, u32[]{:S(2)}, u32[]{:S(2)}) %collective-permute-start.54) | collective-permute-done | bytes 114720 | tf_op jit(solution)/shard_map/ppermute | solution.py:27
  170.8 1.8 %collective-permute-done.60 = bf16[16,1792]{1,0:T(8,128)(2,1)S(1)} collective-permute-done((bf16[16,1792]{1,0:T(8,128)(2,1)S(1)}, bf16[16,1792]{1,0:T(8,128)(2,1)S(1)}, u32[]{:S(2)}, u32[]{:S(2)}) %collective-permute-start.60) | collective-permute-done | bytes 57376 | tf_op jit(solution)/shard_map/ppermute | solution.py:27
  (250 shorter events, 76.6 us)
Async XLA Ops:
  0.6 35.0 %collective-permute-start = (s32[1,8]{1,0:T(1,128)}, s32[1,8]{1,0:T(1,128)S(1)}, u32[]{:S(2)}, u32[]{:S(2)}) collective-permute-start(s32[1,8]{1,0:T(1,128)} %param.19), channel_id=1, source_target_pairs={{0,2},{1,3},{2,0},{3,1},{4,6},{5,7},{6,4},{7,5},{8,10},{9,11},{10,... | collective-permute-start | bytes 104 | tf_op jit(solution)/shard_map/ppermute | solution.py:27
  4.7 14.3 %collective-permute-start.5 = (bf16[2,512,128]{2,1,0:T(8,128)(2,1)S(1)}, bf16[2,512,128]{2,1,0:T(8,128)(2,1)S(1)}, u32[]{:S(2)}, u32[]{:S(2)}) collective-permute-start(bf16[2,512,128]{2,1,0:T(8,128)(2,1)S(1)} %constant_dynamic-slice_fusion), channel_id=1, source_target_pairs={{0,4},{1,5},{2,6},{3,7},{4,0},{5,1},{6,2},{7,3},{8,12},{9,13},{10,... | collective-permute-start | bytes 786440 | tf_op jit(solution)/shard_map/ppermute | solution.py:27
  14.3 15.0 %collective-permute-start.2 = (bf16[2,8,16,512]{3,2,1,0:T(8,128)(2,1)S(1)}, bf16[2,8,16,512]{3,2,1,0:T(8,128)(2,1)S(1)}, u32[]{:S(2)}, u32[]{:S(2)}) collective-permute-start(bf16[2,8,16,512]{3,2,1,0:T(8,128)(2,1)S(1)} %get-tuple-element.16), channel_id=1, source_target_pairs={{0,2},{1,3},{2,0},{3,1},{4,6},{5,7},{6,4},{7,5},{8,10},{9,11},{10,... | collective-permute-start | bytes 786440 | tf_op jit(solution)/shard_map/ppermute | solution.py:27
  14.8 14.5 %collective-permute-start.3 = (bf16[2,8,16,512]{3,2,1,0:T(8,128)(2,1)S(1)}, bf16[2,8,16,512]{3,2,1,0:T(8,128)(2,1)S(1)}, u32[]{:S(2)}, u32[]{:S(2)}) collective-permute-start(bf16[2,8,16,512]{3,2,1,0:T(8,128)(2,1)S(1)} %get-tuple-element.17), channel_id=1, source_target_pairs={{0,1},{1,0},{2,3},{3,2},{4,5},{5,4},{6,7},{7,6},{8,9},{9,8},{10,11... | collective-permute-start | bytes 786440 | tf_op jit(solution)/shard_map/ppermute | solution.py:27
  16.4 14.8 %collective-permute-start.4 = (bf16[2,8,16,512]{3,2,1,0:T(8,128)(2,1)S(1)}, bf16[2,8,16,512]{3,2,1,0:T(8,128)(2,1)S(1)}, u32[]{:S(2)}, u32[]{:S(2)}) collective-permute-start(bf16[2,8,16,512]{3,2,1,0:T(8,128)(2,1)S(1)} %get-tuple-element.18), channel_id=1, source_target_pairs={{0,3},{1,2},{2,1},{3,0},{4,7},{5,6},{6,5},{7,4},{8,11},{9,10},{10,... | collective-permute-start | bytes 786440 | tf_op jit(solution)/shard_map/ppermute | solution.py:27
  19.0 8.2 %collective-permute-start.6 = (bf16[2,512,128]{2,1,0:T(8,128)(2,1)S(1)}, bf16[2,512,128]{2,1,0:T(8,128)(2,1)S(1)}, u32[]{:S(2)}, u32[]{:S(2)}) collective-permute-start(bf16[2,512,128]{2,1,0:T(8,128)(2,1)S(1)} %collective-permute-done.5), channel_id=1, source_target_pairs={{0,16},{8,24},{16,0},{24,8},{1,17},{9,25},{17,1},{25,9},{2,18},{10... | collective-permute-start | bytes 786440 | tf_op jit(solution)/shard_map/ppermute | solution.py:27
  39.7 10.3 %collective-permute-start.12 = (bf16[64,1024]{1,0:T(8,128)(2,1)S(1)}, bf16[64,1024]{1,0:T(8,128)(2,1)S(1)}, u32[]{:S(2)}, u32[]{:S(2)}) collective-permute-start(bf16[64,1024]{1,0:T(8,128)(2,1)S(1)} %get-tuple-element.50), channel_id=1, source_target_pairs={{0,4},{1,5},{2,6},{3,7},{4,0},{5,1},{6,2},{7,3},{8,12},{9,13},{10,... | collective-permute-start | bytes 393224 | tf_op jit(solution)/shard_map/ppermute | solution.py:27
  43.8 16.5 %collective-permute-start.16 = (bf16[32,3584]{1,0:T(8,128)(2,1)S(1)}, bf16[32,3584]{1,0:T(8,128)(2,1)S(1)}, u32[]{:S(2)}, u32[]{:S(2)}) collective-permute-start(bf16[32,3584]{1,0:T(8,128)(2,1)S(1)} %get-tuple-element.25), channel_id=1, source_target_pairs={{0,1},{1,0},{2,3},{3,2},{4,5},{5,4},{6,7},{7,6},{8,9},{9,8},{10,11... | collective-permute-start | bytes 688136 | tf_op jit(solution)/shard_map/ppermute | solution.py:27
  48.6 14.4 %collective-permute-start.9 = (bf16[32,3584]{1,0:T(8,128)(2,1)S(1)}, bf16[32,3584]{1,0:T(8,128)(2,1)S(1)}, u32[]{:S(2)}, u32[]{:S(2)}) collective-permute-start(bf16[32,3584]{1,0:T(8,128)(2,1)S(1)} %get-tuple-element.21), channel_id=1, source_target_pairs={{0,1},{1,0},{2,3},{3,2},{4,5},{5,4},{6,7},{7,6},{8,9},{9,8},{10,11... | collective-permute-start | bytes 688136 | tf_op jit(solution)/shard_map/ppermute | solution.py:27
  54.1 9.1 %collective-permute-start.18 = (bf16[32,3584]{1,0:T(8,128)(2,1)S(1)}, bf16[32,3584]{1,0:T(8,128)(2,1)S(1)}, u32[]{:S(2)}, u32[]{:S(2)}) collective-permute-start(bf16[32,3584]{1,0:T(8,128)(2,1)S(1)} %get-tuple-element.27), channel_id=1, source_target_pairs={{0,1},{1,0},{2,3},{3,2},{4,5},{5,4},{6,7},{7,6},{8,9},{9,8},{10,11... | collective-permute-start | bytes 688136 | tf_op jit(solution)/shard_map/ppermute | solution.py:27
  60.4 14.6 %collective-permute-start.17 = (bf16[16,3584]{1,0:T(8,128)(2,1)S(1)}, bf16[16,3584]{1,0:T(8,128)(2,1)S(1)}, u32[]{:S(2)}, u32[]{:S(2)}) collective-permute-start(bf16[16,3584]{1,0:T(8,128)(2,1)S(1)} %slice.586), channel_id=1, source_target_pairs={{0,2},{1,3},{2,0},{3,1},{4,6},{5,7},{6,4},{7,5},{8,10},{9,11},{10,... | collective-permute-start | bytes 344072 | tf_op jit(solution)/shard_map/ppermute | solution.py:27
  63.1 22.2 %collective-permute-start.10 = (bf16[16,3584]{1,0:T(8,128)(2,1)S(1)}, bf16[16,3584]{1,0:T(8,128)(2,1)S(1)}, u32[]{:S(2)}, u32[]{:S(2)}) collective-permute-start(bf16[16,3584]{1,0:T(8,128)(2,1)S(1)} %slice.588), channel_id=1, source_target_pairs={{0,2},{1,3},{2,0},{3,1},{4,6},{5,7},{6,4},{7,5},{8,10},{9,11},{10,... | collective-permute-start | bytes 344072 | tf_op jit(solution)/shard_map/ppermute | solution.py:27
  63.3 7.7 %collective-permute-start.19 = (bf16[16,3584]{1,0:T(8,128)(2,1)S(1)}, bf16[16,3584]{1,0:T(8,128)(2,1)S(1)}, u32[]{:S(2)}, u32[]{:S(2)}) collective-permute-start(bf16[16,3584]{1,0:T(8,128)(2,1)S(1)} %slice.585), channel_id=1, source_target_pairs={{0,2},{1,3},{2,0},{3,1},{4,6},{5,7},{6,4},{7,5},{8,10},{9,11},{10,... | collective-permute-start | bytes 344072 | tf_op jit(solution)/shard_map/ppermute | solution.py:27
  65.4 8.0 %collective-permute-start.14 = (bf16[16,3584]{1,0:T(8,128)(2,1)S(1)}, bf16[16,3584]{1,0:T(8,128)(2,1)S(1)}, u32[]{:S(2)}, u32[]{:S(2)}) collective-permute-start(bf16[16,3584]{1,0:T(8,128)(2,1)S(1)} %slice.587), channel_id=1, source_target_pairs={{0,2},{1,3},{2,0},{3,1},{4,6},{5,7},{6,4},{7,5},{8,10},{9,11},{10,... | collective-permute-start | bytes 344072 | tf_op jit(solution)/shard_map/ppermute | solution.py:27
  71.0 11.3 %collective-permute-start.20 = (bf16[16,3584]{1,0:T(8,128)(2,1)S(1)}, bf16[16,3584]{1,0:T(8,128)(2,1)S(1)}, u32[]{:S(2)}, u32[]{:S(2)}) collective-permute-start(bf16[16,3584]{1,0:T(8,128)(2,1)S(1)} %fusion.107), channel_id=1, source_target_pairs={{0,4},{1,5},{2,6},{3,7},{4,0},{5,1},{6,2},{7,3},{8,12},{9,13},{10,... | collective-permute-start | bytes 344072 | tf_op jit(solution)/shard_map/ppermute | solution.py:27
  73.5 11.9 %collective-permute-start.15 = (bf16[16,3584]{1,0:T(8,128)(2,1)S(1)}, bf16[16,3584]{1,0:T(8,128)(2,1)S(1)}, u32[]{:S(2)}, u32[]{:S(2)}) collective-permute-start(bf16[16,3584]{1,0:T(8,128)(2,1)S(1)} %fusion.109), channel_id=1, source_target_pairs={{0,4},{1,5},{2,6},{3,7},{4,0},{5,1},{6,2},{7,3},{8,12},{9,13},{10,... | collective-permute-start | bytes 344072 | tf_op jit(solution)/shard_map/ppermute | solution.py:27
  95.3 8.6 %collective-permute-start.33 = (bf16[64,1792]{1,0:T(8,128)(2,1)S(1)}, bf16[64,1792]{1,0:T(8,128)(2,1)S(1)}, u32[]{:S(2)}, u32[]{:S(2)}) collective-permute-start(bf16[64,1792]{1,0:T(8,128)(2,1)S(1)} %pad_maximum_fusion.13), channel_id=1, source_target_pairs={{0,1},{1,0},{2,3},{3,2},{4,5},{5,4},{6,7},{7,6},{8,9},{9,8},{10,11... | collective-permute-start | bytes 688136 | tf_op jit(solution)/shard_map/ppermute | solution.py:27
  96.8 9.5 %collective-permute-start.28 = (bf16[64,1792]{1,0:T(8,128)(2,1)S(1)}, bf16[64,1792]{1,0:T(8,128)(2,1)S(1)}, u32[]{:S(2)}, u32[]{:S(2)}) collective-permute-start(bf16[64,1792]{1,0:T(8,128)(2,1)S(1)} %pad_maximum_fusion.12), channel_id=1, source_target_pairs={{0,1},{1,0},{2,3},{3,2},{4,5},{5,4},{6,7},{7,6},{8,9},{9,8},{10,11... | collective-permute-start | bytes 688136 | tf_op jit(solution)/shard_map/ppermute | solution.py:27
  98.0 10.8 %collective-permute-start.23 = (bf16[64,1792]{1,0:T(8,128)(2,1)S(1)}, bf16[64,1792]{1,0:T(8,128)(2,1)S(1)}, u32[]{:S(2)}, u32[]{:S(2)}) collective-permute-start(bf16[64,1792]{1,0:T(8,128)(2,1)S(1)} %pad_maximum_fusion.11), channel_id=1, source_target_pairs={{0,1},{1,0},{2,3},{3,2},{4,5},{5,4},{6,7},{7,6},{8,9},{9,8},{10,11... | collective-permute-start | bytes 688136 | tf_op jit(solution)/shard_map/ppermute | solution.py:27
  101.6 8.5 %collective-permute-start.39 = (bf16[64,1792]{1,0:T(8,128)(2,1)S(1)}, bf16[64,1792]{1,0:T(8,128)(2,1)S(1)}, u32[]{:S(2)}, u32[]{:S(2)}) collective-permute-start(bf16[64,1792]{1,0:T(8,128)(2,1)S(1)} %convolution_convert_fusion.4), channel_id=1, source_target_pairs={{0,16},{8,24},{16,0},{24,8},{1,17},{9,25},{17,1},{25,9},{2,18},{10... | collective-permute-start | bytes 688136 | tf_op jit(solution)/shard_map/ppermute | solution.py:27
  129.8 8.5 %collective-permute-start.42 = (bf16[64,1792]{1,0:T(8,128)(2,1)S(1)}, bf16[64,1792]{1,0:T(8,128)(2,1)S(1)}, u32[]{:S(2)}, u32[]{:S(2)}) collective-permute-start(bf16[64,1792]{1,0:T(8,128)(2,1)S(1)} %slice.580), channel_id=1, source_target_pairs={{0,16},{8,24},{16,0},{24,8},{1,17},{9,25},{17,1},{25,9},{2,18},{10... | collective-permute-start | bytes 688136 | tf_op jit(solution)/shard_map/ppermute | solution.py:27
  130.8 12.4 %collective-permute-start.57 = (bf16[64,1792]{1,0:T(8,128)(2,1)S(1)}, bf16[64,1792]{1,0:T(8,128)(2,1)S(1)}, u32[]{:S(2)}, u32[]{:S(2)}) collective-permute-start(bf16[64,1792]{1,0:T(8,128)(2,1)S(1)} %slice.577), channel_id=1, source_target_pairs={{0,16},{8,24},{16,0},{24,8},{1,17},{9,25},{17,1},{25,9},{2,18},{10... | collective-permute-start | bytes 688136 | tf_op jit(solution)/shard_map/ppermute | solution.py:27
  132.8 15.2 %collective-permute-start.52 = (bf16[64,1792]{1,0:T(8,128)(2,1)S(1)}, bf16[64,1792]{1,0:T(8,128)(2,1)S(1)}, u32[]{:S(2)}, u32[]{:S(2)}) collective-permute-start(bf16[64,1792]{1,0:T(8,128)(2,1)S(1)} %slice.578), channel_id=1, source_target_pairs={{0,16},{8,24},{16,0},{24,8},{1,17},{9,25},{17,1},{25,9},{2,18},{10... | collective-permute-start | bytes 688136 | tf_op jit(solution)/shard_map/ppermute | solution.py:27
  133.9 18.5 %collective-permute-start.47 = (bf16[64,1792]{1,0:T(8,128)(2,1)S(1)}, bf16[64,1792]{1,0:T(8,128)(2,1)S(1)}, u32[]{:S(2)}, u32[]{:S(2)}) collective-permute-start(bf16[64,1792]{1,0:T(8,128)(2,1)S(1)} %slice.579), channel_id=1, source_target_pairs={{0,16},{8,24},{16,0},{24,8},{1,17},{9,25},{17,1},{25,9},{2,18},{10... | collective-permute-start | bytes 688136 | tf_op jit(solution)/shard_map/ppermute | solution.py:27
  138.6 15.8 %collective-permute-start.43 = (bf16[64,1792]{1,0:T(8,128)(2,1)S(1)}, bf16[64,1792]{1,0:T(8,128)(2,1)S(1)}, u32[]{:S(2)}, u32[]{:S(2)}) collective-permute-start(bf16[64,1792]{1,0:T(8,128)(2,1)S(1)} %fusion.4), channel_id=1, source_target_pairs={{0,1},{1,0},{2,3},{3,2},{4,5},{5,4},{6,7},{7,6},{8,9},{9,8},{10,11... | collective-permute-start | bytes 688136 | tf_op jit(solution)/shard_map/ppermute | solution.py:27
  143.5 11.5 %collective-permute-start.58 = (bf16[64,1792]{1,0:T(8,128)(2,1)S(1)}, bf16[64,1792]{1,0:T(8,128)(2,1)S(1)}, u32[]{:S(2)}, u32[]{:S(2)}) collective-permute-start(bf16[64,1792]{1,0:T(8,128)(2,1)S(1)} %fusion.7), channel_id=1, source_target_pairs={{0,1},{1,0},{2,3},{3,2},{4,5},{5,4},{6,7},{7,6},{8,9},{9,8},{10,11... | collective-permute-start | bytes 688136 | tf_op jit(solution)/shard_map/ppermute | solution.py:27
  148.4 8.7 %collective-permute-start.53 = (bf16[64,1792]{1,0:T(8,128)(2,1)S(1)}, bf16[64,1792]{1,0:T(8,128)(2,1)S(1)}, u32[]{:S(2)}, u32[]{:S(2)}) collective-permute-start(bf16[64,1792]{1,0:T(8,128)(2,1)S(1)} %fusion.6), channel_id=1, source_target_pairs={{0,1},{1,0},{2,3},{3,2},{4,5},{5,4},{6,7},{7,6},{8,9},{9,8},{10,11... | collective-permute-start | bytes 688136 | tf_op jit(solution)/shard_map/ppermute | solution.py:27
  155.3 7.9 %collective-permute-start.59 = (bf16[32,1792]{1,0:T(8,128)(2,1)S(1)}, bf16[32,1792]{1,0:T(8,128)(2,1)S(1)}, u32[]{:S(2)}, u32[]{:S(2)}) collective-permute-start(bf16[32,1792]{1,0:T(8,128)(2,1)S(1)} %slice.581), channel_id=1, source_target_pairs={{0,2},{1,3},{2,0},{3,1},{4,6},{5,7},{6,4},{7,5},{8,10},{9,11},{10,... | collective-permute-start | bytes 344072 | tf_op jit(solution)/shard_map/ppermute | solution.py:27
  157.4 9.3 %collective-permute-start.54 = (bf16[32,1792]{1,0:T(8,128)(2,1)S(1)}, bf16[32,1792]{1,0:T(8,128)(2,1)S(1)}, u32[]{:S(2)}, u32[]{:S(2)}) collective-permute-start(bf16[32,1792]{1,0:T(8,128)(2,1)S(1)} %slice.582), channel_id=1, source_target_pairs={{0,2},{1,3},{2,0},{3,1},{4,6},{5,7},{6,4},{7,5},{8,10},{9,11},{10,... | collective-permute-start | bytes 344072 | tf_op jit(solution)/shard_map/ppermute | solution.py:27
  160.1 8.6 %collective-permute-start.49 = (bf16[32,1792]{1,0:T(8,128)(2,1)S(1)}, bf16[32,1792]{1,0:T(8,128)(2,1)S(1)}, u32[]{:S(2)}, u32[]{:S(2)}) collective-permute-start(bf16[32,1792]{1,0:T(8,128)(2,1)S(1)} %slice.583), channel_id=1, source_target_pairs={{0,2},{1,3},{2,0},{3,1},{4,6},{5,7},{6,4},{7,5},{8,10},{9,11},{10,... | collective-permute-start | bytes 344072 | tf_op jit(solution)/shard_map/ppermute | solution.py:27
  161.5 9.2 %collective-permute-start.45 = (bf16[16,1792]{1,0:T(8,128)(2,1)S(1)}, bf16[16,1792]{1,0:T(8,128)(2,1)S(1)}, u32[]{:S(2)}, u32[]{:S(2)}) collective-permute-start(bf16[16,1792]{1,0:T(8,128)(2,1)S(1)} %slice.592), channel_id=1, source_target_pairs={{0,4},{1,5},{2,6},{3,7},{4,0},{5,1},{6,2},{7,3},{8,12},{9,13},{10,... | collective-permute-start | bytes 172040 | tf_op jit(solution)/shard_map/ppermute | solution.py:27
  163.3 9.3 %collective-permute-start.60 = (bf16[16,1792]{1,0:T(8,128)(2,1)S(1)}, bf16[16,1792]{1,0:T(8,128)(2,1)S(1)}, u32[]{:S(2)}, u32[]{:S(2)}) collective-permute-start(bf16[16,1792]{1,0:T(8,128)(2,1)S(1)} %slice.589), channel_id=1, source_target_pairs={{0,4},{1,5},{2,6},{3,7},{4,0},{5,1},{6,2},{7,3},{8,12},{9,13},{10,... | collective-permute-start | bytes 172040 | tf_op jit(solution)/shard_map/ppermute | solution.py:27
  (45 other events, 254.3 us)
